TPU v7x, 512 devices: a whole 4x4x16 slice. The times are simulated.
512 devices in a mesh: dp: 64 (over x_lo, z, core), pipe: 8 (over y, x_hi).
Axes of the slice: x: 4 (x_hi: 2, x_lo: 2; x = x_hi * 2 + x_lo), y: 4, z: 16, core: 2. Of those that a mesh axis runs over, the one named last changes fastest.
Arguments:
- pixels: bfloat16 [4, 2048, 512], P(None, 'dp'), may hold values from -6 to 6
- cotangent: bfloat16 [4, 2048, 512], P(None, 'dp'), may hold values from -6 to 6
- weights_a: bfloat16 [2, 8, 512, 512], P(None, 'pipe'), may hold values from -0.25 to 0.25
- weights_b: bfloat16 [2, 8, 512, 512], P(None, 'pipe'), may hold values from -0.25 to 0.25
Outputs:
- grads_a: float32 [2, 8, 512, 512], P(None, 'pipe', 'dp')
- grads_b: float32 [2, 8, 512, 512], P(None, 'pipe', 'dp')
All inputs are finite; a program needn't handle non-finite values.
Results may differ from a plain program's by a relative error of at most 0.023.
Values may be sent and summed in bfloat16 or wider, within the bound.
No kernel may reach another device: no remote copies, remote signals or barrier semaphores. Data moves between devices by JAX's collectives and lax.ppermute only.
A program may use at most 64 MiB of HBM per device.

v0:
```python
import math

import jax
import jax.numpy as jnp
from jax import lax
from jax.sharding import PartitionSpec as P

EPS = 1e-06


def shifted(block, axis, distance):
    devices = range(lax.axis_size(axis))
    route = [(i - distance, i) for i in devices if i - distance in devices]
    return lax.ppermute(block, axis, route)


def run_block(section_in, weight_a, weight_b):
    inv_rms = lax.rsqrt(jnp.mean(section_in * section_in, axis=-1, keepdims=True) + EPS)
    normed = section_in * inv_rms
    normed_low = normed.astype(jnp.bfloat16)
    pre_act = jnp.dot(normed_low, weight_a, preferred_element_type=jnp.float32)
    hidden = jax.nn.silu(pre_act).astype(jnp.bfloat16)
    branch = jnp.dot(hidden, weight_b, preferred_element_type=jnp.float32)
    return (
        (section_in + branch).astype(jnp.bfloat16),
        (inv_rms, normed, normed_low, pre_act, hidden),
    )


def back_block(grad_out, saved, weight_a, weight_b):
    inv_rms, normed, normed_low, pre_act, hidden = saved
    grad_hidden = jnp.dot(grad_out, weight_b.T, preferred_element_type=jnp.float32)
    grad_b = jnp.dot(hidden.T, grad_out, preferred_element_type=jnp.float32)
    sigmoid_z = jax.nn.sigmoid(pre_act)
    grad_pre = (grad_hidden * sigmoid_z * (1.0 + pre_act * (1.0 - sigmoid_z))).astype(jnp.bfloat16)
    grad_a = jnp.dot(normed_low.T, grad_pre, preferred_element_type=jnp.float32)
    grad_normed = jnp.dot(grad_pre, weight_a.T, preferred_element_type=jnp.float32)
    grad_input = grad_out.astype(jnp.float32) + inv_rms * (
        grad_normed - normed * jnp.mean(grad_normed * normed, axis=-1, keepdims=True)
    )
    return (grad_input.astype(jnp.bfloat16), grad_a, grad_b)


def take_slot(stack_tree, slot_index):
    return jax.tree.map(
        lambda a: lax.dynamic_index_in_dim(a, slot_index, 0, keepdims=False), stack_tree
    )


def put_slot(stack_tree, slot_index, is_live, value_tree):

    def update(target, value):
        old_value = lax.dynamic_index_in_dim(target, slot_index, 0, keepdims=False)
        return lax.dynamic_update_index_in_dim(
            target, jnp.where(is_live, value, old_value), slot_index, 0
        )

    return jax.tree.map(update, stack_tree, value_tree)


def zero_saved(row_count, feature_width):
    return (
        jnp.zeros((row_count, 1), jnp.float32),
        jnp.zeros((row_count, feature_width), jnp.float32),
        jnp.zeros((row_count, feature_width), jnp.bfloat16),
        jnp.zeros((row_count, feature_width), jnp.float32),
        jnp.zeros((row_count, feature_width), jnp.bfloat16),
    )


def local(pixels, cotangent, weights_a, weights_b):
    pipe_count = lax.axis_size("pipe")
    pipe_index = lax.axis_index("pipe")
    micro_count = pixels.shape[0]
    row_count = pixels.shape[1]
    feature_width = pixels.shape[2]
    sweep_length = micro_count + pipe_count - 1
    enc_a, enc_b = (weights_a[0, 0], weights_b[0, 0])
    dec_a, dec_b = (weights_a[1, 0], weights_b[1, 0])
    zero_rows = jnp.zeros((row_count, feature_width), jnp.bfloat16)
    zero_square = jnp.zeros((feature_width, feature_width), jnp.float32)
    saved_blank = jax.tree.map(
        lambda a: jnp.zeros((micro_count,) + a.shape, a.dtype), zero_saved(row_count, feature_width)
    )
    stack_blank = jnp.zeros((micro_count, row_count, feature_width), jnp.bfloat16)

    def slot_of(tick, offset):
        batch_index = tick - offset
        is_live = (batch_index >= 0) & (batch_index < micro_count)
        return (jnp.clip(batch_index, 0, micro_count - 1), is_live)

    def enc_step(tick, state_tuple):
        received, enc_outputs, enc_inputs, saved_stack = state_tuple
        batch_slot, is_live = slot_of(tick, pipe_index)
        current = jnp.where(pipe_index == 0, take_slot(pixels, batch_slot), received)
        section_out, saved = lax.cond(
            is_live,
            lambda: run_block(current.astype(jnp.float32), enc_a, enc_b),
            lambda: (zero_rows, zero_saved(row_count, feature_width)),
        )
        enc_outputs = put_slot(enc_outputs, batch_slot, is_live, section_out)
        enc_inputs = put_slot(enc_inputs, batch_slot, is_live, current)
        saved_stack = put_slot(saved_stack, batch_slot, is_live, saved)
        received = shifted(section_out, "pipe", 1)
        return (received, enc_outputs, enc_inputs, saved_stack)

    state_tuple = lax.fori_loop(
        0, sweep_length, enc_step, (zero_rows, stack_blank, stack_blank, saved_blank)
    )
    enc_outputs, enc_inputs, enc_saved = (state_tuple[1], state_tuple[2], state_tuple[3])

    def dec_step(tick, state_tuple):
        received, dec_inputs, saved_stack = state_tuple
        batch_slot, is_live = slot_of(tick, pipe_count - 1 - pipe_index)
        skip_in = take_slot(enc_outputs, batch_slot)
        flowing = jnp.where(pipe_index == pipe_count - 1, skip_in, received)
        section_out, saved = lax.cond(
            is_live,
            lambda: run_block(
                flowing.astype(jnp.float32) + skip_in.astype(jnp.float32), dec_a, dec_b
            ),
            lambda: (zero_rows, zero_saved(row_count, feature_width)),
        )
        dec_inputs = put_slot(dec_inputs, batch_slot, is_live, flowing)
        saved_stack = put_slot(saved_stack, batch_slot, is_live, saved)
        received = shifted(section_out, "pipe", -1)
        return (received, dec_inputs, saved_stack)

    state_tuple = lax.fori_loop(0, sweep_length, dec_step, (zero_rows, stack_blank, saved_blank))
    dec_inputs, dec_saved = (state_tuple[1], state_tuple[2])

    def dec_back_step(tick, state_tuple):
        received, skip_grads, sum_a, sum_b = state_tuple
        batch_slot, is_live = slot_of(tick, pipe_index)
        grad_out = jnp.where(pipe_index == 0, take_slot(cotangent, batch_slot), received)

        def dec_live_branch():
            saved = take_slot(dec_saved, batch_slot)
            return back_block(grad_out, saved, dec_a, dec_b)

        grad_in, grad_a, grad_b = lax.cond(
            is_live, dec_live_branch, lambda: (zero_rows, zero_square, zero_square)
        )
        skip_grads = put_slot(skip_grads, batch_slot, is_live, grad_in)
        received = shifted(grad_in, "pipe", 1)
        return (received, skip_grads, sum_a + grad_a, sum_b + grad_b)

    state_tuple = lax.fori_loop(
        0, sweep_length, dec_back_step, (zero_rows, stack_blank, zero_square, zero_square)
    )
    skip_grads, dec_sum_a, dec_sum_b = (state_tuple[1], state_tuple[2], state_tuple[3])
    factor = 1.0 / math.sqrt(micro_count * row_count * lax.axis_size("dp"))

    def enc_back_step(tick, state_tuple):
        received, sum_a, sum_b = state_tuple
        batch_slot, is_live = slot_of(tick, pipe_count - 1 - pipe_index)
        skip_grad = take_slot(skip_grads, batch_slot)
        grad_next = jnp.where(pipe_index == pipe_count - 1, skip_grad, received)
        grad_out = (grad_next.astype(jnp.float32) + skip_grad.astype(jnp.float32)).astype(
            jnp.bfloat16
        )

        def enc_live_branch():
            saved = take_slot(enc_saved, batch_slot)
            return back_block(grad_out, saved, enc_a, enc_b)

        grad_in, grad_a, grad_b = lax.cond(
            is_live, enc_live_branch, lambda: (zero_rows, zero_square, zero_square)
        )
        received = shifted(grad_in, "pipe", -1)
        return (received, sum_a + grad_a, sum_b + grad_b)

    state_tuple = lax.fori_loop(
        0, sweep_length, enc_back_step, (zero_rows, zero_square, zero_square)
    )
    enc_sum_a, enc_sum_b = (state_tuple[1], state_tuple[2])
    enc_part_a, enc_part_b, dec_part_a, dec_part_b = (
        lax.psum_scatter(enc_sum_a, "dp", scatter_dimension=0, tiled=True),
        lax.psum_scatter(enc_sum_b, "dp", scatter_dimension=0, tiled=True),
        lax.psum_scatter(dec_sum_a, "dp", scatter_dimension=0, tiled=True),
        lax.psum_scatter(dec_sum_b, "dp", scatter_dimension=0, tiled=True),
    )
    grads_a = jnp.stack([enc_part_a, dec_part_a])[:, None] * factor
    grads_b = jnp.stack([enc_part_b, dec_part_b])[:, None] * factor
    return (grads_a, grads_b)


def solution(mesh):
    return jax.shard_map(
        local,
        mesh=mesh,
        in_specs=(
            P(None, "dp", None),
            P(None, "dp", None),
            P(None, "pipe", None, None),
            P(None, "pipe", None, None),
        ),
        out_specs=(P(None, "pipe", "dp", None), P(None, "pipe", "dp", None)),
        check_vma=False,
    )
```

profile of v0, /device:TPU:16, one launch (start us, length us, event | category | flops | bytes accessed | tf_op | source)
XLA Modules:
  0.0 1261.5 jit_solution(13690936574438050144)
XLA Ops:
  9.9 108.6 %while.92 = (s32[]{:T(128)}, bf16[32,512]{1,0:T(8,128)(2,1)S(1)}, bf16[4,32,512]{2,1,0:T(8,128)(2,1)S(1)}, f32[4,32,1]{1,2,0:T(1,128)S(1)}, f32[4,32,512]{2,1,0:...) while((s32[]{:T(128)}, bf16[32,512]{1,0:T(8,128)(2,1)S(1)}, ...), condition=%wide.region_4.5_spmd, body=%wide.region_0.4_spmd.sunk | while | flops 33882184 | bytes 3050316 | solution.py:107
  39.7 8.2 collective-permute-done
  53.6 5.3 collective-permute-done
  64.6 5.3 collective-permute-done
  75.6 5.3 collective-permute-done
  103.9 5.7 collective-permute-done
  112.5 6.0 collective-permute-done
  121.5 105.5 %while.93 = (s32[]{:T(128)}, bf16[32,512]{1,0:T(8,128)(2,1)S(1)}, f32[4,32,1]{1,2,0:T(1,128)S(1)}, f32[4,32,512]{2,1,0:T(8,128)}, bf16[4,32,512]{2,1,0:T(8,128)(...) while((s32[]{:T(128)}, bf16[32,512]{1,0:T(8,128)(2,1)S(1)}, ...), condition=%wide.region_9.10_spmd, body=%wide.region_5.9_spmd.sunk | while | flops 33996872 | bytes 2920253 | solution.py:129
  130.1 5.6 collective-permute-start.1
  227.6 137.1 %while.94 = (s32[]{:T(128)}, bf16[32,512]{1,0:T(8,128)(2,1)S(1)}, bf16[4,32,512]{2,1,0:T(8,128)(2,1)}, f32[512,512]{1,0:T(8,128)}, f32[512,512]{1,0:T(8,128)}, /...) while((s32[]{:T(128)}, bf16[32,512]{1,0:T(8,128)(2,1)S(1)}, ...), condition=%wide.region_14.15_spmd.clone, body=%wide.region_10.14_spmd.clone.sunk | while | flops 68468744 | bytes 10454865 | solution.py:148
  263.0 9.5 collective-permute-done.2
  272.5 6.4 conditional.12
  287.1 6.4 conditional.12
  301.7 6.4 conditional.12
  316.4 6.4 conditional.12
  331.2 7.2 collective-permute-start.2
  351.9 8.1 collective-permute-start.2
  365.8 120.8 %while.95 = (s32[]{:T(128)}, bf16[32,512]{1,0:T(8,128)(2,1)S(1)}, f32[512,512]{1,0:T(8,128)}, f32[512,512]{1,0:T(8,128)}, s32[]{:T(128)}, /*index=5*/pred[]{:T(5...) while((s32[]{:T(128)}, bf16[32,512]{1,0:T(8,128)(2,1)S(1)}, ...), condition=%wide.region_19.20_spmd.clone, body=%wide.region_15.19_spmd.clone.sunk | while | flops 68517896 | bytes 10290484 | solution.py:173
  390.9 6.8 collective-permute-done.3
  448.9 6.4 collective-permute-start.3
  487.9 105.7 %reduce-scatter.7.cloned.1.call-done = f32[8,512]{1,0:T(8,128)} async-done(((f32[512,512]{1,0:T(8,128)}), f32[8,512]{1,0:T(8,128)}) %reduce-scatter.7.cloned.1.call-update) | async-done | bytes 16400 | tf_op jit(solution)/shard_map/reduce_scatter | solution.py:180
  593.6 220.5 %reduce-scatter.5.cloned.1.call-done = f32[8,512]{1,0:T(8,128)} async-done(((f32[512,512]{1,0:T(8,128)}), f32[8,512]{1,0:T(8,128)}) %reduce-scatter.5.cloned.1.call-update) | async-done | bytes 16400 | tf_op jit(solution)/shard_map/reduce_scatter | solution.py:178
  815.4 218.0 %reduce-scatter.11.cloned.1.call-done = f32[8,512]{1,0:T(8,128)} async-done(((f32[512,512]{1,0:T(8,128)}), f32[8,512]{1,0:T(8,128)}) %reduce-scatter.11.cloned.1.call-update) | async-done | bytes 16400 | tf_op jit(solution)/shard_map/reduce_scatter | solution.py:181
  1033.4 220.1 %reduce-scatter.9.cloned.1.call-done = f32[8,512]{1,0:T(8,128)} async-done(((f32[512,512]{1,0:T(8,128)}), f32[8,512]{1,0:T(8,128)}) %reduce-scatter.9.cloned.1.call-update) | async-done | bytes 16400 | tf_op jit(solution)/shard_map/reduce_scatter | solution.py:179
  (668 shorter events, 449.5 us)
Async XLA Ops:
  7.2 586.4 %reduce-scatter.7.cloned.1.call-start = ((), (), s32[]{:S(2)}) async-start(), calls=%async_computation.5 | async-start | bytes 1064960 | tf_op jit(solution)/shard_map/reduce_scatter | solution.py:180
  37.2 10.7 collective-permute-start
  50.7 8.2 collective-permute-start
  61.7 8.2 collective-permute-start
  83.7 8.2 collective-permute-start
  130.1 10.2 collective-permute-start.1
  191.3 9.1 collective-permute-start.1
  227.9 8.2 collective-permute-start.2
  236.3 8.4 collective-permute-start.2
  245.0 9.5 collective-permute-start.2
  254.8 17.7 %collective-permute-start.2 = (bf16[32,512]{1,0:T(8,128)(2,1)S(1)}, bf16[32,512]{1,0:T(8,128)(2,1)S(1)}, u32[]{:S(2)}, u32[]{:S(2)}) collective-permute-start(bf16[32,512]{1,0:T(8,128)(2,1)S(1)} %get-tuple-element.1952), channel_id=1, source_target_pairs={{0,1},{1,2},{2,3},{3,4},{4,5},{5,6},{6,7},{8,9},{9,10},{10,11},{11... | collective-permute-start | bytes 98312 | tf_op jit(solution)/shard_map/while/body/eval_jaxpr/ppermute | solution.py:14
  278.9 8.2 collective-permute-start.2
  293.5 8.2 collective-permute-start.2
  308.1 8.2 collective-permute-start.2
  322.8 8.2 collective-permute-start.2
  331.2 11.9 collective-permute-start.2
  351.9 12.8 %collective-permute-start.2 = (bf16[32,512]{1,0:T(8,128)(2,1)S(1)}, bf16[32,512]{1,0:T(8,128)(2,1)S(1)}, u32[]{:S(2)}, u32[]{:S(2)}) collective-permute-start(bf16[32,512]{1,0:T(8,128)(2,1)S(1)} %get-tuple-element.1952), channel_id=1, source_target_pairs={{0,1},{1,2},{2,3},{3,4},{4,5},{5,6},{6,7},{8,9},{9,10},{10,11},{11... | collective-permute-start | bytes 98312 | tf_op jit(solution)/shard_map/while/body/eval_jaxpr/ppermute | solution.py:14
  364.7 449.3 %reduce-scatter.5.cloned.1.call-start = ((), (), s32[]{:S(2)}) async-start(), calls=%async_computation.4 | async-start | bytes 1064960 | tf_op jit(solution)/shard_map/reduce_scatter | solution.py:178
  383.6 14.1 %collective-permute-start.3 = (bf16[32,512]{1,0:T(8,128)(2,1)S(1)}, bf16[32,512]{1,0:T(8,128)(2,1)S(1)}, u32[]{:S(2)}, u32[]{:S(2)}) collective-permute-start(bf16[32,512]{1,0:T(8,128)(2,1)S(1)} %get-tuple-element.1971), channel_id=1, source_target_pairs={{1,0},{2,1},{3,2},{4,3},{5,4},{6,5},{7,6},{9,8},{10,9},{11,10},{12... | collective-permute-start | bytes 98312 | tf_op jit(solution)/shard_map/while/body/eval_jaxpr/ppermute | solution.py:14
  415.0 8.3 collective-permute-start.3
  448.9 9.7 collective-permute-start.3
  469.0 8.3 collective-permute-start.3
  486.5 546.9 %reduce-scatter.11.cloned.1.call-start = ((), (), s32[]{:S(2)}) async-start(), calls=%async_computation.7 | async-start | bytes 1064960 | tf_op jit(solution)/shard_map/reduce_scatter | solution.py:181
  487.3 766.3 %reduce-scatter.9.cloned.1.call-start = ((), (), s32[]{:S(2)}) async-start(), calls=%async_computation.6 | async-start | bytes 1064960 | tf_op jit(solution)/shard_map/reduce_scatter | solution.py:179
  (45 other events, 220.5 us)
Sparse Core Ops, SparseCore 0:
  364.9 228.6 reduce-scatter.6
  596.6 217.4 reduce-scatter.4
  816.9 216.5 reduce-scatter.10
  1036.3 217.2 reduce-scatter.8
where the time goes:
time: 1270 us; the launch traced here: 1260 us
  waiting for transfers between devices  864 us (68%)
  starting transfers between devices  145 us (11%)
  other arithmetic  122 us (10%)
  local copies, waits for them, and re-layouts  64.5 us (5%)
  matrix products  48.7 us (4%)
  between operations  13.9 us (1%)
    reduce_scatter x1, waiting for transfers between devices, local(): lax.psum_scatter(enc_sum_a, 'dp', scatter_dimension=0, tiled=True)  220 us
    reduce_scatter x1, waiting for transfers between devices, local(): lax.psum_scatter(enc_sum_b, 'dp', scatter_dimension=0, tiled=True)  220 us
    reduce_scatter x1, waiting for transfers between devices, local(): lax.psum_scatter(dec_sum_b, 'dp', scatter_dimension=0, tiled=True)  218 us
    ppermute x44, starting transfers between devices, shifted(): return lax.ppermute(block, axis, route)  144 us
    reduce_scatter x1, waiting for transfers between devices, local(): lax.psum_scatter(dec_sum_a, 'dp', scatter_dimension=0, tiled=True)  106 us
    ppermute x44, waiting for transfers between devices, shifted(): return lax.ppermute(block, axis, route)  98.7 us
    dynamic_slice x110, local copies, waits for them, and re-layouts, update(): old_value = lax.dynamic_index_in_dim(target, slot_index, 0, keepdims=False)  44.5 us
    add x11, other arithmetic, enc_back_step(): return (received, sum_a + grad_a, sum_b + grad_b)  35.5 us
  transfers between devices with their start and end apart: 48, of which 32 were waited for; matrix products, arithmetic and copies ran while one was open for 13% of the time, Pallas kernels for 0%

commit v1 on v0

v1 whole, which is shorter than its diff:
```python
import functools
import math

import jax
import jax.numpy as jnp
from jax import lax
from jax.experimental import pallas as pl
from jax.experimental.pallas import tpu as pltpu
from jax.sharding import PartitionSpec as P

EPS = 1e-06
LEVELS = 4
ROWS = 32
WIDTH = 512
HALF = WIDTH // 2
BF16 = jnp.bfloat16
F32 = jnp.float32
VMEM_BYTES = 48 * 1024 * 1024


def dot(a, b):
    return jnp.dot(a, b, preferred_element_type=F32)


def dot_t(a, b):
    return lax.dot_general(a, b, (((1,), (1,)), ((), ())), preferred_element_type=F32)


def t_dot(a, b):
    return lax.dot_general(a, b, (((0,), (0,)), ((), ())), preferred_element_type=F32)


def forward_level(v, weight, save, slot):
    save_q, save_z, save_r = save
    r = lax.rsqrt(jnp.mean(v * v, axis=-1, keepdims=True) + EPS)
    q = v * r
    z = dot(q.astype(BF16), weight[0])
    h = (z * jax.nn.sigmoid(z)).astype(BF16)
    save_q[slot] = q
    save_z[slot] = z
    save_r[slot] = jnp.broadcast_to(r, (ROWS, 128))
    return (v + dot(h, weight[1])).astype(BF16)


def backward_level(g, weight, save, slot, acts, last=False):
    save_q, save_z, save_r = save
    gh = dot_t(g, weight[1])
    z = save_z[slot]
    s = jax.nn.sigmoid(z)
    gz = (gh * s * (1.0 + z * (1.0 - s))).astype(BF16)
    q = save_q[slot]
    acts[slot, 0] = q.astype(BF16)
    acts[slot, 1] = gz
    acts[slot, 2] = (z * s).astype(BF16)
    acts[slot, 3] = g
    gn = dot_t(gz, weight[0])
    r = save_r[slot][:, :1]
    return (g.astype(F32) + r * (gn - q * jnp.mean(gn * q, axis=-1, keepdims=True))).astype(BF16)


def start_weights(place, weights, side, held, sems, order):
    own_a, own_b, *pieces = weights
    both = pl.ds(2 * side, 2)
    near = (pieces[0].at[both], pieces[2].at[both], pieces[4 + 2 * side])
    far = (pieces[1].at[both], pieces[3].at[both], pieces[5 + 2 * side])

    def start(m, apart):
        if apart == 0:
            pltpu.make_async_copy(own_a.at[side, 0], held.at[m, 0], sems.at[m]).start()
            pltpu.make_async_copy(own_b.at[side, 0], held.at[m, 1], sems.at[m]).start()
            return
        for part, core in ((near[apart - 1], place[2]), (far[apart - 1], 1 - place[2])):
            rows = pl.ds(pl.multiple_of(core * HALF, HALF), HALF)
            pltpu.make_async_copy(part, held.at[m, :, rows, :], sems.at[m]).start()

    for m in order:
        for apart in range(LEVELS):
            pl.when(place[1] == (m ^ apart))(functools.partial(start, m, apart))


def wait_weights(held, sems, m):
    pltpu.make_async_copy(held.at[m], held.at[m], sems.at[m]).wait()
    return held.at[m]


UP = tuple(range(LEVELS))
DOWN = tuple(reversed(UP))
N_WEIGHTS = 10


def own_level_kernel(level, place, x, own_a, own_b, out, held, sems):
    @pl.when(place[3] == level)
    def _():
        copies = [
            pltpu.make_async_copy(own.at[0, 0], held.at[i], sems.at[i]) for i, own in enumerate((own_a, own_b))
        ]
        for copy in copies:
            copy.start()
        v = x[...].reshape(LEVELS * ROWS, WIDTH).astype(F32)
        n = (v * lax.rsqrt(jnp.mean(v * v, axis=-1, keepdims=True) + EPS)).astype(BF16)
        copies[0].wait()
        z = dot(n, held[0])
        h = (z * jax.nn.sigmoid(z)).astype(BF16)
        copies[1].wait()
        out[...] = (v + dot(h, held[1])).astype(BF16).reshape(LEVELS, ROWS, WIDTH)


def forward_kernel(place, pixels, *refs):
    arrived, weights, refs = refs[:LEVELS], refs[LEVELS : LEVELS + N_WEIGHTS], refs[LEVELS + N_WEIGHTS :]
    hop, e, qe, ze, re, qd, zd, rd, held_e, held_d, sems_e, sems_d = refs
    late = place[0] == 1
    start_weights(place, weights, 0, held_e, sems_e, UP)
    pl.when(late)(lambda: start_weights(place, weights, 1, held_d, sems_d, DOWN))
    x = jnp.where(late, sum(a[...].astype(F32) for a in arrived), pixels[place[1]].astype(F32))
    for m in UP:
        x = forward_level(x.astype(F32), wait_weights(held_e, sems_e, m), (qe, ze, re), m)
        e[m] = x

    @pl.when(late)
    def _():
        d = e[LEVELS - 1]
        for m in DOWN:
            v = d.astype(F32) + e[m].astype(F32)
            d = forward_level(v, wait_weights(held_d, sems_d, m), (qd, zd, rd), m)
        hop[...] = d


def turn_dec_kernel(place, arrived, e, cotangent, *refs):
    weights, refs = refs[:N_WEIGHTS], refs[N_WEIGHTS:]
    hop, skip_grads, acts, held, sems, q, z, r, local_acts, acts_sem = refs

    @pl.when(place[0] == 0)
    def _():
        start_weights(place, weights, 1, held, sems, DOWN)
        x = arrived[...]
        for m in DOWN:
            v = x.astype(F32) + e[m].astype(F32)
            x = forward_level(v, wait_weights(held, sems, m), (q, z, r), m)
        g = cotangent[place[1]]
        for m in UP:
            g = backward_level(g, held.at[m], (q, z, r), m, local_acts)
            skip_grads[m] = g
        hop[...] = g
        out = pltpu.make_async_copy(local_acts, acts.at[:, 1], acts_sem)
        out.start()
        out.wait()


def enc_backward(g, skip_grads, weights, save, acts):
    for m in DOWN:
        g = (g.astype(F32) + skip_grads[m].astype(F32)).astype(BF16)
        g = backward_level(g, weights(m), save, m, acts)
    return g


def turn_backward_kernel(place, arrived, qe, ze, re, qd, zd, rd, *refs):
    weights, refs = refs[:N_WEIGHTS], refs[N_WEIGHTS + 1 :]
    hop, acts, held_e, held_d, sems_e, sems_d, acts_e, acts_d, acts_sems = refs

    @pl.when(place[0] == 1)
    def _():
        start_weights(place, weights, 1, held_d, sems_d, UP)
        start_weights(place, weights, 0, held_e, sems_e, DOWN)
        g = arrived[...]
        skip_grads = []
        for m in UP:
            g = backward_level(g, wait_weights(held_d, sems_d, m), (qd, zd, rd), m, acts_d)
            skip_grads.append(g)
        out_d = pltpu.make_async_copy(acts_d, acts.at[:, 1], acts_sems.at[1])
        out_d.start()
        hop[...] = enc_backward(
            g, skip_grads, lambda m: wait_weights(held_e, sems_e, m), (qe, ze, re), acts_e
        )
        out_e = pltpu.make_async_copy(acts_e, acts.at[:, 0], acts_sems.at[0])
        out_e.start()
        out_d.wait()
        out_e.wait()


def enc_backward_kernel(place, arrived, q, z, r, skip_grads, *refs):
    weights, refs = refs[:N_WEIGHTS], refs[N_WEIGHTS + 1 :]
    acts, held, sems, local_acts, acts_sem = refs

    @pl.when(place[0] == 0)
    def _():
        start_weights(place, weights, 0, held, sems, DOWN)
        enc_backward(
            arrived[...], skip_grads, lambda m: wait_weights(held, sems, m), (q, z, r), local_acts
        )
        out = pltpu.make_async_copy(local_acts, acts.at[:, 0], acts_sem)
        out.start()
        out.wait()


def grads_kernel(acts, out):
    rows = acts.shape[0] * ROWS
    grad = t_dot(acts[:, 0].reshape(rows, WIDTH), acts[:, 1].reshape(rows, WIDTH))
    for z_low in range(4):
        for z_high in range(4):
            for x in range(2):
                for core in range(2):
                    first = x * 256 + (z_high * 4 + z_low) * 16 + core * 8
                    out[z_low, x, core, z_high] = grad[first : first + 8].astype(BF16)


SMEM = pl.BlockSpec(memory_space=pltpu.SMEM)
VMEM = pl.BlockSpec(memory_space=pltpu.VMEM)
ANY = pl.BlockSpec(memory_space=pl.ANY)
PARAMS = pltpu.CompilerParams(vmem_limit_bytes=VMEM_BYTES)

ROW = jax.ShapeDtypeStruct((ROWS, WIDTH), BF16)
STACK = jax.ShapeDtypeStruct((LEVELS, ROWS, WIDTH), BF16)
SAVE = jax.ShapeDtypeStruct((LEVELS, ROWS, WIDTH), F32)
SAVE_R = jax.ShapeDtypeStruct((LEVELS, ROWS, 128), F32)
SAVES = (SAVE, SAVE, SAVE_R)
ACTS = jax.ShapeDtypeStruct((LEVELS, 2, 4, ROWS, WIDTH), BF16)

HELD = pltpu.VMEM((LEVELS, 2, WIDTH, WIDTH), BF16)
SEMS = pltpu.SemaphoreType.DMA((LEVELS,))
LOCAL_ACTS = pltpu.VMEM((LEVELS, 4, ROWS, WIDTH), BF16)
SCRATCH_SAVES = tuple(pltpu.VMEM(s.shape, s.dtype) for s in SAVES)


def call(kernel, operands, spaces, outs, out_spaces, scratch=(), aliases=None, name=None):
    return pl.pallas_call(
        kernel,
        out_shape=outs,
        in_specs=spaces,
        out_specs=out_spaces,
        scratch_shapes=scratch,
        input_output_aliases=aliases or {},
        compiler_params=PARAMS,
        name=name,
    )(*operands)


def local(pixels, cotangent, weights_a, weights_b):
    core = lax.axis_index("core")
    level = lax.axis_index(PIPE)
    place = jnp.stack([level // LEVELS, level % LEVELS, core, level]).astype(jnp.int32)

    half = jnp.stack(
        [
            lax.dynamic_slice_in_dim(w[side, 0], core * HALF, HALF, 0)
            for side in (0, 1)
            for w in (weights_a, weights_b)
        ]
    )

    def along_x(block):
        return lax.ppermute(block, ("x_lo", "x_hi"), [(i, 3 - i) for i in range(4)])

    def along_y(block):
        return lax.ppermute(block, "y_lo", [(0, 1), (1, 0)])

    from_x = along_x(half)
    from_y = along_y(half)

    x = pixels
    for k in range(LEVELS):
        if k:
            x = lax.ppermute(x, PIPE, [(k - 1, k)])
        x = call(
            functools.partial(own_level_kernel, k), (place, x, weights_a, weights_b), (SMEM, VMEM, ANY, ANY),
            STACK, VMEM, (pltpu.VMEM((2, WIDTH, WIDTH), BF16), pltpu.SemaphoreType.DMA((2,))), name="own_level",
        )
    x, from_x, from_y = lax.optimization_barrier((x, from_x, from_y))

    pieces = [from_x, from_y, along_y(from_x[:2]), along_x(from_y[2:])]
    pieces = [v for piece in pieces for v in (piece, lax.ppermute(piece, "core", [(0, 1), (1, 0)]))]
    weights = (weights_a, weights_b, *pieces)

    up = [(0, 3), (1, 2)]
    down = [(3, 0), (2, 1)]
    y = ("stage", "y_lo")
    arrived = [lax.ppermute(x[j], PIPE, [(LEVELS - 1, (3 - j // 2) * 2 + j % 2)]) for j in range(LEVELS)]

    hop, e, *saves = call(
        forward_kernel, (place, pixels, *arrived, *weights), (SMEM,) + (VMEM,) * 5 + (ANY,) * N_WEIGHTS,
        (ROW, STACK) + SAVES + SAVES, (VMEM,) * 8, (HELD, HELD, SEMS, SEMS), name="forward",
    )
    arrived = lax.ppermute(hop, y, down)
    hop, skip_grads, acts = call(
        turn_dec_kernel, (place, arrived, e, cotangent, *weights),
        (SMEM, VMEM, VMEM, VMEM) + (ANY,) * N_WEIGHTS,
        (ROW, STACK, ACTS), (VMEM, VMEM, ANY),
        (HELD, SEMS) + SCRATCH_SAVES + (LOCAL_ACTS, pltpu.SemaphoreType.DMA), name="turn_dec",
    )
    arrived = lax.ppermute(hop, y, up)
    hop, acts = call(
        turn_backward_kernel, (place, arrived, *saves, *weights, acts),
        (SMEM, VMEM) + (VMEM,) * 6 + (ANY,) * (N_WEIGHTS + 1),
        (ROW, ACTS), (VMEM, ANY),
        (HELD, HELD, SEMS, SEMS, LOCAL_ACTS, LOCAL_ACTS, pltpu.SemaphoreType.DMA((2,))),
        {8 + N_WEIGHTS: 1}, name="turn_backward",
    )
    arrived = lax.ppermute(hop, y, down)
    acts = call(
        enc_backward_kernel, (place, arrived, *saves[:3], skip_grads, *weights, acts),
        (SMEM, VMEM) + (VMEM,) * 4 + (ANY,) * (N_WEIGHTS + 1),
        ACTS, ANY, (HELD, SEMS, LOCAL_ACTS, pltpu.SemaphoreType.DMA), {6 + N_WEIGHTS: 0}, name="enc_backward",
    )

    acts = lax.all_to_all(acts.reshape(16, 2, ROWS, WIDTH), MEMBERS + ("x_lo", "core"), 0, 0)
    grad = call(
        grads_kernel, (acts,), (VMEM,), jax.ShapeDtypeStruct((4, 2, 2, 4, 8, WIDTH), BF16), VMEM, name="grads"
    )

    total = lax.all_to_all(grad.reshape(16, 4, 8, WIDTH), ("z_lo", "x_lo", "core"), 0, 0)
    total = jnp.sum(total.astype(F32).reshape(4, 4, 4, 8, WIDTH), axis=0).astype(BF16)
    total = lax.all_to_all(total.transpose(1, 0, 2, 3), "z_hi", 0, 0)
    factor = 1.0 / math.sqrt(LEVELS * ROWS * 64)
    total = jnp.sum(total.astype(F32), axis=0).reshape(2, 2, 1, 8, WIDTH) * factor
    return total[:, 0], total[:, 1]


MEMBERS = ("y_lo", "x_hi")
DP = ("x_lo", "z_hi", "z_lo", "core")
PIPE = ("stage", "y_lo", "x_hi")


def solution(mesh):
    fine = jax.sharding.Mesh(mesh.devices.reshape(2, 4, 4, 2, 2, 2, 2), DP + PIPE)
    return jax.shard_map(
        local,
        mesh=fine,
        in_specs=(
            P(None, DP, None),
            P(None, DP, None),
            P(None, PIPE, None, None),
            P(None, PIPE, None, None),
        ),
        out_specs=(P(None, PIPE, DP, None), P(None, PIPE, DP, None)),
        check_vma=False,
    )
```

time: 1270 us -> 178 us (0.14)
  the two profiles are of different devices: /device:TPU:16 before, /device:TPU:33 now
where the time goes in v1:
time: 178 us; the launch traced here: 177 us
  blocking collectives  70.6 us (40%)
  waiting for transfers between devices  44.5 us (25%)
  starting transfers between devices  39 us (22%)
  Pallas kernels  15.5 us (9%)
  local copies, waits for them, and re-layouts  5.37 us (3%)
    all_to_all x1, blocking collectives, local(): total = lax.all_to_all(total.transpose(1, 0, 2, 3), 'z_hi', 0, 0)  26.9 us
    ppermute x2, waiting for transfers between devices, local(): arrived = lax.ppermute(hop, y, down)  23.3 us
    all_to_all x1, blocking collectives, local(): lax.all_to_all(acts.reshape(16, 2, ROWS, WIDTH), MEMBERS + ('x_lo', 'core...  23 us
    all_to_all x1, blocking collectives, local(): lax.all_to_all(grad.reshape(16, 4, 8, WIDTH), ('z_lo', 'x_lo', 'core'), 0...  20.7 us
    pallas_call x9, Pallas kernels, call(): pl.pallas_call(kernel, out_shape=outs, in_specs=spaces, out_specs=out_spa...  15.5 us
    ppermute x4, starting transfers between devices, local(): lax.ppermute(piece, 'core', [(0, 1), (1, 0)])  15.2 us
    ppermute x2, waiting for transfers between devices, along_y(): return lax.ppermute(block, 'y_lo', [(0, 1), (1, 0)])  12.4 us
    ppermute x2, starting transfers between devices, along_x(): return lax.ppermute(block, ('x_lo', 'x_hi'), [(i, 3 - i) for i in range(4)])  8.77 us
  transfers between devices with their start and end apart: 18, of which 7 were waited for; matrix products, arithmetic and copies ran while one was open for 1% of the time, Pallas kernels for 2%

profile of v1, /device:TPU:33, one launch (start us, length us, event | category | flops | bytes accessed | tf_op | source)
XLA Modules:
  0.0 177.2 jit_solution(9195980370293083176)
XLA Ops:
  0.6 1.4 fusion
  3.5 3.2 %collective-permute-start.4 = (bf16[4,256,512]{2,1,0:T(8,128)(2,1)}, bf16[4,256,512]{2,1,0:T(8,128)(2,1)S(1)}, u32[]{:S(2)}, u32[]{:S(2)}) collective-permute-start(bf16[4,256,512]{2,1,0:T(8,128)(2,1)} %pad_maximum_fusion), channel_id=1, source_target_pairs={{0,2},{2,0},{1,3},{3,1},{4,6},{6,4},{5,7},{7,5},{8,10},{10,8},{9,1... | collective-permute-start | bytes 3145736 | tf_op jit(solution)/shard_map/ppermute | solution.py:254
  6.7 4.4 %collective-permute-start.3 = (bf16[4,256,512]{2,1,0:T(8,128)(2,1)}, bf16[4,256,512]{2,1,0:T(8,128)(2,1)}, u32[]{:S(2)}, u32[]{:S(2)}) collective-permute-start(bf16[4,256,512]{2,1,0:T(8,128)(2,1)} %pad_maximum_fusion), channel_id=1, source_target_pairs={{0,257},{1,256},{256,1},{257,0},{2,259},{3,258},{258,3},{259,2},{4... | collective-permute-start | bytes 3145736 | tf_op jit(solution)/shard_map/ppermute | solution.py:251
  12.4 1.8 collective-permute-start
  14.2 1.9 %collective-permute-done.x = bf16[4,32,512]{2,1,0:T(8,128)(2,1)S(1)} collective-permute-done((bf16[4,32,512]{2,1,0:T(8,128)(2,1)S(1)}, bf16[4,32,512]{2,1,0:T(8,128)(2,1)S(1)}, u32[]{:S(2)}, u32[]{:S(2)}) %collective-permute-start) | collective-permute-done | bytes 131104 | tf_op jit(solution)/shard_map/ppermute | solution.py:262
  19.2 12.4 %collective-permute-done.4.refs_8_.refs_4_ = bf16[4,256,512]{2,1,0:T(8,128)(2,1)S(1)} collective-permute-done((bf16[4,256,512]{2,1,0:T(8,128)(2,1)}, bf16[4,256,512]{2,1,0:T(8,128)(2,1)S(1)}, u32[]{:S(2)}, u32[]{:S(2)}) %collective-permute-start.4) | collective-permute-done | bytes 1048608 | tf_op jit(solution)/shard_map/ppermute | solution.py:254
  31.6 5.0 %collective-permute-done.3.refs_6_.refs_2_ = bf16[4,256,512]{2,1,0:T(8,128)(2,1)} collective-permute-done((bf16[4,256,512]{2,1,0:T(8,128)(2,1)}, bf16[4,256,512]{2,1,0:T(8,128)(2,1)}, u32[]{:S(2)}, u32[]{:S(2)}) %collective-permute-start.3) | collective-permute-done | bytes 1048608 | tf_op jit(solution)/shard_map/ppermute | solution.py:251
  36.6 4.4 %collective-permute-start.13 = (bf16[2,256,512]{2,1,0:T(8,128)(2,1)S(1)}, bf16[2,256,512]{2,1,0:T(8,128)(2,1)S(1)}, u32[]{:S(2)}, u32[]{:S(2)}) collective-permute-start(bf16[2,256,512]{2,1,0:T(8,128)(2,1)S(1)} %slice.45), channel_id=1, source_target_pairs={{0,257},{1,256},{256,1},{257,0},{2,259},{3,258},{258,3},{259,2},{4... | collective-permute-start | bytes 1572872 | tf_op jit(solution)/shard_map/ppermute | solution.py:251
  42.1 2.1 %collective-permute-start.11 = (bf16[2,256,512]{2,1,0:T(8,128)(2,1)S(1)}, bf16[2,256,512]{2,1,0:T(8,128)(2,1)S(1)}, u32[]{:S(2)}, u32[]{:S(2)}) collective-permute-start(bf16[2,256,512]{2,1,0:T(8,128)(2,1)S(1)} %slice.44), channel_id=1, source_target_pairs={{0,2},{2,0},{1,3},{3,1},{4,6},{6,4},{5,7},{7,5},{8,10},{10,8},{9,1... | collective-permute-start | bytes 1572872 | tf_op jit(solution)/shard_map/ppermute | solution.py:254
  44.2 4.3 %collective-permute-start.9 = (bf16[4,256,512]{2,1,0:T(8,128)(2,1)}, bf16[4,256,512]{2,1,0:T(8,128)(2,1)S(1)}, u32[]{:S(2)}, u32[]{:S(2)}) collective-permute-start(bf16[4,256,512]{2,1,0:T(8,128)(2,1)} %collective-permute-done.3.refs_6_.refs_2_), channel_id=1, source_target_pairs={{0,8},{8,0},{1,9},{9,1},{2,10},{10,2},{3,11},{11,3},{4,12},{12,4},... | collective-permute-start | bytes 3145736 | tf_op jit(solution)/shard_map/ppermute | solution.py:270
  48.6 1.9 %collective-permute-start.10 = (bf16[4,256,512]{2,1,0:T(8,128)(2,1)S(1)}, bf16[4,256,512]{2,1,0:T(8,128)(2,1)S(1)}, u32[]{:S(2)}, u32[]{:S(2)}) collective-permute-start(bf16[4,256,512]{2,1,0:T(8,128)(2,1)S(1)} %collective-permute-done.4.refs_8_.refs_4_), channel_id=1, source_target_pairs={{0,8},{8,0},{1,9},{9,1},{2,10},{10,2},{3,11},{11,3},{4,12},{12,4},... | collective-permute-start | bytes 3145736 | tf_op jit(solution)/shard_map/ppermute | solution.py:270
  51.3 4.7 %collective-permute-start.14 = (bf16[2,256,512]{2,1,0:T(8,128)(2,1)S(1)}, bf16[2,256,512]{2,1,0:T(8,128)(2,1)S(1)}, u32[]{:S(2)}, u32[]{:S(2)}) collective-permute-start(bf16[2,256,512]{2,1,0:T(8,128)(2,1)S(1)} %collective-permute-done.13.refs_12_.refs_8_), channel_id=1, source_target_pairs={{0,8},{8,0},{1,9},{9,1},{2,10},{10,2},{3,11},{11,3},{4,12},{12,4},... | collective-permute-start | bytes 1572872 | tf_op jit(solution)/shard_map/ppermute | solution.py:270
  56.0 4.2 %collective-permute-start.12 = (bf16[2,256,512]{2,1,0:T(8,128)(2,1)S(1)}, bf16[2,256,512]{2,1,0:T(8,128)(2,1)S(1)}, u32[]{:S(2)}, u32[]{:S(2)}) collective-permute-start(bf16[2,256,512]{2,1,0:T(8,128)(2,1)S(1)} %collective-permute-done.11.refs_10_.refs_6_), channel_id=1, source_target_pairs={{0,8},{8,0},{1,9},{9,1},{2,10},{10,2},{3,11},{11,3},{4,12},{12,4},... | collective-permute-start | bytes 1572872 | tf_op jit(solution)/shard_map/ppermute | solution.py:270
  65.1 3.2 %forward.1 = (bf16[32,512]{1,0:T(8,128)(2,1)S(1)}, bf16[4,32,512]{2,1,0:T(8,128)(2,1)S(1)}, f32[4,32,512]{2,1,0:T(8,128)S(1)}, f32[4,32,512]{2,1,0:T(8,128)S(1)}...) custom-call(s32[4]{0:T(128)S(1)} %pad_add_fusion.place, ...), custom_call_target="tpu_custom_call" | custom-call | tf_op jit(solution)/shard_map/forward/pallas_call | solution.py:225
  68.3 1.3 collective-permute-start.15
  69.6 13.3 %collective-permute-done.15.arrived = bf16[32,512]{1,0:T(8,128)(2,1)S(1)} collective-permute-done((bf16[32,512]{1,0:T(8,128)(2,1)S(1)}, bf16[32,512]{1,0:T(8,128)(2,1)S(1)}, u32[]{:S(2)}, u32[]{:S(2)}) %collective-permute-start.15) | collective-permute-done | bytes 32800 | tf_op jit(solution)/shard_map/ppermute | solution.py:282
  82.9 4.9 %turn_dec.1 = (bf16[32,512]{1,0:T(8,128)(2,1)S(1)}, bf16[4,32,512]{2,1,0:T(8,128)(2,1)S(1)}, bf16[4,2,4,32,512]{4,3,2,1,0:T(8,128)(2,1)S(1)}) custom-call(s32[4]{0:T(128)S(1)} %pad_add_fusion.place, bf16[32,512]{1,0:T(8,128)(2,1)S(1)} %collective-permute-done.15.arrived, bf16[4,32,512]{2,1,0:T(8,128)(2,1)S(1)} %get-tuple-element.22.e, ...), custom_call_target="tpu_custom_call" | custom-call | tf_op jit(solution)/shard_map/turn_dec/pallas_call | solution.py:225
  87.8 1.3 collective-permute-start.16
  90.8 1.3 collective-permute-start.17
  92.1 10.0 %collective-permute-done.17.arrived = bf16[32,512]{1,0:T(8,128)(2,1)S(1)} collective-permute-done((bf16[32,512]{1,0:T(8,128)(2,1)S(1)}, bf16[32,512]{1,0:T(8,128)(2,1)S(1)}, u32[]{:S(2)}, u32[]{:S(2)}) %collective-permute-start.17) | collective-permute-done | bytes 32800 | tf_op jit(solution)/shard_map/ppermute | solution.py:297
  102.1 3.3 %enc_backward.1 = bf16[4,2,4,32,512]{4,3,2,1,0:T(8,128)(2,1)S(1)} custom-call(s32[4]{0:T(128)S(1)} %pad_add_fusion.place, bf16[32,512]{1,0:T(8,128)(2,1)S(1)} %collective-permute-done.17.arrived, f32[4,32,512]{2,1,0:T(8,128)S(1)} %get-tuple-element.24.qe.q, f32[4,32,512]{2,1,0:T(8,128)S(1)} %get-tuple-element.25.ze.z, ...), custom_call_target="tpu_custom_call", output_to_operand_aliasing={{}: (16, {})} | custom-call | tf_op jit(solution)/shard_map/enc_backward/pallas_call | solution.py:225
  105.4 23.0 %all_to_all.15.acts = bf16[16,2,32,512]{3,2,1,0:T(8,128)(2,1)S(1)} all-to-all(bf16[16,2,32,512]{3,2,1,0:T(8,128)(2,1)S(1)} %bitcast.33), channel_id=1, replica_groups=mesh['x_lo'=2,'z_hi'=4,'z_lo'=4,'core'=2,'stage'=2,'y_lo'=2,'x_hi'=2] {'..., dimensions={0} | all-to-all | bytes 2097152 | tf_op jit(solution)/shard_map/all_to_all | solution.py:304
  128.8 20.7 %all_to_all.16 = bf16[16,4,8,512]{3,2,1,0:T(8,128)(2,1)S(1)} all-to-all(bf16[16,4,8,512]{3,2,1,0:T(8,128)(2,1)S(1)} %bitcast.34), channel_id=1, replica_groups=mesh['x_lo'=2,'z_hi'=4,'z_lo'=4,'core'=2,'stage'=2,'y_lo'=2,'x_hi'=2] {'..., dimensions={0} | all-to-all | bytes 1048576 | tf_op jit(solution)/shard_map/all_to_all | solution.py:309
  149.6 26.9 %all_to_all.17 = bf16[4,4,8,512]{3,2,1,0:T(8,128)(2,1)S(1)} all-to-all(bf16[4,4,8,512]{3,2,1,0:T(8,128)(2,1)S(1)} %copy.12), channel_id=1, replica_groups=mesh['x_lo'=2,'z_hi'=4,'z_lo'=4,'core'=2,'stage'=2,'y_lo'=2,'x_hi'=2] {'..., dimensions={0} | all-to-all | bytes 262144 | tf_op jit(solution)/shard_map/all_to_all | solution.py:311
  (54 shorter events, 15.3 us)
Async XLA Ops:
  0.6 1.5 copy-start.1
  2.4 8.8 %copy-start = (bf16[2,1,512,512]{3,2,1,0:T(8,128)(2,1)S(1)}, bf16[2,1,512,512]{3,2,1,0:T(8,128)(2,1)}, u32[]{:S(2)}) copy-start(bf16[2,1,512,512]{3,2,1,0:T(8,128)(2,1)} %refs_0_.5) | copy-start | bytes 3145732
  2.4 8.8 %copy-start.3 = (bf16[4,32,512]{2,1,0:T(8,128)(2,1)S(1)}, bf16[4,32,512]{2,1,0:T(8,128)(2,1)}, u32[]{:S(2)}) copy-start(bf16[4,32,512]{2,1,0:T(8,128)(2,1)} %pixels.1) | copy-start | bytes 393220
  3.5 28.1 %collective-permute-start.4 = (bf16[4,256,512]{2,1,0:T(8,128)(2,1)}, bf16[4,256,512]{2,1,0:T(8,128)(2,1)S(1)}, u32[]{:S(2)}, u32[]{:S(2)}) collective-permute-start(bf16[4,256,512]{2,1,0:T(8,128)(2,1)} %pad_maximum_fusion), channel_id=1, source_target_pairs={{0,2},{2,0},{1,3},{3,1},{4,6},{6,4},{5,7},{7,5},{8,10},{10,8},{9,1... | collective-permute-start | bytes 3145736 | tf_op jit(solution)/shard_map/ppermute | solution.py:254
  6.7 29.9 %collective-permute-start.3 = (bf16[4,256,512]{2,1,0:T(8,128)(2,1)}, bf16[4,256,512]{2,1,0:T(8,128)(2,1)}, u32[]{:S(2)}, u32[]{:S(2)}) collective-permute-start(bf16[4,256,512]{2,1,0:T(8,128)(2,1)} %pad_maximum_fusion), channel_id=1, source_target_pairs={{0,257},{1,256},{256,1},{257,0},{2,259},{3,258},{258,3},{259,2},{4... | collective-permute-start | bytes 3145736 | tf_op jit(solution)/shard_map/ppermute | solution.py:251
  12.4 3.7 %collective-permute-start = (bf16[4,32,512]{2,1,0:T(8,128)(2,1)S(1)}, bf16[4,32,512]{2,1,0:T(8,128)(2,1)S(1)}, u32[]{:S(2)}, u32[]{:S(2)}) collective-permute-start(bf16[4,32,512]{2,1,0:T(8,128)(2,1)S(1)} %own_level.4), channel_id=1, source_target_pairs={{0,1},{8,9},{16,17},{24,25},{32,33},{40,41},{48,49},{56,57},{64,65... | collective-permute-start | bytes 393224 | tf_op jit(solution)/shard_map/ppermute | solution.py:262
  16.7 0.7 collective-permute-start.1
  18.0 0.7 collective-permute-start.2
  31.6 17.0 %copy-start.5 = (bf16[4,256,512]{2,1,0:T(8,128)(2,1)}, bf16[4,256,512]{2,1,0:T(8,128)(2,1)S(1)}, u32[]{:S(2)}) copy-start(bf16[4,256,512]{2,1,0:T(8,128)(2,1)S(1)} %collective-permute-done.4.refs_8_.refs_4_) | copy-start | bytes 3145732
  36.6 14.7 %collective-permute-start.13 = (bf16[2,256,512]{2,1,0:T(8,128)(2,1)S(1)}, bf16[2,256,512]{2,1,0:T(8,128)(2,1)S(1)}, u32[]{:S(2)}, u32[]{:S(2)}) collective-permute-start(bf16[2,256,512]{2,1,0:T(8,128)(2,1)S(1)} %slice.45), channel_id=1, source_target_pairs={{0,257},{1,256},{256,1},{257,0},{2,259},{3,258},{258,3},{259,2},{4... | collective-permute-start | bytes 1572872 | tf_op jit(solution)/shard_map/ppermute | solution.py:251
  42.1 13.9 %collective-permute-start.11 = (bf16[2,256,512]{2,1,0:T(8,128)(2,1)S(1)}, bf16[2,256,512]{2,1,0:T(8,128)(2,1)S(1)}, u32[]{:S(2)}, u32[]{:S(2)}) collective-permute-start(bf16[2,256,512]{2,1,0:T(8,128)(2,1)S(1)} %slice.44), channel_id=1, source_target_pairs={{0,2},{2,0},{1,3},{3,1},{4,6},{6,4},{5,7},{7,5},{8,10},{10,8},{9,1... | collective-permute-start | bytes 1572872 | tf_op jit(solution)/shard_map/ppermute | solution.py:254
  44.2 19.0 %collective-permute-start.9 = (bf16[4,256,512]{2,1,0:T(8,128)(2,1)}, bf16[4,256,512]{2,1,0:T(8,128)(2,1)S(1)}, u32[]{:S(2)}, u32[]{:S(2)}) collective-permute-start(bf16[4,256,512]{2,1,0:T(8,128)(2,1)} %collective-permute-done.3.refs_6_.refs_2_), channel_id=1, source_target_pairs={{0,8},{8,0},{1,9},{9,1},{2,10},{10,2},{3,11},{11,3},{4,12},{12,4},... | collective-permute-start | bytes 3145736 | tf_op jit(solution)/shard_map/ppermute | solution.py:270
  48.6 14.6 %collective-permute-start.10 = (bf16[4,256,512]{2,1,0:T(8,128)(2,1)S(1)}, bf16[4,256,512]{2,1,0:T(8,128)(2,1)S(1)}, u32[]{:S(2)}, u32[]{:S(2)}) collective-permute-start(bf16[4,256,512]{2,1,0:T(8,128)(2,1)S(1)} %collective-permute-done.4.refs_8_.refs_4_), channel_id=1, source_target_pairs={{0,8},{8,0},{1,9},{9,1},{2,10},{10,2},{3,11},{11,3},{4,12},{12,4},... | collective-permute-start | bytes 3145736 | tf_op jit(solution)/shard_map/ppermute | solution.py:270
  51.3 11.8 %collective-permute-start.14 = (bf16[2,256,512]{2,1,0:T(8,128)(2,1)S(1)}, bf16[2,256,512]{2,1,0:T(8,128)(2,1)S(1)}, u32[]{:S(2)}, u32[]{:S(2)}) collective-permute-start(bf16[2,256,512]{2,1,0:T(8,128)(2,1)S(1)} %collective-permute-done.13.refs_12_.refs_8_), channel_id=1, source_target_pairs={{0,8},{8,0},{1,9},{9,1},{2,10},{10,2},{3,11},{11,3},{4,12},{12,4},... | collective-permute-start | bytes 1572872 | tf_op jit(solution)/shard_map/ppermute | solution.py:270
  56.0 7.2 %collective-permute-start.12 = (bf16[2,256,512]{2,1,0:T(8,128)(2,1)S(1)}, bf16[2,256,512]{2,1,0:T(8,128)(2,1)S(1)}, u32[]{:S(2)}, u32[]{:S(2)}) collective-permute-start(bf16[2,256,512]{2,1,0:T(8,128)(2,1)S(1)} %collective-permute-done.11.refs_10_.refs_6_), channel_id=1, source_target_pairs={{0,8},{8,0},{1,9},{9,1},{2,10},{10,2},{3,11},{11,3},{4,12},{12,4},... | collective-permute-start | bytes 1572872 | tf_op jit(solution)/shard_map/ppermute | solution.py:270
  60.3 0.7 collective-permute-start.8
  61.0 0.7 collective-permute-start.7
  61.6 0.7 collective-permute-start.6
  62.3 20.6 %copy-start.4 = (bf16[4,32,512]{2,1,0:T(8,128)(2,1)S(1)}, bf16[4,32,512]{2,1,0:T(8,128)(2,1)}, u32[]{:S(2)}) copy-start(bf16[4,32,512]{2,1,0:T(8,128)(2,1)} %cotangent.1) | copy-start | bytes 393220
  62.3 0.8 collective-permute-start.5
  68.3 14.6 %collective-permute-start.15 = (bf16[32,512]{1,0:T(8,128)(2,1)S(1)}, bf16[32,512]{1,0:T(8,128)(2,1)S(1)}, u32[]{:S(2)}, u32[]{:S(2)}) collective-permute-start(bf16[32,512]{1,0:T(8,128)(2,1)S(1)} %get-tuple-element.21), channel_id=1, source_target_pairs={{6,0},{4,2},{7,1},{5,3},{14,8},{12,10},{15,9},{13,11},{22,16},{20,... | collective-permute-start | bytes 98312 | tf_op jit(solution)/shard_map/ppermute | solution.py:282
  87.8 2.3 %collective-permute-start.16 = (bf16[32,512]{1,0:T(8,128)(2,1)S(1)}, bf16[32,512]{1,0:T(8,128)(2,1)S(1)}, u32[]{:S(2)}, u32[]{:S(2)}) collective-permute-start(bf16[32,512]{1,0:T(8,128)(2,1)S(1)} %get-tuple-element.23), channel_id=1, source_target_pairs={{0,6},{2,4},{1,7},{3,5},{8,14},{10,12},{9,15},{11,13},{16,22},{18,... | collective-permute-start | bytes 98312 | tf_op jit(solution)/shard_map/ppermute | solution.py:289
  90.2 11.9 %copy-start.2 = (bf16[2,1,512,512]{3,2,1,0:T(8,128)(2,1)S(1)}, bf16[2,1,512,512]{3,2,1,0:T(8,128)(2,1)}, u32[]{:S(2)}) copy-start(bf16[2,1,512,512]{3,2,1,0:T(8,128)(2,1)} %refs_1_.5) | copy-start | bytes 3145732
  90.8 11.3 %collective-permute-start.17 = (bf16[32,512]{1,0:T(8,128)(2,1)S(1)}, bf16[32,512]{1,0:T(8,128)(2,1)S(1)}, u32[]{:S(2)}, u32[]{:S(2)}) collective-permute-start(bf16[32,512]{1,0:T(8,128)(2,1)S(1)} %get-tuple-element.31), channel_id=1, source_target_pairs={{6,0},{4,2},{7,1},{5,3},{14,8},{12,10},{15,9},{13,11},{22,16},{20,... | collective-permute-start | bytes 98312 | tf_op jit(solution)/shard_map/ppermute | solution.py:297
  (2 other events, 1.9 us)

commit v2 on v1

v2 whole, which is shorter than its diff:
```python
import functools
import math

import jax
import jax.numpy as jnp
from jax import lax
from jax.experimental import pallas as pl
from jax.experimental.pallas import tpu as pltpu
from jax.sharding import PartitionSpec as P

EPS = 1e-06
LEVELS = 4
ROWS = 32
WIDTH = 512
HALF = WIDTH // 2
BF16 = jnp.bfloat16
F32 = jnp.float32
VMEM_BYTES = 26 * 1024 * 1024


def dot(a, b):
    return jnp.dot(a, b, preferred_element_type=F32)


def dot_t(a, b):
    return lax.dot_general(a, b, (((1,), (1,)), ((), ())), preferred_element_type=F32)


def t_dot(a, b):
    return lax.dot_general(a, b, (((0,), (0,)), ((), ())), preferred_element_type=F32)


def forward_level(v, weight, save, slot):
    save_q, save_z, save_r = save
    r = lax.rsqrt(jnp.mean(v * v, axis=-1, keepdims=True) + EPS)
    q = v * r
    z = dot(q.astype(BF16), weight[0])
    h = (z * jax.nn.sigmoid(z)).astype(BF16)
    save_q[slot] = q
    save_z[slot] = z
    save_r[slot] = jnp.broadcast_to(r, (ROWS, 128))
    return (v + dot(h, weight[1])).astype(BF16)


def backward_level(g, weight, save, slot, acts, first=False):
    save_q, save_z, save_r = save
    gh = dot_t(g, weight[1])
    z = save_z[slot]
    s = jax.nn.sigmoid(z)
    gz = (gh * s * (1.0 + z * (1.0 - s))).astype(BF16)
    q = save_q[slot]
    acts[slot, 0] = q.astype(BF16)
    acts[slot, 1] = gz
    acts[slot, 2] = (z * s).astype(BF16)
    acts[slot, 3] = g
    if first:
        return None
    gn = dot_t(gz, weight[0])
    r = save_r[slot][:, :1]
    return (g.astype(F32) + r * (gn - q * jnp.mean(gn * q, axis=-1, keepdims=True))).astype(BF16)


def own_weights_kernel(place, own_a, own_b, half_e, half_d, held_e, held_d, sems):
    rows = pl.ds(pl.multiple_of(place[2] * HALF, HALF), HALF)
    copies = []
    for side, (half, held) in enumerate(((half_e, held_e), (half_d, held_d))):
        for i, own in enumerate((own_a, own_b)):
            copies.append(pltpu.make_async_copy(own.at[side, 0, rows, :], half.at[i], sems.at[len(copies)]))
            copies.append(pltpu.make_async_copy(own.at[side, 0], held.at[place[1], i], sems.at[len(copies)]))
    for copy in copies:
        copy.start()
    for copy in copies:
        copy.wait()


def start_weights(place, pieces, held, sems, order):
    def start(m, apart):
        for part, core in ((pieces[2 * apart - 2], place[2]), (pieces[2 * apart - 1], 1 - place[2])):
            rows = pl.ds(pl.multiple_of(core * HALF, HALF), HALF)
            pltpu.make_async_copy(part, held.at[m, :, rows, :], sems.at[m]).start()

    for m in order:
        for apart in range(1, LEVELS):
            pl.when(place[1] == (m ^ apart))(functools.partial(start, m, apart))


def wait_weights(place, held, sems, m):
    pl.when(place[1] != m)(pltpu.make_async_copy(held.at[m], held.at[m], sems.at[m]).wait)
    return held.at[m]


N_PIECES = 6


UP = tuple(range(LEVELS))
DOWN = tuple(reversed(UP))


def enc_forward_kernel(place, pixels, *refs):
    pieces, (_, hop, e, q, z, r, held, sems) = refs[:N_PIECES], refs[N_PIECES:]
    start_weights(place, pieces, held, sems, UP)

    @pl.when(place[0] == 0)
    def _():
        x = pixels[place[1]]
        for m in UP:
            x = forward_level(x.astype(F32), wait_weights(place, held, sems, m), (q, z, r), m)
            e[m] = x
        hop[...] = x

    @pl.when(place[0] != 0)
    def _():
        for m in UP:
            wait_weights(place, held, sems, m)


def turn_forward_kernel(place, arrived, weights_e, *refs):
    pieces, (_, hop, qe, ze, re, qd, zd, rd, held, sems) = refs[:N_PIECES], refs[N_PIECES:]
    start_weights(place, pieces, held, sems, DOWN)

    @pl.when(place[0] == 1)
    def _():
        x = arrived[...]
        skips = []
        for m in UP:
            x = forward_level(x.astype(F32), weights_e.at[m], (qe, ze, re), m)
            skips.append(x)
        for m in DOWN:
            v = x.astype(F32) + skips[m].astype(F32)
            x = forward_level(v, wait_weights(place, held, sems, m), (qd, zd, rd), m)
        hop[...] = x

    @pl.when(place[0] != 1)
    def _():
        for m in DOWN:
            wait_weights(place, held, sems, m)


def turn_dec_kernel(
    place, arrived, e, cotangent, weights, hop, skip_grads, acts, q, z, r, local_acts, acts_sem
):
    @pl.when(place[0] == 0)
    def _():
        x = arrived[...]
        for m in DOWN:
            v = x.astype(F32) + e[m].astype(F32)
            x = forward_level(v, weights.at[m], (q, z, r), m)
        g = cotangent[place[1]]
        for m in UP:
            g = backward_level(g, weights.at[m], (q, z, r), m, local_acts)
            skip_grads[m] = g
        hop[...] = g
        out = pltpu.make_async_copy(local_acts, acts.at[:, 1], acts_sem)
        out.start()
        out.wait()


def enc_backward(g, skip_grads, weights, save, acts, first=False):
    for m in DOWN:
        g = (g.astype(F32) + skip_grads[m].astype(F32)).astype(BF16)
        g = backward_level(g, weights.at[m], save, m, acts, first and m == 0)
    return g


def turn_backward_kernel(
    place, arrived, qe, ze, re, qd, zd, rd, weights_e, weights_d, acts_in, hop, acts, acts_e, acts_d, acts_sems
):
    del acts_in

    @pl.when(place[0] == 1)
    def _():
        g = arrived[...]
        skip_grads = []
        for m in UP:
            g = backward_level(g, weights_d.at[m], (qd, zd, rd), m, acts_d)
            skip_grads.append(g)
        out_d = pltpu.make_async_copy(acts_d, acts.at[:, 1], acts_sems.at[1])
        out_d.start()
        hop[...] = enc_backward(g, skip_grads, weights_e, (qe, ze, re), acts_e)
        out_e = pltpu.make_async_copy(acts_e, acts.at[:, 0], acts_sems.at[0])
        out_e.start()
        out_d.wait()
        out_e.wait()


def enc_backward_kernel(place, arrived, q, z, r, skip_grads, weights, acts_in, acts, local_acts, acts_sem):
    del acts_in

    @pl.when(place[0] == 0)
    def _():
        enc_backward(arrived[...], skip_grads, weights, (q, z, r), local_acts, first=True)
        out = pltpu.make_async_copy(local_acts, acts.at[:, 0], acts_sem)
        out.start()
        out.wait()


def grads_kernel(acts, out):
    rows = acts.shape[0] * ROWS
    grad = t_dot(acts[:, 0].reshape(rows, WIDTH), acts[:, 1].reshape(rows, WIDTH))
    for z_low in range(4):
        for z_high in range(4):
            for x in range(2):
                for core in range(2):
                    first = x * 256 + (z_high * 4 + z_low) * 16 + core * 8
                    out[z_low, x, core, z_high] = grad[first : first + 8].astype(BF16)


SMEM = pl.BlockSpec(memory_space=pltpu.SMEM)
VMEM = pl.BlockSpec(memory_space=pltpu.VMEM)
ANY = pl.BlockSpec(memory_space=pl.ANY)
PARAMS = pltpu.CompilerParams(vmem_limit_bytes=VMEM_BYTES)

ROW = jax.ShapeDtypeStruct((ROWS, WIDTH), BF16)
STACK = jax.ShapeDtypeStruct((LEVELS, ROWS, WIDTH), BF16)
SAVE = jax.ShapeDtypeStruct((LEVELS, ROWS, WIDTH), F32)
SAVE_R = jax.ShapeDtypeStruct((LEVELS, ROWS, 128), F32)
SAVES = (SAVE, SAVE, SAVE_R)
ACTS = jax.ShapeDtypeStruct((LEVELS, 2, 4, ROWS, WIDTH), BF16)

WEIGHTS = jax.ShapeDtypeStruct((LEVELS, 2, WIDTH, WIDTH), BF16)

SEMS = pltpu.SemaphoreType.DMA((LEVELS,))
LOCAL_ACTS = pltpu.VMEM((LEVELS, 4, ROWS, WIDTH), BF16)
SCRATCH_SAVES = tuple(pltpu.VMEM(s.shape, s.dtype) for s in SAVES)


def call(kernel, operands, spaces, outs, out_spaces, scratch=(), aliases=None, name=None):
    return pl.pallas_call(
        kernel,
        out_shape=outs,
        in_specs=spaces,
        out_specs=out_spaces,
        scratch_shapes=scratch,
        input_output_aliases=aliases or {},
        compiler_params=PARAMS,
        name=name,
    )(*operands)


def local(pixels, cotangent, weights_a, weights_b):
    core = lax.axis_index("core")
    level = lax.axis_index(PIPE)
    place = jnp.stack([level // LEVELS, level % LEVELS, core, level]).astype(jnp.int32)

    piece = jax.ShapeDtypeStruct((2, HALF, WIDTH), BF16)
    half_e, half_d, own_e, own_d = call(
        own_weights_kernel, (place, weights_a, weights_b), (SMEM, ANY, ANY), (piece, piece, WEIGHTS, WEIGHTS),
        (VMEM,) * 4, (pltpu.SemaphoreType.DMA((8,)),), name="own_weights",
    )

    def along_x(block):
        return lax.ppermute(block, ("x_lo", "x_hi"), [(i, 3 - i) for i in range(4)])

    def along_y(block):
        return lax.ppermute(block, "y_lo", [(0, 1), (1, 0)])

    def swap(block):
        return lax.ppermute(block, "core", [(0, 1), (1, 0)])

    x_e, y_d = along_x(half_e), along_y(half_d)
    x_d, y_e = along_x(half_d), along_y(half_e)
    diagonal_e, diagonal_d = along_y(x_e), along_x(y_d)

    pieces = []
    for piece in (x_e, y_e, diagonal_e, x_d, y_d):
        pieces += [piece, swap(piece)]
    *pieces, diagonal_d = lax.optimization_barrier((*pieces, diagonal_d))

    up = [(0, 3), (1, 2)]
    down = [(3, 0), (2, 1)]
    y = ("stage", "y_lo")

    hop, e, *saves_0, weights_e = call(
        enc_forward_kernel, (place, pixels, *pieces[:6], own_e), (SMEM, VMEM) + (ANY,) * N_PIECES + (VMEM,),
        (ROW, STACK) + SAVES + (WEIGHTS,), (VMEM,) * 6, (SEMS,), {2 + N_PIECES: 5}, name="enc_forward",
    )
    hop, diagonal_d = lax.optimization_barrier((hop, diagonal_d))
    arrived = lax.ppermute(hop, y, up)
    pieces = (*pieces[6:], diagonal_d, swap(diagonal_d))
    hop, *saves, weights_d = call(
        turn_forward_kernel, (place, arrived, weights_e, *pieces, own_d),
        (SMEM, VMEM, VMEM) + (ANY,) * N_PIECES + (VMEM,),
        (ROW,) + SAVES + SAVES + (WEIGHTS,), (VMEM,) * 8, (SEMS,), {3 + N_PIECES: 7}, name="turn_forward",
    )
    arrived = lax.ppermute(hop, y, down)
    hop, skip_grads, acts = call(
        turn_dec_kernel, (place, arrived, e, cotangent, weights_d), (SMEM,) + (VMEM,) * 4,
        (ROW, STACK, ACTS), (VMEM, VMEM, ANY),
        SCRATCH_SAVES + (LOCAL_ACTS, pltpu.SemaphoreType.DMA), name="turn_dec",
    )
    arrived = lax.ppermute(hop, y, up)
    hop, acts = call(
        turn_backward_kernel, (place, arrived, *saves, weights_e, weights_d, acts), (SMEM,) + (VMEM,) * 9 + (ANY,),
        (ROW, ACTS), (VMEM, ANY),
        (LOCAL_ACTS, LOCAL_ACTS, pltpu.SemaphoreType.DMA((2,))), {10: 1}, name="turn_backward",
    )
    arrived = lax.ppermute(hop, y, down)
    acts = call(
        enc_backward_kernel, (place, arrived, *saves_0, skip_grads, weights_e, acts), (SMEM,) + (VMEM,) * 6 + (ANY,),
        ACTS, ANY, (LOCAL_ACTS, pltpu.SemaphoreType.DMA), {7: 0}, name="enc_backward",
    )

    acts = lax.all_to_all(acts.reshape(16, 2, ROWS, WIDTH), MEMBERS + ("x_lo", "core"), 0, 0)
    grad = call(
        grads_kernel, (acts,), (VMEM,), jax.ShapeDtypeStruct((4, 2, 2, 4, 8, WIDTH), BF16), VMEM, name="grads"
    )

    total = lax.all_to_all(grad.reshape(16, 4, 8, WIDTH), ("z_lo", "x_lo", "core"), 0, 0)
    total = jnp.sum(total.astype(F32).reshape(4, 4, 4, 8, WIDTH), axis=0).astype(BF16)
    total = lax.all_to_all(total.transpose(1, 0, 2, 3), "z_hi", 0, 0)
    factor = 1.0 / math.sqrt(LEVELS * ROWS * 64)
    total = jnp.sum(total.astype(F32), axis=0).reshape(2, 2, 1, 8, WIDTH) * factor
    return total[:, 0], total[:, 1]


MEMBERS = ("y_lo", "x_hi")
DP = ("x_lo", "z_hi", "z_lo", "core")
PIPE = ("stage", "y_lo", "x_hi")


def solution(mesh):
    fine = jax.sharding.Mesh(mesh.devices.reshape(2, 4, 4, 2, 2, 2, 2), DP + PIPE)
    return jax.shard_map(
        local,
        mesh=fine,
        in_specs=(
            P(None, DP, None),
            P(None, DP, None),
            P(None, PIPE, None, None),
            P(None, PIPE, None, None),
        ),
        out_specs=(P(None, PIPE, DP, None), P(None, PIPE, DP, None)),
        check_vma=False,
    )
```

time: 178 us -> 159 us (0.89)
  waiting for transfers between devices: 44.5 us -> 22.3 us
  starting transfers between devices: 39 us -> 48 us
  Pallas kernels: 15.5 us -> 11.7 us
    ppermute x2 -> x3, waiting for transfers between devices: 12.4 us -> 2.89 us  [along_y(): return lax.ppermute(block, 'y_lo', [(0, 1), (1, 0)])]
    ppermute x2, waiting for transfers between devices: 23.3 us -> 15.9 us  [local(): arrived = lax.ppermute(hop, y, down)]
    ppermute x2 -> x3, waiting for transfers between devices: 5.82 us -> 0.1 us  [along_x(): return lax.ppermute(block, ('x_lo', 'x_hi'), [(i, 3 - i) for i in range(4)])]
    pallas_call x9 -> x7, Pallas kernels: 15.5 us -> 11.7 us  [call(): pl.pallas_call(kernel, out_shape=outs, in_specs=spaces, out_specs=out_spa...]
    ppermute x2 -> x3, starting transfers between devices: 5.27 us -> 8.49 us  [along_y(): return lax.ppermute(block, 'y_lo', [(0, 1), (1, 0)])]
    ppermute x1 -> x2, starting transfers between devices: 1.29 us -> 4.23 us  [local(): arrived = lax.ppermute(hop, y, up)]
    slice x4 -> x0, local copies, waits for them, and re-layouts: 2.54 us -> none  [the longest x2 1.43 us: local(): w[side, 0]]
    ppermute x2 -> x3, starting transfers between devices: 8.77 us -> 10.9 us  [along_x(): return lax.ppermute(block, ('x_lo', 'x_hi'), [(i, 3 - i) for i in range(4)])]
  transfers between devices with their start and end apart: 18 -> 16, of which waited for: 7 -> 7; matrix products, arithmetic and copies ran while one was open for 1% -> 0% of each run, Pallas kernels for 2% -> 0%
where the time goes in v2:
time: 159 us; the launch traced here: 158 us
  blocking collectives  70.7 us (44%)
  starting transfers between devices  48 us (30%)
  waiting for transfers between devices  22.3 us (14%)
  Pallas kernels  11.7 us (7%)
  local copies, waits for them, and re-layouts  4 us (3%)
    all_to_all x1, blocking collectives, local(): total = lax.all_to_all(total.transpose(1, 0, 2, 3), 'z_hi', 0, 0)  26.9 us
    all_to_all x1, blocking collectives, local(): lax.all_to_all(acts.reshape(16, 2, ROWS, WIDTH), MEMBERS + ('x_lo', 'core...  23.1 us
    ppermute x6, starting transfers between devices, swap(): return lax.ppermute(block, 'core', [(0, 1), (1, 0)])  21.9 us
    all_to_all x1, blocking collectives, local(): lax.all_to_all(grad.reshape(16, 4, 8, WIDTH), ('z_lo', 'x_lo', 'core'), 0...  20.7 us
    ppermute x2, waiting for transfers between devices, local(): arrived = lax.ppermute(hop, y, down)  15.9 us
    pallas_call x7, Pallas kernels, call(): pl.pallas_call(kernel, out_shape=outs, in_specs=spaces, out_specs=out_spa...  11.7 us
    ppermute x3, starting transfers between devices, along_x(): return lax.ppermute(block, ('x_lo', 'x_hi'), [(i, 3 - i) for i in range(4)])  10.9 us
    ppermute x3, starting transfers between devices, along_y(): return lax.ppermute(block, 'y_lo', [(0, 1), (1, 0)])  8.49 us
  transfers between devices with their start and end apart: 16, of which 7 were waited for; matrix products, arithmetic and copies ran while one was open for 0% of the time, Pallas kernels for 0%

profile of v2, /device:TPU:33, one launch (start us, length us, event | category | flops | bytes accessed | tf_op | source)
XLA Modules:
  0.0 157.8 jit_solution(81038437218427204)
XLA Ops:
  4.0 3.2 %collective-permute-start.2 = (bf16[2,256,512]{2,1,0:T(8,128)(2,1)S(1)}, bf16[2,256,512]{2,1,0:T(8,128)(2,1)S(1)}, u32[]{:S(2)}, u32[]{:S(2)}) collective-permute-start(bf16[2,256,512]{2,1,0:T(8,128)(2,1)S(1)} %get-tuple-element.38), channel_id=1, source_target_pairs={{0,2},{2,0},{1,3},{3,1},{4,6},{6,4},{5,7},{7,5},{8,10},{10,8},{9,1... | collective-permute-start | bytes 1572872 | tf_op jit(solution)/shard_map/ppermute | solution.py:255
  7.3 4.4 %collective-permute-start = (bf16[2,256,512]{2,1,0:T(8,128)(2,1)S(1)}, bf16[2,256,512]{2,1,0:T(8,128)(2,1)S(1)}, u32[]{:S(2)}, u32[]{:S(2)}) collective-permute-start(bf16[2,256,512]{2,1,0:T(8,128)(2,1)S(1)} %get-tuple-element.38), channel_id=1, source_target_pairs={{0,257},{1,256},{256,1},{257,0},{2,259},{3,258},{258,3},{259,2},{4... | collective-permute-start | bytes 1572872 | tf_op jit(solution)/shard_map/ppermute | solution.py:252
  11.6 2.1 %collective-permute-start.8 = (bf16[2,256,512]{2,1,0:T(8,128)(2,1)S(1)}, bf16[2,256,512]{2,1,0:T(8,128)(2,1)S(1)}, u32[]{:S(2)}, u32[]{:S(2)}) collective-permute-start(bf16[2,256,512]{2,1,0:T(8,128)(2,1)S(1)} %get-tuple-element.39), channel_id=1, source_target_pairs={{0,2},{2,0},{1,3},{3,1},{4,6},{6,4},{5,7},{7,5},{8,10},{10,8},{9,1... | collective-permute-start | bytes 1572872 | tf_op jit(solution)/shard_map/ppermute | solution.py:255
  13.7 2.1 %collective-permute-start.6 = (bf16[2,256,512]{2,1,0:T(8,128)(2,1)S(1)}, bf16[2,256,512]{2,1,0:T(8,128)(2,1)S(1)}, u32[]{:S(2)}, u32[]{:S(2)}) collective-permute-start(bf16[2,256,512]{2,1,0:T(8,128)(2,1)S(1)} %get-tuple-element.39), channel_id=1, source_target_pairs={{0,257},{1,256},{256,1},{257,0},{2,259},{3,258},{258,3},{259,2},{4... | collective-permute-start | bytes 1572872 | tf_op jit(solution)/shard_map/ppermute | solution.py:252
  15.8 2.9 %collective-permute-done.2.refs_2_ = bf16[2,256,512]{2,1,0:T(8,128)(2,1)S(1)} collective-permute-done((bf16[2,256,512]{2,1,0:T(8,128)(2,1)S(1)}, bf16[2,256,512]{2,1,0:T(8,128)(2,1)S(1)}, u32[]{:S(2)}, u32[]{:S(2)}) %collective-permute-start.2) | collective-permute-done | bytes 524320 | tf_op jit(solution)/shard_map/ppermute | solution.py:255
  18.7 4.6 %collective-permute-start.3 = (bf16[2,256,512]{2,1,0:T(8,128)(2,1)S(1)}, bf16[2,256,512]{2,1,0:T(8,128)(2,1)S(1)}, u32[]{:S(2)}, u32[]{:S(2)}) collective-permute-start(bf16[2,256,512]{2,1,0:T(8,128)(2,1)S(1)} %collective-permute-done.2.refs_2_), channel_id=1, source_target_pairs={{0,8},{8,0},{1,9},{9,1},{2,10},{10,2},{3,11},{11,3},{4,12},{12,4},... | collective-permute-start | bytes 1572872 | tf_op jit(solution)/shard_map/ppermute | solution.py:258
  23.3 3.2 %collective-permute-start.4 = (bf16[2,256,512]{2,1,0:T(8,128)(2,1)S(1)}, bf16[2,256,512]{2,1,0:T(8,128)(2,1)S(1)}, u32[]{:S(2)}, u32[]{:S(2)}) collective-permute-start(bf16[2,256,512]{2,1,0:T(8,128)(2,1)S(1)} %collective-permute-done.refs_0_), channel_id=1, source_target_pairs={{0,2},{2,0},{1,3},{3,1},{4,6},{6,4},{5,7},{7,5},{8,10},{10,8},{9,1... | collective-permute-start | bytes 1572872 | tf_op jit(solution)/shard_map/ppermute | solution.py:255
  26.5 3.9 %collective-permute-start.1 = (bf16[2,256,512]{2,1,0:T(8,128)(2,1)S(1)}, bf16[2,256,512]{2,1,0:T(8,128)(2,1)S(1)}, u32[]{:S(2)}, u32[]{:S(2)}) collective-permute-start(bf16[2,256,512]{2,1,0:T(8,128)(2,1)S(1)} %collective-permute-done.refs_0_), channel_id=1, source_target_pairs={{0,8},{8,0},{1,9},{9,1},{2,10},{10,2},{3,11},{11,3},{4,12},{12,4},... | collective-permute-start | bytes 1572872 | tf_op jit(solution)/shard_map/ppermute | solution.py:258
  30.4 4.4 %collective-permute-start.10 = (bf16[2,256,512]{2,1,0:T(8,128)(2,1)S(1)}, bf16[2,256,512]{2,1,0:T(8,128)(2,1)S(1)}, u32[]{:S(2)}, u32[]{:S(2)}) collective-permute-start(bf16[2,256,512]{2,1,0:T(8,128)(2,1)S(1)} %collective-permute-done.8.refs_2_), channel_id=1, source_target_pairs={{0,257},{1,256},{256,1},{257,0},{2,259},{3,258},{258,3},{259,2},{4... | collective-permute-start | bytes 1572872 | tf_op jit(solution)/shard_map/ppermute | solution.py:252
  34.8 4.4 %collective-permute-start.9 = (bf16[2,256,512]{2,1,0:T(8,128)(2,1)S(1)}, bf16[2,256,512]{2,1,0:T(8,128)(2,1)S(1)}, u32[]{:S(2)}, u32[]{:S(2)}) collective-permute-start(bf16[2,256,512]{2,1,0:T(8,128)(2,1)S(1)} %collective-permute-done.8.refs_2_), channel_id=1, source_target_pairs={{0,8},{8,0},{1,9},{9,1},{2,10},{10,2},{3,11},{11,3},{4,12},{12,4},... | collective-permute-start | bytes 1572872 | tf_op jit(solution)/shard_map/ppermute | solution.py:258
  39.3 1.9 %collective-permute-start.7 = (bf16[2,256,512]{2,1,0:T(8,128)(2,1)S(1)}, bf16[2,256,512]{2,1,0:T(8,128)(2,1)S(1)}, u32[]{:S(2)}, u32[]{:S(2)}) collective-permute-start(bf16[2,256,512]{2,1,0:T(8,128)(2,1)S(1)} %collective-permute-done.6.refs_0_), channel_id=1, source_target_pairs={{0,8},{8,0},{1,9},{9,1},{2,10},{10,2},{3,11},{11,3},{4,12},{12,4},... | collective-permute-start | bytes 1572872 | tf_op jit(solution)/shard_map/ppermute | solution.py:258
  41.2 3.4 %collective-permute-start.5 = (bf16[2,256,512]{2,1,0:T(8,128)(2,1)S(1)}, bf16[2,256,512]{2,1,0:T(8,128)(2,1)S(1)}, u32[]{:S(2)}, u32[]{:S(2)}) collective-permute-start(bf16[2,256,512]{2,1,0:T(8,128)(2,1)S(1)} %collective-permute-done.4.refs_4_), channel_id=1, source_target_pairs={{0,8},{8,0},{1,9},{9,1},{2,10},{10,2},{3,11},{11,3},{4,12},{12,4},... | collective-permute-start | bytes 1572872 | tf_op jit(solution)/shard_map/ppermute | solution.py:258
  44.8 1.4 collective-permute-done.5.refs_5_
  47.1 2.6 %enc_forward.1 = (bf16[32,512]{1,0:T(8,128)(2,1)S(1)}, bf16[4,32,512]{2,1,0:T(8,128)(2,1)S(1)}, f32[4,32,512]{2,1,0:T(8,128)S(1)}, f32[4,32,512]{2,1,0:T(8,128)S...) custom-call(s32[4]{0:T(128)S(1)} %pad_add_fusion.place, ...), custom_call_target="tpu_custom_call", output_to_operand_aliasing={{5}: (8, {})} | custom-call | tf_op jit(solution)/shard_map/enc_forward/pallas_call | solution.py:228
  49.7 3.6 %collective-permute-start.12 = (bf16[2,256,512]{2,1,0:T(8,128)(2,1)S(1)}, bf16[2,256,512]{2,1,0:T(8,128)(2,1)S(1)}, u32[]{:S(2)}, u32[]{:S(2)}) collective-permute-start(bf16[2,256,512]{2,1,0:T(8,128)(2,1)S(1)} %collective-permute-done.10.refs_4_), channel_id=1, source_target_pairs={{0,8},{8,0},{1,9},{9,1},{2,10},{10,2},{3,11},{11,3},{4,12},{12,4},... | collective-permute-start | bytes 1572872 | tf_op jit(solution)/shard_map/ppermute | solution.py:258
  53.4 2.9 %collective-permute-start.11 = (bf16[32,512]{1,0:T(8,128)(2,1)S(1)}, bf16[32,512]{1,0:T(8,128)(2,1)S(1)}, u32[]{:S(2)}, u32[]{:S(2)}) collective-permute-start(bf16[32,512]{1,0:T(8,128)(2,1)S(1)} %get-tuple-element.49), channel_id=1, source_target_pairs={{0,6},{2,4},{1,7},{3,5},{8,14},{10,12},{9,15},{11,13},{16,22},{18,... | collective-permute-start | bytes 98312 | tf_op jit(solution)/shard_map/ppermute | solution.py:278
  58.3 1.3 collective-permute-start.13
  59.6 7.6 %collective-permute-done.13.arrived = bf16[32,512]{1,0:T(8,128)(2,1)S(1)} collective-permute-done((bf16[32,512]{1,0:T(8,128)(2,1)S(1)}, bf16[32,512]{1,0:T(8,128)(2,1)S(1)}, u32[]{:S(2)}, u32[]{:S(2)}) %collective-permute-start.13) | collective-permute-done | bytes 32800 | tf_op jit(solution)/shard_map/ppermute | solution.py:285
  67.2 4.0 %turn_dec.1 = (bf16[32,512]{1,0:T(8,128)(2,1)S(1)}, bf16[4,32,512]{2,1,0:T(8,128)(2,1)S(1)}, bf16[4,2,4,32,512]{4,3,2,1,0:T(8,128)(2,1)S(1)}) custom-call(s32[4]{0:T(128)S(1)} %pad_add_fusion.place, bf16[32,512]{1,0:T(8,128)(2,1)S(1)} %collective-permute-done.13.arrived, bf16[4,32,512]{2,1,0:T(8,128)(2,1)S(1)} %get-tuple-element.58.e, ...), custom_call_target="tpu_custom_call" | custom-call | tf_op jit(solution)/shard_map/turn_dec/pallas_call | solution.py:228
  75.3 8.2 %collective-permute-done.15.arrived = bf16[32,512]{1,0:T(8,128)(2,1)S(1)} collective-permute-done((bf16[32,512]{1,0:T(8,128)(2,1)S(1)}, bf16[32,512]{1,0:T(8,128)(2,1)S(1)}, u32[]{:S(2)}, u32[]{:S(2)}) %collective-permute-start.15) | collective-permute-done | bytes 32800 | tf_op jit(solution)/shard_map/ppermute | solution.py:297
  83.6 2.3 %enc_backward.1 = bf16[4,2,4,32,512]{4,3,2,1,0:T(8,128)(2,1)S(1)} custom-call(s32[4]{0:T(128)S(1)} %pad_add_fusion.place, bf16[32,512]{1,0:T(8,128)(2,1)S(1)} %collective-permute-done.15.arrived, f32[4,32,512]{2,1,0:T(8,128)S(1)} %get-tuple-element.69.q, f32[4,32,512]{2,1,0:T(8,128)S(1)} %get-tuple-element.70.z, ...), custom_call_target="tpu_custom_call", output_to_operand_aliasing={{}: (7, {})} | custom-call | tf_op jit(solution)/shard_map/enc_backward/pallas_call | solution.py:228
  85.9 23.1 %all_to_all.15.acts = bf16[16,2,32,512]{3,2,1,0:T(8,128)(2,1)S(1)} all-to-all(bf16[16,2,32,512]{3,2,1,0:T(8,128)(2,1)S(1)} %bitcast.17), channel_id=1, replica_groups=mesh['x_lo'=2,'z_hi'=4,'z_lo'=4,'core'=2,'stage'=2,'y_lo'=2,'x_hi'=2] {'..., dimensions={0} | all-to-all | bytes 2097152 | tf_op jit(solution)/shard_map/all_to_all | solution.py:303
  109.5 20.7 %all_to_all.16 = bf16[16,4,8,512]{3,2,1,0:T(8,128)(2,1)S(1)} all-to-all(bf16[16,4,8,512]{3,2,1,0:T(8,128)(2,1)S(1)} %bitcast.18), channel_id=1, replica_groups=mesh['x_lo'=2,'z_hi'=4,'z_lo'=4,'core'=2,'stage'=2,'y_lo'=2,'x_hi'=2] {'..., dimensions={0} | all-to-all | bytes 1048576 | tf_op jit(solution)/shard_map/all_to_all | solution.py:308
  130.2 26.9 %all_to_all.17 = bf16[4,4,8,512]{3,2,1,0:T(8,128)(2,1)S(1)} all-to-all(bf16[4,4,8,512]{3,2,1,0:T(8,128)(2,1)S(1)} %copy.14), channel_id=1, replica_groups=mesh['x_lo'=2,'z_hi'=4,'z_lo'=4,'core'=2,'stage'=2,'y_lo'=2,'x_hi'=2] {'..., dimensions={0} | all-to-all | bytes 262144 | tf_op jit(solution)/shard_map/all_to_all | solution.py:310
  (32 shorter events, 11.7 us)
Async XLA Ops:
  0.7 1.2 copy-start
  2.0 1.2 copy-start.1
  4.0 14.7 %collective-permute-start.2 = (bf16[2,256,512]{2,1,0:T(8,128)(2,1)S(1)}, bf16[2,256,512]{2,1,0:T(8,128)(2,1)S(1)}, u32[]{:S(2)}, u32[]{:S(2)}) collective-permute-start(bf16[2,256,512]{2,1,0:T(8,128)(2,1)S(1)} %get-tuple-element.38), channel_id=1, source_target_pairs={{0,2},{2,0},{1,3},{3,1},{4,6},{6,4},{5,7},{7,5},{8,10},{10,8},{9,1... | collective-permute-start | bytes 1572872 | tf_op jit(solution)/shard_map/ppermute | solution.py:255
  7.3 16.1 %collective-permute-start = (bf16[2,256,512]{2,1,0:T(8,128)(2,1)S(1)}, bf16[2,256,512]{2,1,0:T(8,128)(2,1)S(1)}, u32[]{:S(2)}, u32[]{:S(2)}) collective-permute-start(bf16[2,256,512]{2,1,0:T(8,128)(2,1)S(1)} %get-tuple-element.38), channel_id=1, source_target_pairs={{0,257},{1,256},{256,1},{257,0},{2,259},{3,258},{258,3},{259,2},{4... | collective-permute-start | bytes 1572872 | tf_op jit(solution)/shard_map/ppermute | solution.py:252
  11.6 18.8 %collective-permute-start.8 = (bf16[2,256,512]{2,1,0:T(8,128)(2,1)S(1)}, bf16[2,256,512]{2,1,0:T(8,128)(2,1)S(1)}, u32[]{:S(2)}, u32[]{:S(2)}) collective-permute-start(bf16[2,256,512]{2,1,0:T(8,128)(2,1)S(1)} %get-tuple-element.39), channel_id=1, source_target_pairs={{0,2},{2,0},{1,3},{3,1},{4,6},{6,4},{5,7},{7,5},{8,10},{10,8},{9,1... | collective-permute-start | bytes 1572872 | tf_op jit(solution)/shard_map/ppermute | solution.py:255
  13.7 21.1 %collective-permute-start.6 = (bf16[2,256,512]{2,1,0:T(8,128)(2,1)S(1)}, bf16[2,256,512]{2,1,0:T(8,128)(2,1)S(1)}, u32[]{:S(2)}, u32[]{:S(2)}) collective-permute-start(bf16[2,256,512]{2,1,0:T(8,128)(2,1)S(1)} %get-tuple-element.39), channel_id=1, source_target_pairs={{0,257},{1,256},{256,1},{257,0},{2,259},{3,258},{258,3},{259,2},{4... | collective-permute-start | bytes 1572872 | tf_op jit(solution)/shard_map/ppermute | solution.py:252
  18.7 20.5 %collective-permute-start.3 = (bf16[2,256,512]{2,1,0:T(8,128)(2,1)S(1)}, bf16[2,256,512]{2,1,0:T(8,128)(2,1)S(1)}, u32[]{:S(2)}, u32[]{:S(2)}) collective-permute-start(bf16[2,256,512]{2,1,0:T(8,128)(2,1)S(1)} %collective-permute-done.2.refs_2_), channel_id=1, source_target_pairs={{0,8},{8,0},{1,9},{9,1},{2,10},{10,2},{3,11},{11,3},{4,12},{12,4},... | collective-permute-start | bytes 1572872 | tf_op jit(solution)/shard_map/ppermute | solution.py:258
  23.3 17.9 %collective-permute-start.4 = (bf16[2,256,512]{2,1,0:T(8,128)(2,1)S(1)}, bf16[2,256,512]{2,1,0:T(8,128)(2,1)S(1)}, u32[]{:S(2)}, u32[]{:S(2)}) collective-permute-start(bf16[2,256,512]{2,1,0:T(8,128)(2,1)S(1)} %collective-permute-done.refs_0_), channel_id=1, source_target_pairs={{0,2},{2,0},{1,3},{3,1},{4,6},{6,4},{5,7},{7,5},{8,10},{10,8},{9,1... | collective-permute-start | bytes 1572872 | tf_op jit(solution)/shard_map/ppermute | solution.py:255
  26.5 18.1 %collective-permute-start.1 = (bf16[2,256,512]{2,1,0:T(8,128)(2,1)S(1)}, bf16[2,256,512]{2,1,0:T(8,128)(2,1)S(1)}, u32[]{:S(2)}, u32[]{:S(2)}) collective-permute-start(bf16[2,256,512]{2,1,0:T(8,128)(2,1)S(1)} %collective-permute-done.refs_0_), channel_id=1, source_target_pairs={{0,8},{8,0},{1,9},{9,1},{2,10},{10,2},{3,11},{11,3},{4,12},{12,4},... | collective-permute-start | bytes 1572872 | tf_op jit(solution)/shard_map/ppermute | solution.py:258
  30.4 14.3 %collective-permute-start.10 = (bf16[2,256,512]{2,1,0:T(8,128)(2,1)S(1)}, bf16[2,256,512]{2,1,0:T(8,128)(2,1)S(1)}, u32[]{:S(2)}, u32[]{:S(2)}) collective-permute-start(bf16[2,256,512]{2,1,0:T(8,128)(2,1)S(1)} %collective-permute-done.8.refs_2_), channel_id=1, source_target_pairs={{0,257},{1,256},{256,1},{257,0},{2,259},{3,258},{258,3},{259,2},{4... | collective-permute-start | bytes 1572872 | tf_op jit(solution)/shard_map/ppermute | solution.py:252
  34.8 9.9 %collective-permute-start.9 = (bf16[2,256,512]{2,1,0:T(8,128)(2,1)S(1)}, bf16[2,256,512]{2,1,0:T(8,128)(2,1)S(1)}, u32[]{:S(2)}, u32[]{:S(2)}) collective-permute-start(bf16[2,256,512]{2,1,0:T(8,128)(2,1)S(1)} %collective-permute-done.8.refs_2_), channel_id=1, source_target_pairs={{0,8},{8,0},{1,9},{9,1},{2,10},{10,2},{3,11},{11,3},{4,12},{12,4},... | collective-permute-start | bytes 1572872 | tf_op jit(solution)/shard_map/ppermute | solution.py:258
  39.3 5.5 %collective-permute-start.7 = (bf16[2,256,512]{2,1,0:T(8,128)(2,1)S(1)}, bf16[2,256,512]{2,1,0:T(8,128)(2,1)S(1)}, u32[]{:S(2)}, u32[]{:S(2)}) collective-permute-start(bf16[2,256,512]{2,1,0:T(8,128)(2,1)S(1)} %collective-permute-done.6.refs_0_), channel_id=1, source_target_pairs={{0,8},{8,0},{1,9},{9,1},{2,10},{10,2},{3,11},{11,3},{4,12},{12,4},... | collective-permute-start | bytes 1572872 | tf_op jit(solution)/shard_map/ppermute | solution.py:258
  41.2 5.0 %collective-permute-start.5 = (bf16[2,256,512]{2,1,0:T(8,128)(2,1)S(1)}, bf16[2,256,512]{2,1,0:T(8,128)(2,1)S(1)}, u32[]{:S(2)}, u32[]{:S(2)}) collective-permute-start(bf16[2,256,512]{2,1,0:T(8,128)(2,1)S(1)} %collective-permute-done.4.refs_4_), channel_id=1, source_target_pairs={{0,8},{8,0},{1,9},{9,1},{2,10},{10,2},{3,11},{11,3},{4,12},{12,4},... | collective-permute-start | bytes 1572872 | tf_op jit(solution)/shard_map/ppermute | solution.py:258
  46.2 0.9 copy-start.2
  49.7 7.6 %collective-permute-start.12 = (bf16[2,256,512]{2,1,0:T(8,128)(2,1)S(1)}, bf16[2,256,512]{2,1,0:T(8,128)(2,1)S(1)}, u32[]{:S(2)}, u32[]{:S(2)}) collective-permute-start(bf16[2,256,512]{2,1,0:T(8,128)(2,1)S(1)} %collective-permute-done.10.refs_4_), channel_id=1, source_target_pairs={{0,8},{8,0},{1,9},{9,1},{2,10},{10,2},{3,11},{11,3},{4,12},{12,4},... | collective-permute-start | bytes 1572872 | tf_op jit(solution)/shard_map/ppermute | solution.py:258
  53.4 3.9 %collective-permute-start.11 = (bf16[32,512]{1,0:T(8,128)(2,1)S(1)}, bf16[32,512]{1,0:T(8,128)(2,1)S(1)}, u32[]{:S(2)}, u32[]{:S(2)}) collective-permute-start(bf16[32,512]{1,0:T(8,128)(2,1)S(1)} %get-tuple-element.49), channel_id=1, source_target_pairs={{0,6},{2,4},{1,7},{3,5},{8,14},{10,12},{9,15},{11,13},{16,22},{18,... | collective-permute-start | bytes 98312 | tf_op jit(solution)/shard_map/ppermute | solution.py:278
  57.3 9.9 %copy-start.3 = (bf16[4,32,512]{2,1,0:T(8,128)(2,1)S(1)}, bf16[4,32,512]{2,1,0:T(8,128)(2,1)}, u32[]{:S(2)}) copy-start(bf16[4,32,512]{2,1,0:T(8,128)(2,1)} %cotangent.1) | copy-start | bytes 393220
  58.3 8.9 %collective-permute-start.13 = (bf16[32,512]{1,0:T(8,128)(2,1)S(1)}, bf16[32,512]{1,0:T(8,128)(2,1)S(1)}, u32[]{:S(2)}, u32[]{:S(2)}) collective-permute-start(bf16[32,512]{1,0:T(8,128)(2,1)S(1)} %get-tuple-element.57), channel_id=1, source_target_pairs={{6,0},{4,2},{7,1},{5,3},{14,8},{12,10},{15,9},{13,11},{22,16},{20,... | collective-permute-start | bytes 98312 | tf_op jit(solution)/shard_map/ppermute | solution.py:285
  71.2 2.3 %collective-permute-start.14 = (bf16[32,512]{1,0:T(8,128)(2,1)S(1)}, bf16[32,512]{1,0:T(8,128)(2,1)S(1)}, u32[]{:S(2)}, u32[]{:S(2)}) collective-permute-start(bf16[32,512]{1,0:T(8,128)(2,1)S(1)} %get-tuple-element.60), channel_id=1, source_target_pairs={{0,6},{2,4},{1,7},{3,5},{8,14},{10,12},{9,15},{11,13},{16,22},{18,... | collective-permute-start | bytes 98312 | tf_op jit(solution)/shard_map/ppermute | solution.py:291
  74.0 9.5 %collective-permute-start.15 = (bf16[32,512]{1,0:T(8,128)(2,1)S(1)}, bf16[32,512]{1,0:T(8,128)(2,1)S(1)}, u32[]{:S(2)}, u32[]{:S(2)}) collective-permute-start(bf16[32,512]{1,0:T(8,128)(2,1)S(1)} %get-tuple-element.68), channel_id=1, source_target_pairs={{6,0},{4,2},{7,1},{5,3},{14,8},{12,10},{15,9},{13,11},{22,16},{20,... | collective-permute-start | bytes 98312 | tf_op jit(solution)/shard_map/ppermute | solution.py:297

commit v3 on v2

--- a/solution.py
+++ b/solution.py
@@ -42,17 +42,17 @@
     return (v + dot(h, weight[1])).astype(BF16)
 
 
-def backward_level(g, weight, save, slot, acts, first=False):
+def backward_level(g, weight, save, slot, acts, side, first=False):
     save_q, save_z, save_r = save
     gh = dot_t(g, weight[1])
     z = save_z[slot]
     s = jax.nn.sigmoid(z)
     gz = (gh * s * (1.0 + z * (1.0 - s))).astype(BF16)
     q = save_q[slot]
-    acts[slot, 0] = q.astype(BF16)
-    acts[slot, 1] = gz
-    acts[slot, 2] = (z * s).astype(BF16)
-    acts[slot, 3] = g
+    acts[slot, side, 0] = q.astype(BF16)
+    acts[slot, side, 1] = gz
+    acts[slot, side, 2] = (z * s).astype(BF16)
+    acts[slot, side, 3] = g
     if first:
         return None
     gn = dot_t(gz, weight[0])
@@ -136,9 +136,7 @@
             wait_weights(place, held, sems, m)
 
 
-def turn_dec_kernel(
-    place, arrived, e, cotangent, weights, hop, skip_grads, acts, q, z, r, local_acts, acts_sem
-):
+def turn_dec_kernel(place, arrived, e, cotangent, weights, hop, skip_grads, acts, q, z, r):
     @pl.when(place[0] == 0)
     def _():
         x = arrived[...]
@@ -147,24 +145,19 @@
             x = forward_level(v, weights.at[m], (q, z, r), m)
         g = cotangent[place[1]]
         for m in UP:
-            g = backward_level(g, weights.at[m], (q, z, r), m, local_acts)
+            g = backward_level(g, weights.at[m], (q, z, r), m, acts, 1)
             skip_grads[m] = g
         hop[...] = g
-        out = pltpu.make_async_copy(local_acts, acts.at[:, 1], acts_sem)
-        out.start()
-        out.wait()
 
 
 def enc_backward(g, skip_grads, weights, save, acts, first=False):
     for m in DOWN:
         g = (g.astype(F32) + skip_grads[m].astype(F32)).astype(BF16)
-        g = backward_level(g, weights.at[m], save, m, acts, first and m == 0)
+        g = backward_level(g, weights.at[m], save, m, acts, 0, first and m == 0)
     return g
 
 
-def turn_backward_kernel(
-    place, arrived, qe, ze, re, qd, zd, rd, weights_e, weights_d, acts_in, hop, acts, acts_e, acts_d, acts_sems
-):
+def turn_backward_kernel(place, arrived, qe, ze, re, qd, zd, rd, weights_e, weights_d, acts_in, hop, acts):
     del acts_in
 
     @pl.when(place[0] == 1)
@@ -172,26 +165,17 @@
         g = arrived[...]
         skip_grads = []
         for m in UP:
-            g = backward_level(g, weights_d.at[m], (qd, zd, rd), m, acts_d)
+            g = backward_level(g, weights_d.at[m], (qd, zd, rd), m, acts, 1)
             skip_grads.append(g)
-        out_d = pltpu.make_async_copy(acts_d, acts.at[:, 1], acts_sems.at[1])
-        out_d.start()
-        hop[...] = enc_backward(g, skip_grads, weights_e, (qe, ze, re), acts_e)
-        out_e = pltpu.make_async_copy(acts_e, acts.at[:, 0], acts_sems.at[0])
-        out_e.start()
-        out_d.wait()
-        out_e.wait()
-
-
-def enc_backward_kernel(place, arrived, q, z, r, skip_grads, weights, acts_in, acts, local_acts, acts_sem):
+        hop[...] = enc_backward(g, skip_grads, weights_e, (qe, ze, re), acts)
+
+
+def enc_backward_kernel(place, arrived, q, z, r, skip_grads, weights, acts_in, acts):
     del acts_in
 
     @pl.when(place[0] == 0)
     def _():
-        enc_backward(arrived[...], skip_grads, weights, (q, z, r), local_acts, first=True)
-        out = pltpu.make_async_copy(local_acts, acts.at[:, 0], acts_sem)
-        out.start()
-        out.wait()
+        enc_backward(arrived[...], skip_grads, weights, (q, z, r), acts, first=True)
 
 
 def grads_kernel(acts, out):
@@ -205,6 +189,13 @@
                     out[z_low, x, core, z_high] = grad[first : first + 8].astype(BF16)
 
 
+def last_sum_kernel(factor, parts, grads_a, grads_b):
+    total = sum(parts[i].astype(F32) for i in range(4)) * factor
+    for side in (0, 1):
+        grads_a[side, 0] = total[2 * side]
+        grads_b[side, 0] = total[2 * side + 1]
+
+
 SMEM = pl.BlockSpec(memory_space=pltpu.SMEM)
 VMEM = pl.BlockSpec(memory_space=pltpu.VMEM)
 ANY = pl.BlockSpec(memory_space=pl.ANY)
@@ -220,7 +211,6 @@
 WEIGHTS = jax.ShapeDtypeStruct((LEVELS, 2, WIDTH, WIDTH), BF16)
 
 SEMS = pltpu.SemaphoreType.DMA((LEVELS,))
-LOCAL_ACTS = pltpu.VMEM((LEVELS, 4, ROWS, WIDTH), BF16)
 SCRATCH_SAVES = tuple(pltpu.VMEM(s.shape, s.dtype) for s in SAVES)
 
 
@@ -285,19 +275,17 @@
     arrived = lax.ppermute(hop, y, down)
     hop, skip_grads, acts = call(
         turn_dec_kernel, (place, arrived, e, cotangent, weights_d), (SMEM,) + (VMEM,) * 4,
-        (ROW, STACK, ACTS), (VMEM, VMEM, ANY),
-        SCRATCH_SAVES + (LOCAL_ACTS, pltpu.SemaphoreType.DMA), name="turn_dec",
+        (ROW, STACK, ACTS), (VMEM,) * 3, SCRATCH_SAVES, name="turn_dec",
     )
     arrived = lax.ppermute(hop, y, up)
     hop, acts = call(
-        turn_backward_kernel, (place, arrived, *saves, weights_e, weights_d, acts), (SMEM,) + (VMEM,) * 9 + (ANY,),
-        (ROW, ACTS), (VMEM, ANY),
-        (LOCAL_ACTS, LOCAL_ACTS, pltpu.SemaphoreType.DMA((2,))), {10: 1}, name="turn_backward",
+        turn_backward_kernel, (place, arrived, *saves, weights_e, weights_d, acts), (SMEM,) + (VMEM,) * 10,
+        (ROW, ACTS), (VMEM,) * 2, (), {10: 1}, name="turn_backward",
     )
     arrived = lax.ppermute(hop, y, down)
     acts = call(
-        enc_backward_kernel, (place, arrived, *saves_0, skip_grads, weights_e, acts), (SMEM,) + (VMEM,) * 6 + (ANY,),
-        ACTS, ANY, (LOCAL_ACTS, pltpu.SemaphoreType.DMA), {7: 0}, name="enc_backward",
+        enc_backward_kernel, (place, arrived, *saves_0, skip_grads, weights_e, acts), (SMEM,) + (VMEM,) * 7,
+        ACTS, VMEM, (), {7: 0}, name="enc_backward",
     )
 
     acts = lax.all_to_all(acts.reshape(16, 2, ROWS, WIDTH), MEMBERS + ("x_lo", "core"), 0, 0)
@@ -309,8 +297,10 @@
     total = jnp.sum(total.astype(F32).reshape(4, 4, 4, 8, WIDTH), axis=0).astype(BF16)
     total = lax.all_to_all(total.transpose(1, 0, 2, 3), "z_hi", 0, 0)
     factor = 1.0 / math.sqrt(LEVELS * ROWS * 64)
-    total = jnp.sum(total.astype(F32), axis=0).reshape(2, 2, 1, 8, WIDTH) * factor
-    return total[:, 0], total[:, 1]
+    out = jax.ShapeDtypeStruct((2, 1, 8, WIDTH), F32)
+    return tuple(
+        call(functools.partial(last_sum_kernel, factor), (total,), (VMEM,), (out, out), (VMEM, VMEM), name="last_sum")
+    )
 
 
 MEMBERS = ("y_lo", "x_hi")

time: 159 us -> 158 us (level)
    unnamed x9 -> x8, local copies, waits for them, and re-layouts: 3.99 us -> 3.36 us
    pallas_call x7 -> x8, Pallas kernels: 11.7 us -> 12.2 us  [call(): pl.pallas_call(kernel, out_shape=outs, in_specs=spaces, out_specs=out_spa...]
where the time goes in v3:
time: 158 us
  blocking collectives  70.7 us (45%)
  starting transfers between devices  48 us (30%)
  waiting for transfers between devices  22.1 us (14%)
  Pallas kernels  12.2 us (8%)
  local copies, waits for them, and re-layouts  3.37 us (2%)
    all_to_all x1, blocking collectives, local(): total = lax.all_to_all(total.transpose(1, 0, 2, 3), 'z_hi', 0, 0)  26.9 us
    all_to_all x1, blocking collectives, local(): lax.all_to_all(acts.reshape(16, 2, ROWS, WIDTH), MEMBERS + ('x_lo', 'core...  23.1 us
    ppermute x6, starting transfers between devices, swap(): return lax.ppermute(block, 'core', [(0, 1), (1, 0)])  21.9 us
    all_to_all x1, blocking collectives, local(): lax.all_to_all(grad.reshape(16, 4, 8, WIDTH), ('z_lo', 'x_lo', 'core'), 0...  20.7 us
    ppermute x2, waiting for transfers between devices, local(): arrived = lax.ppermute(hop, y, down)  15.7 us
    pallas_call x8, Pallas kernels, call(): pl.pallas_call(kernel, out_shape=outs, in_specs=spaces, out_specs=out_spa...  12.2 us
    ppermute x3, starting transfers between devices, along_x(): return lax.ppermute(block, ('x_lo', 'x_hi'), [(i, 3 - i) for i in range(4)])  10.9 us
    ppermute x3, starting transfers between devices, along_y(): return lax.ppermute(block, 'y_lo', [(0, 1), (1, 0)])  8.49 us
  transfers between devices with their start and end apart: 16, of which 7 were waited for; matrix products, arithmetic and copies ran while one was open for 0% of the time, Pallas kernels for 0%

profile of v3, /device:TPU:33, one launch (start us, length us, event | category | flops | bytes accessed | tf_op | source)
XLA Modules:
  0.0 157.5 jit_solution(12998211481464073077)
XLA Ops:
  4.0 3.2 %collective-permute-start.2 = (bf16[2,256,512]{2,1,0:T(8,128)(2,1)S(1)}, bf16[2,256,512]{2,1,0:T(8,128)(2,1)S(1)}, u32[]{:S(2)}, u32[]{:S(2)}) collective-permute-start(bf16[2,256,512]{2,1,0:T(8,128)(2,1)S(1)} %get-tuple-element.38), channel_id=1, source_target_pairs={{0,2},{2,0},{1,3},{3,1},{4,6},{6,4},{5,7},{7,5},{8,10},{10,8},{9,1... | collective-permute-start | bytes 1572872 | tf_op jit(solution)/shard_map/ppermute | solution.py:245
  7.3 4.4 %collective-permute-start = (bf16[2,256,512]{2,1,0:T(8,128)(2,1)S(1)}, bf16[2,256,512]{2,1,0:T(8,128)(2,1)S(1)}, u32[]{:S(2)}, u32[]{:S(2)}) collective-permute-start(bf16[2,256,512]{2,1,0:T(8,128)(2,1)S(1)} %get-tuple-element.38), channel_id=1, source_target_pairs={{0,257},{1,256},{256,1},{257,0},{2,259},{3,258},{258,3},{259,2},{4... | collective-permute-start | bytes 1572872 | tf_op jit(solution)/shard_map/ppermute | solution.py:242
  11.6 2.1 %collective-permute-start.8 = (bf16[2,256,512]{2,1,0:T(8,128)(2,1)S(1)}, bf16[2,256,512]{2,1,0:T(8,128)(2,1)S(1)}, u32[]{:S(2)}, u32[]{:S(2)}) collective-permute-start(bf16[2,256,512]{2,1,0:T(8,128)(2,1)S(1)} %get-tuple-element.39), channel_id=1, source_target_pairs={{0,2},{2,0},{1,3},{3,1},{4,6},{6,4},{5,7},{7,5},{8,10},{10,8},{9,1... | collective-permute-start | bytes 1572872 | tf_op jit(solution)/shard_map/ppermute | solution.py:245
  13.7 2.1 %collective-permute-start.6 = (bf16[2,256,512]{2,1,0:T(8,128)(2,1)S(1)}, bf16[2,256,512]{2,1,0:T(8,128)(2,1)S(1)}, u32[]{:S(2)}, u32[]{:S(2)}) collective-permute-start(bf16[2,256,512]{2,1,0:T(8,128)(2,1)S(1)} %get-tuple-element.39), channel_id=1, source_target_pairs={{0,257},{1,256},{256,1},{257,0},{2,259},{3,258},{258,3},{259,2},{4... | collective-permute-start | bytes 1572872 | tf_op jit(solution)/shard_map/ppermute | solution.py:242
  15.8 2.9 %collective-permute-done.2.refs_2_ = bf16[2,256,512]{2,1,0:T(8,128)(2,1)S(1)} collective-permute-done((bf16[2,256,512]{2,1,0:T(8,128)(2,1)S(1)}, bf16[2,256,512]{2,1,0:T(8,128)(2,1)S(1)}, u32[]{:S(2)}, u32[]{:S(2)}) %collective-permute-start.2) | collective-permute-done | bytes 524320 | tf_op jit(solution)/shard_map/ppermute | solution.py:245
  18.7 4.6 %collective-permute-start.3 = (bf16[2,256,512]{2,1,0:T(8,128)(2,1)S(1)}, bf16[2,256,512]{2,1,0:T(8,128)(2,1)S(1)}, u32[]{:S(2)}, u32[]{:S(2)}) collective-permute-start(bf16[2,256,512]{2,1,0:T(8,128)(2,1)S(1)} %collective-permute-done.2.refs_2_), channel_id=1, source_target_pairs={{0,8},{8,0},{1,9},{9,1},{2,10},{10,2},{3,11},{11,3},{4,12},{12,4},... | collective-permute-start | bytes 1572872 | tf_op jit(solution)/shard_map/ppermute | solution.py:248
  23.3 3.2 %collective-permute-start.4 = (bf16[2,256,512]{2,1,0:T(8,128)(2,1)S(1)}, bf16[2,256,512]{2,1,0:T(8,128)(2,1)S(1)}, u32[]{:S(2)}, u32[]{:S(2)}) collective-permute-start(bf16[2,256,512]{2,1,0:T(8,128)(2,1)S(1)} %collective-permute-done.refs_0_), channel_id=1, source_target_pairs={{0,2},{2,0},{1,3},{3,1},{4,6},{6,4},{5,7},{7,5},{8,10},{10,8},{9,1... | collective-permute-start | bytes 1572872 | tf_op jit(solution)/shard_map/ppermute | solution.py:245
  26.5 3.9 %collective-permute-start.1 = (bf16[2,256,512]{2,1,0:T(8,128)(2,1)S(1)}, bf16[2,256,512]{2,1,0:T(8,128)(2,1)S(1)}, u32[]{:S(2)}, u32[]{:S(2)}) collective-permute-start(bf16[2,256,512]{2,1,0:T(8,128)(2,1)S(1)} %collective-permute-done.refs_0_), channel_id=1, source_target_pairs={{0,8},{8,0},{1,9},{9,1},{2,10},{10,2},{3,11},{11,3},{4,12},{12,4},... | collective-permute-start | bytes 1572872 | tf_op jit(solution)/shard_map/ppermute | solution.py:248
  30.4 4.4 %collective-permute-start.10 = (bf16[2,256,512]{2,1,0:T(8,128)(2,1)S(1)}, bf16[2,256,512]{2,1,0:T(8,128)(2,1)S(1)}, u32[]{:S(2)}, u32[]{:S(2)}) collective-permute-start(bf16[2,256,512]{2,1,0:T(8,128)(2,1)S(1)} %collective-permute-done.8.refs_2_), channel_id=1, source_target_pairs={{0,257},{1,256},{256,1},{257,0},{2,259},{3,258},{258,3},{259,2},{4... | collective-permute-start | bytes 1572872 | tf_op jit(solution)/shard_map/ppermute | solution.py:242
  34.8 4.4 %collective-permute-start.9 = (bf16[2,256,512]{2,1,0:T(8,128)(2,1)S(1)}, bf16[2,256,512]{2,1,0:T(8,128)(2,1)S(1)}, u32[]{:S(2)}, u32[]{:S(2)}) collective-permute-start(bf16[2,256,512]{2,1,0:T(8,128)(2,1)S(1)} %collective-permute-done.8.refs_2_), channel_id=1, source_target_pairs={{0,8},{8,0},{1,9},{9,1},{2,10},{10,2},{3,11},{11,3},{4,12},{12,4},... | collective-permute-start | bytes 1572872 | tf_op jit(solution)/shard_map/ppermute | solution.py:248
  39.3 1.9 %collective-permute-start.7 = (bf16[2,256,512]{2,1,0:T(8,128)(2,1)S(1)}, bf16[2,256,512]{2,1,0:T(8,128)(2,1)S(1)}, u32[]{:S(2)}, u32[]{:S(2)}) collective-permute-start(bf16[2,256,512]{2,1,0:T(8,128)(2,1)S(1)} %collective-permute-done.6.refs_0_), channel_id=1, source_target_pairs={{0,8},{8,0},{1,9},{9,1},{2,10},{10,2},{3,11},{11,3},{4,12},{12,4},... | collective-permute-start | bytes 1572872 | tf_op jit(solution)/shard_map/ppermute | solution.py:248
  41.2 3.4 %collective-permute-start.5 = (bf16[2,256,512]{2,1,0:T(8,128)(2,1)S(1)}, bf16[2,256,512]{2,1,0:T(8,128)(2,1)S(1)}, u32[]{:S(2)}, u32[]{:S(2)}) collective-permute-start(bf16[2,256,512]{2,1,0:T(8,128)(2,1)S(1)} %collective-permute-done.4.refs_4_), channel_id=1, source_target_pairs={{0,8},{8,0},{1,9},{9,1},{2,10},{10,2},{3,11},{11,3},{4,12},{12,4},... | collective-permute-start | bytes 1572872 | tf_op jit(solution)/shard_map/ppermute | solution.py:248
  44.8 1.4 collective-permute-done.5.refs_5_
  47.1 2.6 %enc_forward.1 = (bf16[32,512]{1,0:T(8,128)(2,1)S(1)}, bf16[4,32,512]{2,1,0:T(8,128)(2,1)S(1)}, f32[4,32,512]{2,1,0:T(8,128)S(1)}, f32[4,32,512]{2,1,0:T(8,128)S...) custom-call(s32[4]{0:T(128)S(1)} %pad_add_fusion.place, ...), custom_call_target="tpu_custom_call", output_to_operand_aliasing={{5}: (8, {})} | custom-call | tf_op jit(solution)/shard_map/enc_forward/pallas_call | solution.py:218
  49.7 3.6 %collective-permute-start.12 = (bf16[2,256,512]{2,1,0:T(8,128)(2,1)S(1)}, bf16[2,256,512]{2,1,0:T(8,128)(2,1)S(1)}, u32[]{:S(2)}, u32[]{:S(2)}) collective-permute-start(bf16[2,256,512]{2,1,0:T(8,128)(2,1)S(1)} %collective-permute-done.10.refs_4_), channel_id=1, source_target_pairs={{0,8},{8,0},{1,9},{9,1},{2,10},{10,2},{3,11},{11,3},{4,12},{12,4},... | collective-permute-start | bytes 1572872 | tf_op jit(solution)/shard_map/ppermute | solution.py:248
  53.4 2.9 %collective-permute-start.11 = (bf16[32,512]{1,0:T(8,128)(2,1)S(1)}, bf16[32,512]{1,0:T(8,128)(2,1)S(1)}, u32[]{:S(2)}, u32[]{:S(2)}) collective-permute-start(bf16[32,512]{1,0:T(8,128)(2,1)S(1)} %get-tuple-element.49), channel_id=1, source_target_pairs={{0,6},{2,4},{1,7},{3,5},{8,14},{10,12},{9,15},{11,13},{16,22},{18,... | collective-permute-start | bytes 98312 | tf_op jit(solution)/shard_map/ppermute | solution.py:268
  58.3 1.3 collective-permute-start.13
  59.6 7.6 %collective-permute-done.13.arrived = bf16[32,512]{1,0:T(8,128)(2,1)S(1)} collective-permute-done((bf16[32,512]{1,0:T(8,128)(2,1)S(1)}, bf16[32,512]{1,0:T(8,128)(2,1)S(1)}, u32[]{:S(2)}, u32[]{:S(2)}) %collective-permute-start.13) | collective-permute-done | bytes 32800 | tf_op jit(solution)/shard_map/ppermute | solution.py:275
  67.2 3.9 %turn_dec.1 = (bf16[32,512]{1,0:T(8,128)(2,1)S(1)}, bf16[4,32,512]{2,1,0:T(8,128)(2,1)S(1)}, bf16[4,2,4,32,512]{4,3,2,1,0:T(8,128)(2,1)S(1)}) custom-call(s32[4]{0:T(128)S(1)} %pad_add_fusion.place, bf16[32,512]{1,0:T(8,128)(2,1)S(1)} %collective-permute-done.13.arrived, bf16[4,32,512]{2,1,0:T(8,128)(2,1)S(1)} %get-tuple-element.58.e, ...), custom_call_target="tpu_custom_call" | custom-call | tf_op jit(solution)/shard_map/turn_dec/pallas_call | solution.py:218
  75.3 8.1 %collective-permute-done.15.arrived = bf16[32,512]{1,0:T(8,128)(2,1)S(1)} collective-permute-done((bf16[32,512]{1,0:T(8,128)(2,1)S(1)}, bf16[32,512]{1,0:T(8,128)(2,1)S(1)}, u32[]{:S(2)}, u32[]{:S(2)}) %collective-permute-start.15) | collective-permute-done | bytes 32800 | tf_op jit(solution)/shard_map/ppermute | solution.py:285
  83.3 2.2 %enc_backward.1 = bf16[4,2,4,32,512]{4,3,2,1,0:T(8,128)(2,1)S(1)} custom-call(s32[4]{0:T(128)S(1)} %pad_add_fusion.place, bf16[32,512]{1,0:T(8,128)(2,1)S(1)} %collective-permute-done.15.arrived, f32[4,32,512]{2,1,0:T(8,128)S(1)} %get-tuple-element.69.q, f32[4,32,512]{2,1,0:T(8,128)S(1)} %get-tuple-element.70.z, ...), custom_call_target="tpu_custom_call", output_to_operand_aliasing={{}: (7, {})} | custom-call | tf_op jit(solution)/shard_map/enc_backward/pallas_call | solution.py:218
  85.6 23.1 %all_to_all.15.acts = bf16[16,2,32,512]{3,2,1,0:T(8,128)(2,1)S(1)} all-to-all(bf16[16,2,32,512]{3,2,1,0:T(8,128)(2,1)S(1)} %bitcast.10), channel_id=1, replica_groups=mesh['x_lo'=2,'z_hi'=4,'z_lo'=4,'core'=2,'stage'=2,'y_lo'=2,'x_hi'=2] {'..., dimensions={0} | all-to-all | bytes 2097152 | tf_op jit(solution)/shard_map/all_to_all | solution.py:291
  109.2 20.7 %all_to_all.16 = bf16[16,4,8,512]{3,2,1,0:T(8,128)(2,1)S(1)} all-to-all(bf16[16,4,8,512]{3,2,1,0:T(8,128)(2,1)S(1)} %bitcast.11), channel_id=1, replica_groups=mesh['x_lo'=2,'z_hi'=4,'z_lo'=4,'core'=2,'stage'=2,'y_lo'=2,'x_hi'=2] {'..., dimensions={0} | all-to-all | bytes 1048576 | tf_op jit(solution)/shard_map/all_to_all | solution.py:296
  129.9 26.9 %all_to_all.17.parts = bf16[4,4,8,512]{3,2,1,0:T(8,128)(2,1)S(1)} all-to-all(bf16[4,4,8,512]{3,2,1,0:T(8,128)(2,1)S(1)} %bitcast.13), channel_id=1, replica_groups=mesh['x_lo'=2,'z_hi'=4,'z_lo'=4,'core'=2,'stage'=2,'y_lo'=2,'x_hi'=2] {'..., dimensions={0} | all-to-all | bytes 262144 | tf_op jit(solution)/shard_map/all_to_all | solution.py:298
  (30 shorter events, 11.7 us)
Async XLA Ops:
  0.7 1.2 copy-start
  2.0 1.2 copy-start.1
  4.0 14.7 %collective-permute-start.2 = (bf16[2,256,512]{2,1,0:T(8,128)(2,1)S(1)}, bf16[2,256,512]{2,1,0:T(8,128)(2,1)S(1)}, u32[]{:S(2)}, u32[]{:S(2)}) collective-permute-start(bf16[2,256,512]{2,1,0:T(8,128)(2,1)S(1)} %get-tuple-element.38), channel_id=1, source_target_pairs={{0,2},{2,0},{1,3},{3,1},{4,6},{6,4},{5,7},{7,5},{8,10},{10,8},{9,1... | collective-permute-start | bytes 1572872 | tf_op jit(solution)/shard_map/ppermute | solution.py:245
  7.3 16.1 %collective-permute-start = (bf16[2,256,512]{2,1,0:T(8,128)(2,1)S(1)}, bf16[2,256,512]{2,1,0:T(8,128)(2,1)S(1)}, u32[]{:S(2)}, u32[]{:S(2)}) collective-permute-start(bf16[2,256,512]{2,1,0:T(8,128)(2,1)S(1)} %get-tuple-element.38), channel_id=1, source_target_pairs={{0,257},{1,256},{256,1},{257,0},{2,259},{3,258},{258,3},{259,2},{4... | collective-permute-start | bytes 1572872 | tf_op jit(solution)/shard_map/ppermute | solution.py:242
  11.6 18.8 %collective-permute-start.8 = (bf16[2,256,512]{2,1,0:T(8,128)(2,1)S(1)}, bf16[2,256,512]{2,1,0:T(8,128)(2,1)S(1)}, u32[]{:S(2)}, u32[]{:S(2)}) collective-permute-start(bf16[2,256,512]{2,1,0:T(8,128)(2,1)S(1)} %get-tuple-element.39), channel_id=1, source_target_pairs={{0,2},{2,0},{1,3},{3,1},{4,6},{6,4},{5,7},{7,5},{8,10},{10,8},{9,1... | collective-permute-start | bytes 1572872 | tf_op jit(solution)/shard_map/ppermute | solution.py:245
  13.7 21.1 %collective-permute-start.6 = (bf16[2,256,512]{2,1,0:T(8,128)(2,1)S(1)}, bf16[2,256,512]{2,1,0:T(8,128)(2,1)S(1)}, u32[]{:S(2)}, u32[]{:S(2)}) collective-permute-start(bf16[2,256,512]{2,1,0:T(8,128)(2,1)S(1)} %get-tuple-element.39), channel_id=1, source_target_pairs={{0,257},{1,256},{256,1},{257,0},{2,259},{3,258},{258,3},{259,2},{4... | collective-permute-start | bytes 1572872 | tf_op jit(solution)/shard_map/ppermute | solution.py:242
  18.7 20.5 %collective-permute-start.3 = (bf16[2,256,512]{2,1,0:T(8,128)(2,1)S(1)}, bf16[2,256,512]{2,1,0:T(8,128)(2,1)S(1)}, u32[]{:S(2)}, u32[]{:S(2)}) collective-permute-start(bf16[2,256,512]{2,1,0:T(8,128)(2,1)S(1)} %collective-permute-done.2.refs_2_), channel_id=1, source_target_pairs={{0,8},{8,0},{1,9},{9,1},{2,10},{10,2},{3,11},{11,3},{4,12},{12,4},... | collective-permute-start | bytes 1572872 | tf_op jit(solution)/shard_map/ppermute | solution.py:248
  23.3 17.9 %collective-permute-start.4 = (bf16[2,256,512]{2,1,0:T(8,128)(2,1)S(1)}, bf16[2,256,512]{2,1,0:T(8,128)(2,1)S(1)}, u32[]{:S(2)}, u32[]{:S(2)}) collective-permute-start(bf16[2,256,512]{2,1,0:T(8,128)(2,1)S(1)} %collective-permute-done.refs_0_), channel_id=1, source_target_pairs={{0,2},{2,0},{1,3},{3,1},{4,6},{6,4},{5,7},{7,5},{8,10},{10,8},{9,1... | collective-permute-start | bytes 1572872 | tf_op jit(solution)/shard_map/ppermute | solution.py:245
  26.5 18.1 %collective-permute-start.1 = (bf16[2,256,512]{2,1,0:T(8,128)(2,1)S(1)}, bf16[2,256,512]{2,1,0:T(8,128)(2,1)S(1)}, u32[]{:S(2)}, u32[]{:S(2)}) collective-permute-start(bf16[2,256,512]{2,1,0:T(8,128)(2,1)S(1)} %collective-permute-done.refs_0_), channel_id=1, source_target_pairs={{0,8},{8,0},{1,9},{9,1},{2,10},{10,2},{3,11},{11,3},{4,12},{12,4},... | collective-permute-start | bytes 1572872 | tf_op jit(solution)/shard_map/ppermute | solution.py:248
  30.4 14.3 %collective-permute-start.10 = (bf16[2,256,512]{2,1,0:T(8,128)(2,1)S(1)}, bf16[2,256,512]{2,1,0:T(8,128)(2,1)S(1)}, u32[]{:S(2)}, u32[]{:S(2)}) collective-permute-start(bf16[2,256,512]{2,1,0:T(8,128)(2,1)S(1)} %collective-permute-done.8.refs_2_), channel_id=1, source_target_pairs={{0,257},{1,256},{256,1},{257,0},{2,259},{3,258},{258,3},{259,2},{4... | collective-permute-start | bytes 1572872 | tf_op jit(solution)/shard_map/ppermute | solution.py:242
  34.8 9.9 %collective-permute-start.9 = (bf16[2,256,512]{2,1,0:T(8,128)(2,1)S(1)}, bf16[2,256,512]{2,1,0:T(8,128)(2,1)S(1)}, u32[]{:S(2)}, u32[]{:S(2)}) collective-permute-start(bf16[2,256,512]{2,1,0:T(8,128)(2,1)S(1)} %collective-permute-done.8.refs_2_), channel_id=1, source_target_pairs={{0,8},{8,0},{1,9},{9,1},{2,10},{10,2},{3,11},{11,3},{4,12},{12,4},... | collective-permute-start | bytes 1572872 | tf_op jit(solution)/shard_map/ppermute | solution.py:248
  39.3 5.5 %collective-permute-start.7 = (bf16[2,256,512]{2,1,0:T(8,128)(2,1)S(1)}, bf16[2,256,512]{2,1,0:T(8,128)(2,1)S(1)}, u32[]{:S(2)}, u32[]{:S(2)}) collective-permute-start(bf16[2,256,512]{2,1,0:T(8,128)(2,1)S(1)} %collective-permute-done.6.refs_0_), channel_id=1, source_target_pairs={{0,8},{8,0},{1,9},{9,1},{2,10},{10,2},{3,11},{11,3},{4,12},{12,4},... | collective-permute-start | bytes 1572872 | tf_op jit(solution)/shard_map/ppermute | solution.py:248
  41.2 5.0 %collective-permute-start.5 = (bf16[2,256,512]{2,1,0:T(8,128)(2,1)S(1)}, bf16[2,256,512]{2,1,0:T(8,128)(2,1)S(1)}, u32[]{:S(2)}, u32[]{:S(2)}) collective-permute-start(bf16[2,256,512]{2,1,0:T(8,128)(2,1)S(1)} %collective-permute-done.4.refs_4_), channel_id=1, source_target_pairs={{0,8},{8,0},{1,9},{9,1},{2,10},{10,2},{3,11},{11,3},{4,12},{12,4},... | collective-permute-start | bytes 1572872 | tf_op jit(solution)/shard_map/ppermute | solution.py:248
  46.2 0.9 copy-start.2
  49.7 7.6 %collective-permute-start.12 = (bf16[2,256,512]{2,1,0:T(8,128)(2,1)S(1)}, bf16[2,256,512]{2,1,0:T(8,128)(2,1)S(1)}, u32[]{:S(2)}, u32[]{:S(2)}) collective-permute-start(bf16[2,256,512]{2,1,0:T(8,128)(2,1)S(1)} %collective-permute-done.10.refs_4_), channel_id=1, source_target_pairs={{0,8},{8,0},{1,9},{9,1},{2,10},{10,2},{3,11},{11,3},{4,12},{12,4},... | collective-permute-start | bytes 1572872 | tf_op jit(solution)/shard_map/ppermute | solution.py:248
  53.4 3.9 %collective-permute-start.11 = (bf16[32,512]{1,0:T(8,128)(2,1)S(1)}, bf16[32,512]{1,0:T(8,128)(2,1)S(1)}, u32[]{:S(2)}, u32[]{:S(2)}) collective-permute-start(bf16[32,512]{1,0:T(8,128)(2,1)S(1)} %get-tuple-element.49), channel_id=1, source_target_pairs={{0,6},{2,4},{1,7},{3,5},{8,14},{10,12},{9,15},{11,13},{16,22},{18,... | collective-permute-start | bytes 98312 | tf_op jit(solution)/shard_map/ppermute | solution.py:268
  57.3 9.9 %copy-start.3 = (bf16[4,32,512]{2,1,0:T(8,128)(2,1)S(1)}, bf16[4,32,512]{2,1,0:T(8,128)(2,1)}, u32[]{:S(2)}) copy-start(bf16[4,32,512]{2,1,0:T(8,128)(2,1)} %cotangent.1) | copy-start | bytes 393220
  58.3 8.9 %collective-permute-start.13 = (bf16[32,512]{1,0:T(8,128)(2,1)S(1)}, bf16[32,512]{1,0:T(8,128)(2,1)S(1)}, u32[]{:S(2)}, u32[]{:S(2)}) collective-permute-start(bf16[32,512]{1,0:T(8,128)(2,1)S(1)} %get-tuple-element.57), channel_id=1, source_target_pairs={{6,0},{4,2},{7,1},{5,3},{14,8},{12,10},{15,9},{13,11},{22,16},{20,... | collective-permute-start | bytes 98312 | tf_op jit(solution)/shard_map/ppermute | solution.py:275
  71.1 2.3 %collective-permute-start.14 = (bf16[32,512]{1,0:T(8,128)(2,1)S(1)}, bf16[32,512]{1,0:T(8,128)(2,1)S(1)}, u32[]{:S(2)}, u32[]{:S(2)}) collective-permute-start(bf16[32,512]{1,0:T(8,128)(2,1)S(1)} %get-tuple-element.60), channel_id=1, source_target_pairs={{0,6},{2,4},{1,7},{3,5},{8,14},{10,12},{9,15},{11,13},{16,22},{18,... | collective-permute-start | bytes 98312 | tf_op jit(solution)/shard_map/ppermute | solution.py:280
  74.0 9.4 %collective-permute-start.15 = (bf16[32,512]{1,0:T(8,128)(2,1)S(1)}, bf16[32,512]{1,0:T(8,128)(2,1)S(1)}, u32[]{:S(2)}, u32[]{:S(2)}) collective-permute-start(bf16[32,512]{1,0:T(8,128)(2,1)S(1)} %get-tuple-element.68), channel_id=1, source_target_pairs={{6,0},{4,2},{7,1},{5,3},{14,8},{12,10},{15,9},{13,11},{22,16},{20,... | collective-permute-start | bytes 98312 | tf_op jit(solution)/shard_map/ppermute | solution.py:285

commit v4 on v3

--- a/solution.py
+++ b/solution.py
@@ -264,7 +264,6 @@
         enc_forward_kernel, (place, pixels, *pieces[:6], own_e), (SMEM, VMEM) + (ANY,) * N_PIECES + (VMEM,),
         (ROW, STACK) + SAVES + (WEIGHTS,), (VMEM,) * 6, (SEMS,), {2 + N_PIECES: 5}, name="enc_forward",
     )
-    hop, diagonal_d = lax.optimization_barrier((hop, diagonal_d))
     arrived = lax.ppermute(hop, y, up)
     pieces = (*pieces[6:], diagonal_d, swap(diagonal_d))
     hop, *saves, weights_d = call(

time: 158 us -> 158 us (level)
  transfers between devices with their start and end apart: 16 -> 16, of which waited for: 7 -> 7; matrix products, arithmetic and copies ran while one was open for 0% -> 0% of each run, Pallas kernels for 0% -> 2%
where the time goes in v4:
time: 158 us
  blocking collectives  70.7 us (45%)
  starting transfers between devices  48 us (30%)
  waiting for transfers between devices  22.1 us (14%)
  Pallas kernels  12.2 us (8%)
  local copies, waits for them, and re-layouts  3.36 us (2%)
    all_to_all x1, blocking collectives, local(): total = lax.all_to_all(total.transpose(1, 0, 2, 3), 'z_hi', 0, 0)  26.9 us
    all_to_all x1, blocking collectives, local(): lax.all_to_all(acts.reshape(16, 2, ROWS, WIDTH), MEMBERS + ('x_lo', 'core...  23.1 us
    ppermute x6, starting transfers between devices, swap(): return lax.ppermute(block, 'core', [(0, 1), (1, 0)])  21.9 us
    all_to_all x1, blocking collectives, local(): lax.all_to_all(grad.reshape(16, 4, 8, WIDTH), ('z_lo', 'x_lo', 'core'), 0...  20.7 us
    ppermute x2, waiting for transfers between devices, local(): arrived = lax.ppermute(hop, y, down)  15.7 us
    pallas_call x8, Pallas kernels, call(): pl.pallas_call(kernel, out_shape=outs, in_specs=spaces, out_specs=out_spa...  12.2 us
    ppermute x3, starting transfers between devices, along_x(): return lax.ppermute(block, ('x_lo', 'x_hi'), [(i, 3 - i) for i in range(4)])  10.9 us
    ppermute x3, starting transfers between devices, along_y(): return lax.ppermute(block, 'y_lo', [(0, 1), (1, 0)])  8.49 us
  transfers between devices with their start and end apart: 16, of which 7 were waited for; matrix products, arithmetic and copies ran while one was open for 0% of the time, Pallas kernels for 2%

profile of v4, /device:TPU:33, one launch (start us, length us, event | category | flops | bytes accessed | tf_op | source)
XLA Modules:
  0.0 157.5 jit_solution(16356930289039110957)
XLA Ops:
  4.0 3.2 %collective-permute-start.2 = (bf16[2,256,512]{2,1,0:T(8,128)(2,1)S(1)}, bf16[2,256,512]{2,1,0:T(8,128)(2,1)S(1)}, u32[]{:S(2)}, u32[]{:S(2)}) collective-permute-start(bf16[2,256,512]{2,1,0:T(8,128)(2,1)S(1)} %get-tuple-element.36), channel_id=1, source_target_pairs={{0,2},{2,0},{1,3},{3,1},{4,6},{6,4},{5,7},{7,5},{8,10},{10,8},{9,1... | collective-permute-start | bytes 1572872 | tf_op jit(solution)/shard_map/ppermute | solution.py:245
  7.3 4.4 %collective-permute-start = (bf16[2,256,512]{2,1,0:T(8,128)(2,1)S(1)}, bf16[2,256,512]{2,1,0:T(8,128)(2,1)S(1)}, u32[]{:S(2)}, u32[]{:S(2)}) collective-permute-start(bf16[2,256,512]{2,1,0:T(8,128)(2,1)S(1)} %get-tuple-element.36), channel_id=1, source_target_pairs={{0,257},{1,256},{256,1},{257,0},{2,259},{3,258},{258,3},{259,2},{4... | collective-permute-start | bytes 1572872 | tf_op jit(solution)/shard_map/ppermute | solution.py:242
  11.6 2.1 %collective-permute-start.8 = (bf16[2,256,512]{2,1,0:T(8,128)(2,1)S(1)}, bf16[2,256,512]{2,1,0:T(8,128)(2,1)S(1)}, u32[]{:S(2)}, u32[]{:S(2)}) collective-permute-start(bf16[2,256,512]{2,1,0:T(8,128)(2,1)S(1)} %get-tuple-element.37), channel_id=1, source_target_pairs={{0,2},{2,0},{1,3},{3,1},{4,6},{6,4},{5,7},{7,5},{8,10},{10,8},{9,1... | collective-permute-start | bytes 1572872 | tf_op jit(solution)/shard_map/ppermute | solution.py:245
  13.7 2.1 %collective-permute-start.6 = (bf16[2,256,512]{2,1,0:T(8,128)(2,1)S(1)}, bf16[2,256,512]{2,1,0:T(8,128)(2,1)S(1)}, u32[]{:S(2)}, u32[]{:S(2)}) collective-permute-start(bf16[2,256,512]{2,1,0:T(8,128)(2,1)S(1)} %get-tuple-element.37), channel_id=1, source_target_pairs={{0,257},{1,256},{256,1},{257,0},{2,259},{3,258},{258,3},{259,2},{4... | collective-permute-start | bytes 1572872 | tf_op jit(solution)/shard_map/ppermute | solution.py:242
  15.8 2.9 %collective-permute-done.2.refs_2_ = bf16[2,256,512]{2,1,0:T(8,128)(2,1)S(1)} collective-permute-done((bf16[2,256,512]{2,1,0:T(8,128)(2,1)S(1)}, bf16[2,256,512]{2,1,0:T(8,128)(2,1)S(1)}, u32[]{:S(2)}, u32[]{:S(2)}) %collective-permute-start.2) | collective-permute-done | bytes 524320 | tf_op jit(solution)/shard_map/ppermute | solution.py:245
  18.7 4.6 %collective-permute-start.3 = (bf16[2,256,512]{2,1,0:T(8,128)(2,1)S(1)}, bf16[2,256,512]{2,1,0:T(8,128)(2,1)S(1)}, u32[]{:S(2)}, u32[]{:S(2)}) collective-permute-start(bf16[2,256,512]{2,1,0:T(8,128)(2,1)S(1)} %collective-permute-done.2.refs_2_), channel_id=1, source_target_pairs={{0,8},{8,0},{1,9},{9,1},{2,10},{10,2},{3,11},{11,3},{4,12},{12,4},... | collective-permute-start | bytes 1572872 | tf_op jit(solution)/shard_map/ppermute | solution.py:248
  23.3 3.2 %collective-permute-start.4 = (bf16[2,256,512]{2,1,0:T(8,128)(2,1)S(1)}, bf16[2,256,512]{2,1,0:T(8,128)(2,1)S(1)}, u32[]{:S(2)}, u32[]{:S(2)}) collective-permute-start(bf16[2,256,512]{2,1,0:T(8,128)(2,1)S(1)} %collective-permute-done.refs_0_), channel_id=1, source_target_pairs={{0,2},{2,0},{1,3},{3,1},{4,6},{6,4},{5,7},{7,5},{8,10},{10,8},{9,1... | collective-permute-start | bytes 1572872 | tf_op jit(solution)/shard_map/ppermute | solution.py:245
  26.5 3.9 %collective-permute-start.1 = (bf16[2,256,512]{2,1,0:T(8,128)(2,1)S(1)}, bf16[2,256,512]{2,1,0:T(8,128)(2,1)S(1)}, u32[]{:S(2)}, u32[]{:S(2)}) collective-permute-start(bf16[2,256,512]{2,1,0:T(8,128)(2,1)S(1)} %collective-permute-done.refs_0_), channel_id=1, source_target_pairs={{0,8},{8,0},{1,9},{9,1},{2,10},{10,2},{3,11},{11,3},{4,12},{12,4},... | collective-permute-start | bytes 1572872 | tf_op jit(solution)/shard_map/ppermute | solution.py:248
  30.4 4.4 %collective-permute-start.10 = (bf16[2,256,512]{2,1,0:T(8,128)(2,1)S(1)}, bf16[2,256,512]{2,1,0:T(8,128)(2,1)S(1)}, u32[]{:S(2)}, u32[]{:S(2)}) collective-permute-start(bf16[2,256,512]{2,1,0:T(8,128)(2,1)S(1)} %collective-permute-done.8.refs_2_), channel_id=1, source_target_pairs={{0,257},{1,256},{256,1},{257,0},{2,259},{3,258},{258,3},{259,2},{4... | collective-permute-start | bytes 1572872 | tf_op jit(solution)/shard_map/ppermute | solution.py:242
  34.8 4.4 %collective-permute-start.9 = (bf16[2,256,512]{2,1,0:T(8,128)(2,1)S(1)}, bf16[2,256,512]{2,1,0:T(8,128)(2,1)S(1)}, u32[]{:S(2)}, u32[]{:S(2)}) collective-permute-start(bf16[2,256,512]{2,1,0:T(8,128)(2,1)S(1)} %collective-permute-done.8.refs_2_), channel_id=1, source_target_pairs={{0,8},{8,0},{1,9},{9,1},{2,10},{10,2},{3,11},{11,3},{4,12},{12,4},... | collective-permute-start | bytes 1572872 | tf_op jit(solution)/shard_map/ppermute | solution.py:248
  39.3 1.9 %collective-permute-start.7 = (bf16[2,256,512]{2,1,0:T(8,128)(2,1)S(1)}, bf16[2,256,512]{2,1,0:T(8,128)(2,1)S(1)}, u32[]{:S(2)}, u32[]{:S(2)}) collective-permute-start(bf16[2,256,512]{2,1,0:T(8,128)(2,1)S(1)} %collective-permute-done.6.refs_0_), channel_id=1, source_target_pairs={{0,8},{8,0},{1,9},{9,1},{2,10},{10,2},{3,11},{11,3},{4,12},{12,4},... | collective-permute-start | bytes 1572872 | tf_op jit(solution)/shard_map/ppermute | solution.py:248
  41.2 3.4 %collective-permute-start.5 = (bf16[2,256,512]{2,1,0:T(8,128)(2,1)S(1)}, bf16[2,256,512]{2,1,0:T(8,128)(2,1)S(1)}, u32[]{:S(2)}, u32[]{:S(2)}) collective-permute-start(bf16[2,256,512]{2,1,0:T(8,128)(2,1)S(1)} %collective-permute-done.4.refs_4_), channel_id=1, source_target_pairs={{0,8},{8,0},{1,9},{9,1},{2,10},{10,2},{3,11},{11,3},{4,12},{12,4},... | collective-permute-start | bytes 1572872 | tf_op jit(solution)/shard_map/ppermute | solution.py:248
  44.8 1.4 collective-permute-done.5.refs_5_
  46.2 3.6 %collective-permute-start.12 = (bf16[2,256,512]{2,1,0:T(8,128)(2,1)S(1)}, bf16[2,256,512]{2,1,0:T(8,128)(2,1)S(1)}, u32[]{:S(2)}, u32[]{:S(2)}) collective-permute-start(bf16[2,256,512]{2,1,0:T(8,128)(2,1)S(1)} %collective-permute-done.10.refs_4_), channel_id=1, source_target_pairs={{0,8},{8,0},{1,9},{9,1},{2,10},{10,2},{3,11},{11,3},{4,12},{12,4},... | collective-permute-start | bytes 1572872 | tf_op jit(solution)/shard_map/ppermute | solution.py:248
  50.7 2.6 %enc_forward.1 = (bf16[32,512]{1,0:T(8,128)(2,1)S(1)}, bf16[4,32,512]{2,1,0:T(8,128)(2,1)S(1)}, f32[4,32,512]{2,1,0:T(8,128)S(1)}, f32[4,32,512]{2,1,0:T(8,128)S...) custom-call(s32[4]{0:T(128)S(1)} %pad_add_fusion.place, ...), custom_call_target="tpu_custom_call", output_to_operand_aliasing={{5}: (8, {})} | custom-call | tf_op jit(solution)/shard_map/enc_forward/pallas_call | solution.py:218
  53.4 2.9 %collective-permute-start.11 = (bf16[32,512]{1,0:T(8,128)(2,1)S(1)}, bf16[32,512]{1,0:T(8,128)(2,1)S(1)}, u32[]{:S(2)}, u32[]{:S(2)}) collective-permute-start(bf16[32,512]{1,0:T(8,128)(2,1)S(1)} %get-tuple-element.45), channel_id=1, source_target_pairs={{0,6},{2,4},{1,7},{3,5},{8,14},{10,12},{9,15},{11,13},{16,22},{18,... | collective-permute-start | bytes 98312 | tf_op jit(solution)/shard_map/ppermute | solution.py:267
  58.3 1.3 collective-permute-start.13
  59.6 7.6 %collective-permute-done.13.arrived = bf16[32,512]{1,0:T(8,128)(2,1)S(1)} collective-permute-done((bf16[32,512]{1,0:T(8,128)(2,1)S(1)}, bf16[32,512]{1,0:T(8,128)(2,1)S(1)}, u32[]{:S(2)}, u32[]{:S(2)}) %collective-permute-start.13) | collective-permute-done | bytes 32800 | tf_op jit(solution)/shard_map/ppermute | solution.py:274
  67.2 3.9 %turn_dec.1 = (bf16[32,512]{1,0:T(8,128)(2,1)S(1)}, bf16[4,32,512]{2,1,0:T(8,128)(2,1)S(1)}, bf16[4,2,4,32,512]{4,3,2,1,0:T(8,128)(2,1)S(1)}) custom-call(s32[4]{0:T(128)S(1)} %pad_add_fusion.place, bf16[32,512]{1,0:T(8,128)(2,1)S(1)} %collective-permute-done.13.arrived, bf16[4,32,512]{2,1,0:T(8,128)(2,1)S(1)} %get-tuple-element.54.e, ...), custom_call_target="tpu_custom_call" | custom-call | tf_op jit(solution)/shard_map/turn_dec/pallas_call | solution.py:218
  75.3 8.1 %collective-permute-done.15.arrived = bf16[32,512]{1,0:T(8,128)(2,1)S(1)} collective-permute-done((bf16[32,512]{1,0:T(8,128)(2,1)S(1)}, bf16[32,512]{1,0:T(8,128)(2,1)S(1)}, u32[]{:S(2)}, u32[]{:S(2)}) %collective-permute-start.15) | collective-permute-done | bytes 32800 | tf_op jit(solution)/shard_map/ppermute | solution.py:284
  83.3 2.2 %enc_backward.1 = bf16[4,2,4,32,512]{4,3,2,1,0:T(8,128)(2,1)S(1)} custom-call(s32[4]{0:T(128)S(1)} %pad_add_fusion.place, bf16[32,512]{1,0:T(8,128)(2,1)S(1)} %collective-permute-done.15.arrived, f32[4,32,512]{2,1,0:T(8,128)S(1)} %get-tuple-element.65.q, f32[4,32,512]{2,1,0:T(8,128)S(1)} %get-tuple-element.66.z, ...), custom_call_target="tpu_custom_call", output_to_operand_aliasing={{}: (7, {})} | custom-call | tf_op jit(solution)/shard_map/enc_backward/pallas_call | solution.py:218
  85.6 23.1 %all_to_all.15.acts = bf16[16,2,32,512]{3,2,1,0:T(8,128)(2,1)S(1)} all-to-all(bf16[16,2,32,512]{3,2,1,0:T(8,128)(2,1)S(1)} %bitcast.10), channel_id=1, replica_groups=mesh['x_lo'=2,'z_hi'=4,'z_lo'=4,'core'=2,'stage'=2,'y_lo'=2,'x_hi'=2] {'..., dimensions={0} | all-to-all | bytes 2097152 | tf_op jit(solution)/shard_map/all_to_all | solution.py:290
  109.2 20.7 %all_to_all.16 = bf16[16,4,8,512]{3,2,1,0:T(8,128)(2,1)S(1)} all-to-all(bf16[16,4,8,512]{3,2,1,0:T(8,128)(2,1)S(1)} %bitcast.11), channel_id=1, replica_groups=mesh['x_lo'=2,'z_hi'=4,'z_lo'=4,'core'=2,'stage'=2,'y_lo'=2,'x_hi'=2] {'..., dimensions={0} | all-to-all | bytes 1048576 | tf_op jit(solution)/shard_map/all_to_all | solution.py:295
  129.9 26.9 %all_to_all.17.parts = bf16[4,4,8,512]{3,2,1,0:T(8,128)(2,1)S(1)} all-to-all(bf16[4,4,8,512]{3,2,1,0:T(8,128)(2,1)S(1)} %bitcast.13), channel_id=1, replica_groups=mesh['x_lo'=2,'z_hi'=4,'z_lo'=4,'core'=2,'stage'=2,'y_lo'=2,'x_hi'=2] {'..., dimensions={0} | all-to-all | bytes 262144 | tf_op jit(solution)/shard_map/all_to_all | solution.py:297
  (30 shorter events, 11.7 us)
Async XLA Ops:
  0.7 1.2 copy-start
  2.0 1.2 copy-start.1
  4.0 14.7 %collective-permute-start.2 = (bf16[2,256,512]{2,1,0:T(8,128)(2,1)S(1)}, bf16[2,256,512]{2,1,0:T(8,128)(2,1)S(1)}, u32[]{:S(2)}, u32[]{:S(2)}) collective-permute-start(bf16[2,256,512]{2,1,0:T(8,128)(2,1)S(1)} %get-tuple-element.36), channel_id=1, source_target_pairs={{0,2},{2,0},{1,3},{3,1},{4,6},{6,4},{5,7},{7,5},{8,10},{10,8},{9,1... | collective-permute-start | bytes 1572872 | tf_op jit(solution)/shard_map/ppermute | solution.py:245
  7.3 16.1 %collective-permute-start = (bf16[2,256,512]{2,1,0:T(8,128)(2,1)S(1)}, bf16[2,256,512]{2,1,0:T(8,128)(2,1)S(1)}, u32[]{:S(2)}, u32[]{:S(2)}) collective-permute-start(bf16[2,256,512]{2,1,0:T(8,128)(2,1)S(1)} %get-tuple-element.36), channel_id=1, source_target_pairs={{0,257},{1,256},{256,1},{257,0},{2,259},{3,258},{258,3},{259,2},{4... | collective-permute-start | bytes 1572872 | tf_op jit(solution)/shard_map/ppermute | solution.py:242
  11.6 18.8 %collective-permute-start.8 = (bf16[2,256,512]{2,1,0:T(8,128)(2,1)S(1)}, bf16[2,256,512]{2,1,0:T(8,128)(2,1)S(1)}, u32[]{:S(2)}, u32[]{:S(2)}) collective-permute-start(bf16[2,256,512]{2,1,0:T(8,128)(2,1)S(1)} %get-tuple-element.37), channel_id=1, source_target_pairs={{0,2},{2,0},{1,3},{3,1},{4,6},{6,4},{5,7},{7,5},{8,10},{10,8},{9,1... | collective-permute-start | bytes 1572872 | tf_op jit(solution)/shard_map/ppermute | solution.py:245
  13.7 21.1 %collective-permute-start.6 = (bf16[2,256,512]{2,1,0:T(8,128)(2,1)S(1)}, bf16[2,256,512]{2,1,0:T(8,128)(2,1)S(1)}, u32[]{:S(2)}, u32[]{:S(2)}) collective-permute-start(bf16[2,256,512]{2,1,0:T(8,128)(2,1)S(1)} %get-tuple-element.37), channel_id=1, source_target_pairs={{0,257},{1,256},{256,1},{257,0},{2,259},{3,258},{258,3},{259,2},{4... | collective-permute-start | bytes 1572872 | tf_op jit(solution)/shard_map/ppermute | solution.py:242
  18.7 20.5 %collective-permute-start.3 = (bf16[2,256,512]{2,1,0:T(8,128)(2,1)S(1)}, bf16[2,256,512]{2,1,0:T(8,128)(2,1)S(1)}, u32[]{:S(2)}, u32[]{:S(2)}) collective-permute-start(bf16[2,256,512]{2,1,0:T(8,128)(2,1)S(1)} %collective-permute-done.2.refs_2_), channel_id=1, source_target_pairs={{0,8},{8,0},{1,9},{9,1},{2,10},{10,2},{3,11},{11,3},{4,12},{12,4},... | collective-permute-start | bytes 1572872 | tf_op jit(solution)/shard_map/ppermute | solution.py:248
  23.3 17.9 %collective-permute-start.4 = (bf16[2,256,512]{2,1,0:T(8,128)(2,1)S(1)}, bf16[2,256,512]{2,1,0:T(8,128)(2,1)S(1)}, u32[]{:S(2)}, u32[]{:S(2)}) collective-permute-start(bf16[2,256,512]{2,1,0:T(8,128)(2,1)S(1)} %collective-permute-done.refs_0_), channel_id=1, source_target_pairs={{0,2},{2,0},{1,3},{3,1},{4,6},{6,4},{5,7},{7,5},{8,10},{10,8},{9,1... | collective-permute-start | bytes 1572872 | tf_op jit(solution)/shard_map/ppermute | solution.py:245
  26.5 18.1 %collective-permute-start.1 = (bf16[2,256,512]{2,1,0:T(8,128)(2,1)S(1)}, bf16[2,256,512]{2,1,0:T(8,128)(2,1)S(1)}, u32[]{:S(2)}, u32[]{:S(2)}) collective-permute-start(bf16[2,256,512]{2,1,0:T(8,128)(2,1)S(1)} %collective-permute-done.refs_0_), channel_id=1, source_target_pairs={{0,8},{8,0},{1,9},{9,1},{2,10},{10,2},{3,11},{11,3},{4,12},{12,4},... | collective-permute-start | bytes 1572872 | tf_op jit(solution)/shard_map/ppermute | solution.py:248
  30.4 14.3 %collective-permute-start.10 = (bf16[2,256,512]{2,1,0:T(8,128)(2,1)S(1)}, bf16[2,256,512]{2,1,0:T(8,128)(2,1)S(1)}, u32[]{:S(2)}, u32[]{:S(2)}) collective-permute-start(bf16[2,256,512]{2,1,0:T(8,128)(2,1)S(1)} %collective-permute-done.8.refs_2_), channel_id=1, source_target_pairs={{0,257},{1,256},{256,1},{257,0},{2,259},{3,258},{258,3},{259,2},{4... | collective-permute-start | bytes 1572872 | tf_op jit(solution)/shard_map/ppermute | solution.py:242
  34.8 9.9 %collective-permute-start.9 = (bf16[2,256,512]{2,1,0:T(8,128)(2,1)S(1)}, bf16[2,256,512]{2,1,0:T(8,128)(2,1)S(1)}, u32[]{:S(2)}, u32[]{:S(2)}) collective-permute-start(bf16[2,256,512]{2,1,0:T(8,128)(2,1)S(1)} %collective-permute-done.8.refs_2_), channel_id=1, source_target_pairs={{0,8},{8,0},{1,9},{9,1},{2,10},{10,2},{3,11},{11,3},{4,12},{12,4},... | collective-permute-start | bytes 1572872 | tf_op jit(solution)/shard_map/ppermute | solution.py:248
  39.3 5.5 %collective-permute-start.7 = (bf16[2,256,512]{2,1,0:T(8,128)(2,1)S(1)}, bf16[2,256,512]{2,1,0:T(8,128)(2,1)S(1)}, u32[]{:S(2)}, u32[]{:S(2)}) collective-permute-start(bf16[2,256,512]{2,1,0:T(8,128)(2,1)S(1)} %collective-permute-done.6.refs_0_), channel_id=1, source_target_pairs={{0,8},{8,0},{1,9},{9,1},{2,10},{10,2},{3,11},{11,3},{4,12},{12,4},... | collective-permute-start | bytes 1572872 | tf_op jit(solution)/shard_map/ppermute | solution.py:248
  41.2 5.0 %collective-permute-start.5 = (bf16[2,256,512]{2,1,0:T(8,128)(2,1)S(1)}, bf16[2,256,512]{2,1,0:T(8,128)(2,1)S(1)}, u32[]{:S(2)}, u32[]{:S(2)}) collective-permute-start(bf16[2,256,512]{2,1,0:T(8,128)(2,1)S(1)} %collective-permute-done.4.refs_4_), channel_id=1, source_target_pairs={{0,8},{8,0},{1,9},{9,1},{2,10},{10,2},{3,11},{11,3},{4,12},{12,4},... | collective-permute-start | bytes 1572872 | tf_op jit(solution)/shard_map/ppermute | solution.py:248
  46.2 11.2 %collective-permute-start.12 = (bf16[2,256,512]{2,1,0:T(8,128)(2,1)S(1)}, bf16[2,256,512]{2,1,0:T(8,128)(2,1)S(1)}, u32[]{:S(2)}, u32[]{:S(2)}) collective-permute-start(bf16[2,256,512]{2,1,0:T(8,128)(2,1)S(1)} %collective-permute-done.10.refs_4_), channel_id=1, source_target_pairs={{0,8},{8,0},{1,9},{9,1},{2,10},{10,2},{3,11},{11,3},{4,12},{12,4},... | collective-permute-start | bytes 1572872 | tf_op jit(solution)/shard_map/ppermute | solution.py:248
  49.8 0.9 copy-start.2
  53.4 3.9 %collective-permute-start.11 = (bf16[32,512]{1,0:T(8,128)(2,1)S(1)}, bf16[32,512]{1,0:T(8,128)(2,1)S(1)}, u32[]{:S(2)}, u32[]{:S(2)}) collective-permute-start(bf16[32,512]{1,0:T(8,128)(2,1)S(1)} %get-tuple-element.45), channel_id=1, source_target_pairs={{0,6},{2,4},{1,7},{3,5},{8,14},{10,12},{9,15},{11,13},{16,22},{18,... | collective-permute-start | bytes 98312 | tf_op jit(solution)/shard_map/ppermute | solution.py:267
  57.3 9.9 %copy-start.3 = (bf16[4,32,512]{2,1,0:T(8,128)(2,1)S(1)}, bf16[4,32,512]{2,1,0:T(8,128)(2,1)}, u32[]{:S(2)}) copy-start(bf16[4,32,512]{2,1,0:T(8,128)(2,1)} %cotangent.1) | copy-start | bytes 393220
  58.3 8.9 %collective-permute-start.13 = (bf16[32,512]{1,0:T(8,128)(2,1)S(1)}, bf16[32,512]{1,0:T(8,128)(2,1)S(1)}, u32[]{:S(2)}, u32[]{:S(2)}) collective-permute-start(bf16[32,512]{1,0:T(8,128)(2,1)S(1)} %get-tuple-element.53), channel_id=1, source_target_pairs={{6,0},{4,2},{7,1},{5,3},{14,8},{12,10},{15,9},{13,11},{22,16},{20,... | collective-permute-start | bytes 98312 | tf_op jit(solution)/shard_map/ppermute | solution.py:274
  71.1 2.3 %collective-permute-start.14 = (bf16[32,512]{1,0:T(8,128)(2,1)S(1)}, bf16[32,512]{1,0:T(8,128)(2,1)S(1)}, u32[]{:S(2)}, u32[]{:S(2)}) collective-permute-start(bf16[32,512]{1,0:T(8,128)(2,1)S(1)} %get-tuple-element.56), channel_id=1, source_target_pairs={{0,6},{2,4},{1,7},{3,5},{8,14},{10,12},{9,15},{11,13},{16,22},{18,... | collective-permute-start | bytes 98312 | tf_op jit(solution)/shard_map/ppermute | solution.py:279
  74.0 9.4 %collective-permute-start.15 = (bf16[32,512]{1,0:T(8,128)(2,1)S(1)}, bf16[32,512]{1,0:T(8,128)(2,1)S(1)}, u32[]{:S(2)}, u32[]{:S(2)}) collective-permute-start(bf16[32,512]{1,0:T(8,128)(2,1)S(1)} %get-tuple-element.64), channel_id=1, source_target_pairs={{6,0},{4,2},{7,1},{5,3},{14,8},{12,10},{15,9},{13,11},{22,16},{20,... | collective-permute-start | bytes 98312 | tf_op jit(solution)/shard_map/ppermute | solution.py:284

commit v5 on v4

--- a/solution.py
+++ b/solution.py
@@ -31,27 +31,26 @@
 
 
 def forward_level(v, weight, save, slot):
-    save_q, save_z, save_r = save
+    save_q, save_f, save_h, save_r = save
     r = lax.rsqrt(jnp.mean(v * v, axis=-1, keepdims=True) + EPS)
     q = v * r
     z = dot(q.astype(BF16), weight[0])
-    h = (z * jax.nn.sigmoid(z)).astype(BF16)
+    s = jax.nn.sigmoid(z)
+    h = (z * s).astype(BF16)
     save_q[slot] = q
-    save_z[slot] = z
+    save_f[slot] = s * (1.0 + z * (1.0 - s))
+    save_h[slot] = h
     save_r[slot] = jnp.broadcast_to(r, (ROWS, 128))
     return (v + dot(h, weight[1])).astype(BF16)
 
 
 def backward_level(g, weight, save, slot, acts, side, first=False):
-    save_q, save_z, save_r = save
-    gh = dot_t(g, weight[1])
-    z = save_z[slot]
-    s = jax.nn.sigmoid(z)
-    gz = (gh * s * (1.0 + z * (1.0 - s))).astype(BF16)
+    save_q, save_f, save_h, save_r = save
+    gz = (dot_t(g, weight[1]) * save_f[slot]).astype(BF16)
     q = save_q[slot]
     acts[slot, side, 0] = q.astype(BF16)
     acts[slot, side, 1] = gz
-    acts[slot, side, 2] = (z * s).astype(BF16)
+    acts[slot, side, 2] = save_h[slot]
     acts[slot, side, 3] = g
     if first:
         return None
@@ -97,14 +96,14 @@
 
 
 def enc_forward_kernel(place, pixels, *refs):
-    pieces, (_, hop, e, q, z, r, held, sems) = refs[:N_PIECES], refs[N_PIECES:]
+    pieces, (_, hop, e, q, f, h, r, held, sems) = refs[:N_PIECES], refs[N_PIECES:]
     start_weights(place, pieces, held, sems, UP)
 
     @pl.when(place[0] == 0)
     def _():
         x = pixels[place[1]]
         for m in UP:
-            x = forward_level(x.astype(F32), wait_weights(place, held, sems, m), (q, z, r), m)
+            x = forward_level(x.astype(F32), wait_weights(place, held, sems, m), (q, f, h, r), m)
             e[m] = x
         hop[...] = x
 
@@ -115,7 +114,7 @@
 
 
 def turn_forward_kernel(place, arrived, weights_e, *refs):
-    pieces, (_, hop, qe, ze, re, qd, zd, rd, held, sems) = refs[:N_PIECES], refs[N_PIECES:]
+    pieces, (_, hop, qe, fe, he, re, qd, fd, hd, rd, held, sems) = refs[:N_PIECES], refs[N_PIECES:]
     start_weights(place, pieces, held, sems, DOWN)
 
     @pl.when(place[0] == 1)
@@ -123,11 +122,11 @@
         x = arrived[...]
         skips = []
         for m in UP:
-            x = forward_level(x.astype(F32), weights_e.at[m], (qe, ze, re), m)
+            x = forward_level(x.astype(F32), weights_e.at[m], (qe, fe, he, re), m)
             skips.append(x)
         for m in DOWN:
             v = x.astype(F32) + skips[m].astype(F32)
-            x = forward_level(v, wait_weights(place, held, sems, m), (qd, zd, rd), m)
+            x = forward_level(v, wait_weights(place, held, sems, m), (qd, fd, hd, rd), m)
         hop[...] = x
 
     @pl.when(place[0] != 1)
@@ -136,16 +135,16 @@
             wait_weights(place, held, sems, m)
 
 
-def turn_dec_kernel(place, arrived, e, cotangent, weights, hop, skip_grads, acts, q, z, r):
+def turn_dec_kernel(place, arrived, e, cotangent, weights, hop, skip_grads, acts, q, f, h, r):
     @pl.when(place[0] == 0)
     def _():
         x = arrived[...]
         for m in DOWN:
             v = x.astype(F32) + e[m].astype(F32)
-            x = forward_level(v, weights.at[m], (q, z, r), m)
+            x = forward_level(v, weights.at[m], (q, f, h, r), m)
         g = cotangent[place[1]]
         for m in UP:
-            g = backward_level(g, weights.at[m], (q, z, r), m, acts, 1)
+            g = backward_level(g, weights.at[m], (q, f, h, r), m, acts, 1)
             skip_grads[m] = g
         hop[...] = g
 
@@ -157,7 +156,7 @@
     return g
 
 
-def turn_backward_kernel(place, arrived, qe, ze, re, qd, zd, rd, weights_e, weights_d, acts_in, hop, acts):
+def turn_backward_kernel(place, arrived, qe, fe, he, re, qd, fd, hd, rd, weights_e, weights_d, acts_in, hop, acts):
     del acts_in
 
     @pl.when(place[0] == 1)
@@ -165,17 +164,17 @@
         g = arrived[...]
         skip_grads = []
         for m in UP:
-            g = backward_level(g, weights_d.at[m], (qd, zd, rd), m, acts, 1)
+            g = backward_level(g, weights_d.at[m], (qd, fd, hd, rd), m, acts, 1)
             skip_grads.append(g)
-        hop[...] = enc_backward(g, skip_grads, weights_e, (qe, ze, re), acts)
-
-
-def enc_backward_kernel(place, arrived, q, z, r, skip_grads, weights, acts_in, acts):
+        hop[...] = enc_backward(g, skip_grads, weights_e, (qe, fe, he, re), acts)
+
+
+def enc_backward_kernel(place, arrived, q, f, h, r, skip_grads, weights, acts_in, acts):
     del acts_in
 
     @pl.when(place[0] == 0)
     def _():
-        enc_backward(arrived[...], skip_grads, weights, (q, z, r), acts, first=True)
+        enc_backward(arrived[...], skip_grads, weights, (q, f, h, r), acts, first=True)
 
 
 def grads_kernel(acts, out):
@@ -205,7 +204,7 @@
 STACK = jax.ShapeDtypeStruct((LEVELS, ROWS, WIDTH), BF16)
 SAVE = jax.ShapeDtypeStruct((LEVELS, ROWS, WIDTH), F32)
 SAVE_R = jax.ShapeDtypeStruct((LEVELS, ROWS, 128), F32)
-SAVES = (SAVE, SAVE, SAVE_R)
+SAVES = (SAVE, SAVE, STACK, SAVE_R)
 ACTS = jax.ShapeDtypeStruct((LEVELS, 2, 4, ROWS, WIDTH), BF16)
 
 WEIGHTS = jax.ShapeDtypeStruct((LEVELS, 2, WIDTH, WIDTH), BF16)
@@ -262,14 +261,14 @@
 
     hop, e, *saves_0, weights_e = call(
         enc_forward_kernel, (place, pixels, *pieces[:6], own_e), (SMEM, VMEM) + (ANY,) * N_PIECES + (VMEM,),
-        (ROW, STACK) + SAVES + (WEIGHTS,), (VMEM,) * 6, (SEMS,), {2 + N_PIECES: 5}, name="enc_forward",
+        (ROW, STACK) + SAVES + (WEIGHTS,), (VMEM,) * 7, (SEMS,), {2 + N_PIECES: 6}, name="enc_forward",
     )
     arrived = lax.ppermute(hop, y, up)
     pieces = (*pieces[6:], diagonal_d, swap(diagonal_d))
     hop, *saves, weights_d = call(
         turn_forward_kernel, (place, arrived, weights_e, *pieces, own_d),
         (SMEM, VMEM, VMEM) + (ANY,) * N_PIECES + (VMEM,),
-        (ROW,) + SAVES + SAVES + (WEIGHTS,), (VMEM,) * 8, (SEMS,), {3 + N_PIECES: 7}, name="turn_forward",
+        (ROW,) + SAVES + SAVES + (WEIGHTS,), (VMEM,) * 10, (SEMS,), {3 + N_PIECES: 9}, name="turn_forward",
     )
     arrived = lax.ppermute(hop, y, down)
     hop, skip_grads, acts = call(
@@ -278,13 +277,13 @@
     )
     arrived = lax.ppermute(hop, y, up)
     hop, acts = call(
-        turn_backward_kernel, (place, arrived, *saves, weights_e, weights_d, acts), (SMEM,) + (VMEM,) * 10,
-        (ROW, ACTS), (VMEM,) * 2, (), {10: 1}, name="turn_backward",
+        turn_backward_kernel, (place, arrived, *saves, weights_e, weights_d, acts), (SMEM,) + (VMEM,) * 12,
+        (ROW, ACTS), (VMEM,) * 2, (), {12: 1}, name="turn_backward",
     )
     arrived = lax.ppermute(hop, y, down)
     acts = call(
-        enc_backward_kernel, (place, arrived, *saves_0, skip_grads, weights_e, acts), (SMEM,) + (VMEM,) * 7,
-        ACTS, VMEM, (), {7: 0}, name="enc_backward",
+        enc_backward_kernel, (place, arrived, *saves_0, skip_grads, weights_e, acts), (SMEM,) + (VMEM,) * 8,
+        ACTS, VMEM, (), {8: 0}, name="enc_backward",
     )
 
     acts = lax.all_to_all(acts.reshape(16, 2, ROWS, WIDTH), MEMBERS + ("x_lo", "core"), 0, 0)

time: 158 us -> 158 us (level)
  no operation moved by 1% of the time
where the time goes in v5:
time: 158 us
  blocking collectives  70.7 us (45%)
  starting transfers between devices  48 us (30%)
  waiting for transfers between devices  22.2 us (14%)
  Pallas kernels  12.2 us (8%)
  local copies, waits for them, and re-layouts  3.36 us (2%)
    all_to_all x1, blocking collectives, local(): total = lax.all_to_all(total.transpose(1, 0, 2, 3), 'z_hi', 0, 0)  26.9 us
    all_to_all x1, blocking collectives, local(): lax.all_to_all(acts.reshape(16, 2, ROWS, WIDTH), MEMBERS + ('x_lo', 'core...  23.1 us
    ppermute x6, starting transfers between devices, swap(): return lax.ppermute(block, 'core', [(0, 1), (1, 0)])  21.9 us
    all_to_all x1, blocking collectives, local(): lax.all_to_all(grad.reshape(16, 4, 8, WIDTH), ('z_lo', 'x_lo', 'core'), 0...  20.7 us
    ppermute x2, waiting for transfers between devices, local(): arrived = lax.ppermute(hop, y, down)  15.7 us
    pallas_call x8, Pallas kernels, call(): pl.pallas_call(kernel, out_shape=outs, in_specs=spaces, out_specs=out_spa...  12.2 us
    ppermute x3, starting transfers between devices, along_x(): return lax.ppermute(block, ('x_lo', 'x_hi'), [(i, 3 - i) for i in range(4)])  10.9 us
    ppermute x3, starting transfers between devices, along_y(): return lax.ppermute(block, 'y_lo', [(0, 1), (1, 0)])  8.49 us
  transfers between devices with their start and end apart: 16, of which 7 were waited for; matrix products, arithmetic and copies ran while one was open for 0% of the time, Pallas kernels for 2%

profile of v5, /device:TPU:33, one launch (start us, length us, event | category | flops | bytes accessed | tf_op | source)
XLA Modules:
  0.0 157.6 jit_solution(14329271264240410801)
XLA Ops:
  4.0 3.2 %collective-permute-start.2 = (bf16[2,256,512]{2,1,0:T(8,128)(2,1)S(1)}, bf16[2,256,512]{2,1,0:T(8,128)(2,1)S(1)}, u32[]{:S(2)}, u32[]{:S(2)}) collective-permute-start(bf16[2,256,512]{2,1,0:T(8,128)(2,1)S(1)} %get-tuple-element.39), channel_id=1, source_target_pairs={{0,2},{2,0},{1,3},{3,1},{4,6},{6,4},{5,7},{7,5},{8,10},{10,8},{9,1... | collective-permute-start | bytes 1572872 | tf_op jit(solution)/shard_map/ppermute | solution.py:244
  7.3 4.4 %collective-permute-start = (bf16[2,256,512]{2,1,0:T(8,128)(2,1)S(1)}, bf16[2,256,512]{2,1,0:T(8,128)(2,1)S(1)}, u32[]{:S(2)}, u32[]{:S(2)}) collective-permute-start(bf16[2,256,512]{2,1,0:T(8,128)(2,1)S(1)} %get-tuple-element.39), channel_id=1, source_target_pairs={{0,257},{1,256},{256,1},{257,0},{2,259},{3,258},{258,3},{259,2},{4... | collective-permute-start | bytes 1572872 | tf_op jit(solution)/shard_map/ppermute | solution.py:241
  11.6 2.1 %collective-permute-start.8 = (bf16[2,256,512]{2,1,0:T(8,128)(2,1)S(1)}, bf16[2,256,512]{2,1,0:T(8,128)(2,1)S(1)}, u32[]{:S(2)}, u32[]{:S(2)}) collective-permute-start(bf16[2,256,512]{2,1,0:T(8,128)(2,1)S(1)} %get-tuple-element.40), channel_id=1, source_target_pairs={{0,2},{2,0},{1,3},{3,1},{4,6},{6,4},{5,7},{7,5},{8,10},{10,8},{9,1... | collective-permute-start | bytes 1572872 | tf_op jit(solution)/shard_map/ppermute | solution.py:244
  13.7 2.1 %collective-permute-start.6 = (bf16[2,256,512]{2,1,0:T(8,128)(2,1)S(1)}, bf16[2,256,512]{2,1,0:T(8,128)(2,1)S(1)}, u32[]{:S(2)}, u32[]{:S(2)}) collective-permute-start(bf16[2,256,512]{2,1,0:T(8,128)(2,1)S(1)} %get-tuple-element.40), channel_id=1, source_target_pairs={{0,257},{1,256},{256,1},{257,0},{2,259},{3,258},{258,3},{259,2},{4... | collective-permute-start | bytes 1572872 | tf_op jit(solution)/shard_map/ppermute | solution.py:241
  15.8 2.9 %collective-permute-done.2.refs_2_ = bf16[2,256,512]{2,1,0:T(8,128)(2,1)S(1)} collective-permute-done((bf16[2,256,512]{2,1,0:T(8,128)(2,1)S(1)}, bf16[2,256,512]{2,1,0:T(8,128)(2,1)S(1)}, u32[]{:S(2)}, u32[]{:S(2)}) %collective-permute-start.2) | collective-permute-done | bytes 524320 | tf_op jit(solution)/shard_map/ppermute | solution.py:244
  18.7 4.6 %collective-permute-start.3 = (bf16[2,256,512]{2,1,0:T(8,128)(2,1)S(1)}, bf16[2,256,512]{2,1,0:T(8,128)(2,1)S(1)}, u32[]{:S(2)}, u32[]{:S(2)}) collective-permute-start(bf16[2,256,512]{2,1,0:T(8,128)(2,1)S(1)} %collective-permute-done.2.refs_2_), channel_id=1, source_target_pairs={{0,8},{8,0},{1,9},{9,1},{2,10},{10,2},{3,11},{11,3},{4,12},{12,4},... | collective-permute-start | bytes 1572872 | tf_op jit(solution)/shard_map/ppermute | solution.py:247
  23.3 3.2 %collective-permute-start.4 = (bf16[2,256,512]{2,1,0:T(8,128)(2,1)S(1)}, bf16[2,256,512]{2,1,0:T(8,128)(2,1)S(1)}, u32[]{:S(2)}, u32[]{:S(2)}) collective-permute-start(bf16[2,256,512]{2,1,0:T(8,128)(2,1)S(1)} %collective-permute-done.refs_0_), channel_id=1, source_target_pairs={{0,2},{2,0},{1,3},{3,1},{4,6},{6,4},{5,7},{7,5},{8,10},{10,8},{9,1... | collective-permute-start | bytes 1572872 | tf_op jit(solution)/shard_map/ppermute | solution.py:244
  26.5 3.9 %collective-permute-start.1 = (bf16[2,256,512]{2,1,0:T(8,128)(2,1)S(1)}, bf16[2,256,512]{2,1,0:T(8,128)(2,1)S(1)}, u32[]{:S(2)}, u32[]{:S(2)}) collective-permute-start(bf16[2,256,512]{2,1,0:T(8,128)(2,1)S(1)} %collective-permute-done.refs_0_), channel_id=1, source_target_pairs={{0,8},{8,0},{1,9},{9,1},{2,10},{10,2},{3,11},{11,3},{4,12},{12,4},... | collective-permute-start | bytes 1572872 | tf_op jit(solution)/shard_map/ppermute | solution.py:247
  30.4 4.4 %collective-permute-start.10 = (bf16[2,256,512]{2,1,0:T(8,128)(2,1)S(1)}, bf16[2,256,512]{2,1,0:T(8,128)(2,1)S(1)}, u32[]{:S(2)}, u32[]{:S(2)}) collective-permute-start(bf16[2,256,512]{2,1,0:T(8,128)(2,1)S(1)} %collective-permute-done.8.refs_2_), channel_id=1, source_target_pairs={{0,257},{1,256},{256,1},{257,0},{2,259},{3,258},{258,3},{259,2},{4... | collective-permute-start | bytes 1572872 | tf_op jit(solution)/shard_map/ppermute | solution.py:241
  34.8 4.4 %collective-permute-start.9 = (bf16[2,256,512]{2,1,0:T(8,128)(2,1)S(1)}, bf16[2,256,512]{2,1,0:T(8,128)(2,1)S(1)}, u32[]{:S(2)}, u32[]{:S(2)}) collective-permute-start(bf16[2,256,512]{2,1,0:T(8,128)(2,1)S(1)} %collective-permute-done.8.refs_2_), channel_id=1, source_target_pairs={{0,8},{8,0},{1,9},{9,1},{2,10},{10,2},{3,11},{11,3},{4,12},{12,4},... | collective-permute-start | bytes 1572872 | tf_op jit(solution)/shard_map/ppermute | solution.py:247
  39.3 1.9 %collective-permute-start.7 = (bf16[2,256,512]{2,1,0:T(8,128)(2,1)S(1)}, bf16[2,256,512]{2,1,0:T(8,128)(2,1)S(1)}, u32[]{:S(2)}, u32[]{:S(2)}) collective-permute-start(bf16[2,256,512]{2,1,0:T(8,128)(2,1)S(1)} %collective-permute-done.6.refs_0_), channel_id=1, source_target_pairs={{0,8},{8,0},{1,9},{9,1},{2,10},{10,2},{3,11},{11,3},{4,12},{12,4},... | collective-permute-start | bytes 1572872 | tf_op jit(solution)/shard_map/ppermute | solution.py:247
  41.2 3.4 %collective-permute-start.5 = (bf16[2,256,512]{2,1,0:T(8,128)(2,1)S(1)}, bf16[2,256,512]{2,1,0:T(8,128)(2,1)S(1)}, u32[]{:S(2)}, u32[]{:S(2)}) collective-permute-start(bf16[2,256,512]{2,1,0:T(8,128)(2,1)S(1)} %collective-permute-done.4.refs_4_), channel_id=1, source_target_pairs={{0,8},{8,0},{1,9},{9,1},{2,10},{10,2},{3,11},{11,3},{4,12},{12,4},... | collective-permute-start | bytes 1572872 | tf_op jit(solution)/shard_map/ppermute | solution.py:247
  44.8 1.4 collective-permute-done.5.refs_5_
  46.2 3.6 %collective-permute-start.12 = (bf16[2,256,512]{2,1,0:T(8,128)(2,1)S(1)}, bf16[2,256,512]{2,1,0:T(8,128)(2,1)S(1)}, u32[]{:S(2)}, u32[]{:S(2)}) collective-permute-start(bf16[2,256,512]{2,1,0:T(8,128)(2,1)S(1)} %collective-permute-done.10.refs_4_), channel_id=1, source_target_pairs={{0,8},{8,0},{1,9},{9,1},{2,10},{10,2},{3,11},{11,3},{4,12},{12,4},... | collective-permute-start | bytes 1572872 | tf_op jit(solution)/shard_map/ppermute | solution.py:247
  50.7 2.7 %enc_forward.1 = (bf16[32,512]{1,0:T(8,128)(2,1)S(1)}, bf16[4,32,512]{2,1,0:T(8,128)(2,1)S(1)}, f32[4,32,512]{2,1,0:T(8,128)S(1)}, f32[4,32,512]{2,1,0:T(8,128)S...) custom-call(s32[4]{0:T(128)S(1)} %pad_add_fusion.place, ...), custom_call_target="tpu_custom_call", output_to_operand_aliasing={{6}: (8, {})} | custom-call | tf_op jit(solution)/shard_map/enc_forward/pallas_call | solution.py:217
  53.4 2.9 %collective-permute-start.11 = (bf16[32,512]{1,0:T(8,128)(2,1)S(1)}, bf16[32,512]{1,0:T(8,128)(2,1)S(1)}, u32[]{:S(2)}, u32[]{:S(2)}) collective-permute-start(bf16[32,512]{1,0:T(8,128)(2,1)S(1)} %get-tuple-element.48), channel_id=1, source_target_pairs={{0,6},{2,4},{1,7},{3,5},{8,14},{10,12},{9,15},{11,13},{16,22},{18,... | collective-permute-start | bytes 98312 | tf_op jit(solution)/shard_map/ppermute | solution.py:266
  58.3 1.3 collective-permute-start.13
  59.6 7.7 %collective-permute-done.13.arrived = bf16[32,512]{1,0:T(8,128)(2,1)S(1)} collective-permute-done((bf16[32,512]{1,0:T(8,128)(2,1)S(1)}, bf16[32,512]{1,0:T(8,128)(2,1)S(1)}, u32[]{:S(2)}, u32[]{:S(2)}) %collective-permute-start.13) | collective-permute-done | bytes 32800 | tf_op jit(solution)/shard_map/ppermute | solution.py:273
  67.2 3.9 %turn_dec.1 = (bf16[32,512]{1,0:T(8,128)(2,1)S(1)}, bf16[4,32,512]{2,1,0:T(8,128)(2,1)S(1)}, bf16[4,2,4,32,512]{4,3,2,1,0:T(8,128)(2,1)S(1)}) custom-call(s32[4]{0:T(128)S(1)} %pad_add_fusion.place, bf16[32,512]{1,0:T(8,128)(2,1)S(1)} %collective-permute-done.13.arrived, bf16[4,32,512]{2,1,0:T(8,128)(2,1)S(1)} %get-tuple-element.57.e, ...), custom_call_target="tpu_custom_call" | custom-call | tf_op jit(solution)/shard_map/turn_dec/pallas_call | solution.py:217
  75.3 8.0 %collective-permute-done.15.arrived = bf16[32,512]{1,0:T(8,128)(2,1)S(1)} collective-permute-done((bf16[32,512]{1,0:T(8,128)(2,1)S(1)}, bf16[32,512]{1,0:T(8,128)(2,1)S(1)}, u32[]{:S(2)}, u32[]{:S(2)}) %collective-permute-start.15) | collective-permute-done | bytes 32800 | tf_op jit(solution)/shard_map/ppermute | solution.py:283
  83.4 2.2 %enc_backward.1 = bf16[4,2,4,32,512]{4,3,2,1,0:T(8,128)(2,1)S(1)} custom-call(s32[4]{0:T(128)S(1)} %pad_add_fusion.place, bf16[32,512]{1,0:T(8,128)(2,1)S(1)} %collective-permute-done.15.arrived, f32[4,32,512]{2,1,0:T(8,128)S(1)} %get-tuple-element.70.q, f32[4,32,512]{2,1,0:T(8,128)S(1)} %get-tuple-element.71.f, ...), custom_call_target="tpu_custom_call", output_to_operand_aliasing={{}: (8, {})} | custom-call | tf_op jit(solution)/shard_map/enc_backward/pallas_call | solution.py:217
  85.6 23.1 %all_to_all.15.acts = bf16[16,2,32,512]{3,2,1,0:T(8,128)(2,1)S(1)} all-to-all(bf16[16,2,32,512]{3,2,1,0:T(8,128)(2,1)S(1)} %bitcast.10), channel_id=1, replica_groups=mesh['x_lo'=2,'z_hi'=4,'z_lo'=4,'core'=2,'stage'=2,'y_lo'=2,'x_hi'=2] {'..., dimensions={0} | all-to-all | bytes 2097152 | tf_op jit(solution)/shard_map/all_to_all | solution.py:289
  109.2 20.7 %all_to_all.16 = bf16[16,4,8,512]{3,2,1,0:T(8,128)(2,1)S(1)} all-to-all(bf16[16,4,8,512]{3,2,1,0:T(8,128)(2,1)S(1)} %bitcast.11), channel_id=1, replica_groups=mesh['x_lo'=2,'z_hi'=4,'z_lo'=4,'core'=2,'stage'=2,'y_lo'=2,'x_hi'=2] {'..., dimensions={0} | all-to-all | bytes 1048576 | tf_op jit(solution)/shard_map/all_to_all | solution.py:294
  130.0 26.9 %all_to_all.17.parts = bf16[4,4,8,512]{3,2,1,0:T(8,128)(2,1)S(1)} all-to-all(bf16[4,4,8,512]{3,2,1,0:T(8,128)(2,1)S(1)} %bitcast.13), channel_id=1, replica_groups=mesh['x_lo'=2,'z_hi'=4,'z_lo'=4,'core'=2,'stage'=2,'y_lo'=2,'x_hi'=2] {'..., dimensions={0} | all-to-all | bytes 262144 | tf_op jit(solution)/shard_map/all_to_all | solution.py:296
  (30 shorter events, 11.7 us)
Async XLA Ops:
  0.7 1.2 copy-start
  2.0 1.2 copy-start.1
  4.0 14.7 %collective-permute-start.2 = (bf16[2,256,512]{2,1,0:T(8,128)(2,1)S(1)}, bf16[2,256,512]{2,1,0:T(8,128)(2,1)S(1)}, u32[]{:S(2)}, u32[]{:S(2)}) collective-permute-start(bf16[2,256,512]{2,1,0:T(8,128)(2,1)S(1)} %get-tuple-element.39), channel_id=1, source_target_pairs={{0,2},{2,0},{1,3},{3,1},{4,6},{6,4},{5,7},{7,5},{8,10},{10,8},{9,1... | collective-permute-start | bytes 1572872 | tf_op jit(solution)/shard_map/ppermute | solution.py:244
  7.3 16.1 %collective-permute-start = (bf16[2,256,512]{2,1,0:T(8,128)(2,1)S(1)}, bf16[2,256,512]{2,1,0:T(8,128)(2,1)S(1)}, u32[]{:S(2)}, u32[]{:S(2)}) collective-permute-start(bf16[2,256,512]{2,1,0:T(8,128)(2,1)S(1)} %get-tuple-element.39), channel_id=1, source_target_pairs={{0,257},{1,256},{256,1},{257,0},{2,259},{3,258},{258,3},{259,2},{4... | collective-permute-start | bytes 1572872 | tf_op jit(solution)/shard_map/ppermute | solution.py:241
  11.6 18.8 %collective-permute-start.8 = (bf16[2,256,512]{2,1,0:T(8,128)(2,1)S(1)}, bf16[2,256,512]{2,1,0:T(8,128)(2,1)S(1)}, u32[]{:S(2)}, u32[]{:S(2)}) collective-permute-start(bf16[2,256,512]{2,1,0:T(8,128)(2,1)S(1)} %get-tuple-element.40), channel_id=1, source_target_pairs={{0,2},{2,0},{1,3},{3,1},{4,6},{6,4},{5,7},{7,5},{8,10},{10,8},{9,1... | collective-permute-start | bytes 1572872 | tf_op jit(solution)/shard_map/ppermute | solution.py:244
  13.7 21.1 %collective-permute-start.6 = (bf16[2,256,512]{2,1,0:T(8,128)(2,1)S(1)}, bf16[2,256,512]{2,1,0:T(8,128)(2,1)S(1)}, u32[]{:S(2)}, u32[]{:S(2)}) collective-permute-start(bf16[2,256,512]{2,1,0:T(8,128)(2,1)S(1)} %get-tuple-element.40), channel_id=1, source_target_pairs={{0,257},{1,256},{256,1},{257,0},{2,259},{3,258},{258,3},{259,2},{4... | collective-permute-start | bytes 1572872 | tf_op jit(solution)/shard_map/ppermute | solution.py:241
  18.7 20.5 %collective-permute-start.3 = (bf16[2,256,512]{2,1,0:T(8,128)(2,1)S(1)}, bf16[2,256,512]{2,1,0:T(8,128)(2,1)S(1)}, u32[]{:S(2)}, u32[]{:S(2)}) collective-permute-start(bf16[2,256,512]{2,1,0:T(8,128)(2,1)S(1)} %collective-permute-done.2.refs_2_), channel_id=1, source_target_pairs={{0,8},{8,0},{1,9},{9,1},{2,10},{10,2},{3,11},{11,3},{4,12},{12,4},... | collective-permute-start | bytes 1572872 | tf_op jit(solution)/shard_map/ppermute | solution.py:247
  23.3 17.9 %collective-permute-start.4 = (bf16[2,256,512]{2,1,0:T(8,128)(2,1)S(1)}, bf16[2,256,512]{2,1,0:T(8,128)(2,1)S(1)}, u32[]{:S(2)}, u32[]{:S(2)}) collective-permute-start(bf16[2,256,512]{2,1,0:T(8,128)(2,1)S(1)} %collective-permute-done.refs_0_), channel_id=1, source_target_pairs={{0,2},{2,0},{1,3},{3,1},{4,6},{6,4},{5,7},{7,5},{8,10},{10,8},{9,1... | collective-permute-start | bytes 1572872 | tf_op jit(solution)/shard_map/ppermute | solution.py:244
  26.5 18.1 %collective-permute-start.1 = (bf16[2,256,512]{2,1,0:T(8,128)(2,1)S(1)}, bf16[2,256,512]{2,1,0:T(8,128)(2,1)S(1)}, u32[]{:S(2)}, u32[]{:S(2)}) collective-permute-start(bf16[2,256,512]{2,1,0:T(8,128)(2,1)S(1)} %collective-permute-done.refs_0_), channel_id=1, source_target_pairs={{0,8},{8,0},{1,9},{9,1},{2,10},{10,2},{3,11},{11,3},{4,12},{12,4},... | collective-permute-start | bytes 1572872 | tf_op jit(solution)/shard_map/ppermute | solution.py:247
  30.4 14.3 %collective-permute-start.10 = (bf16[2,256,512]{2,1,0:T(8,128)(2,1)S(1)}, bf16[2,256,512]{2,1,0:T(8,128)(2,1)S(1)}, u32[]{:S(2)}, u32[]{:S(2)}) collective-permute-start(bf16[2,256,512]{2,1,0:T(8,128)(2,1)S(1)} %collective-permute-done.8.refs_2_), channel_id=1, source_target_pairs={{0,257},{1,256},{256,1},{257,0},{2,259},{3,258},{258,3},{259,2},{4... | collective-permute-start | bytes 1572872 | tf_op jit(solution)/shard_map/ppermute | solution.py:241
  34.8 9.9 %collective-permute-start.9 = (bf16[2,256,512]{2,1,0:T(8,128)(2,1)S(1)}, bf16[2,256,512]{2,1,0:T(8,128)(2,1)S(1)}, u32[]{:S(2)}, u32[]{:S(2)}) collective-permute-start(bf16[2,256,512]{2,1,0:T(8,128)(2,1)S(1)} %collective-permute-done.8.refs_2_), channel_id=1, source_target_pairs={{0,8},{8,0},{1,9},{9,1},{2,10},{10,2},{3,11},{11,3},{4,12},{12,4},... | collective-permute-start | bytes 1572872 | tf_op jit(solution)/shard_map/ppermute | solution.py:247
  39.3 5.5 %collective-permute-start.7 = (bf16[2,256,512]{2,1,0:T(8,128)(2,1)S(1)}, bf16[2,256,512]{2,1,0:T(8,128)(2,1)S(1)}, u32[]{:S(2)}, u32[]{:S(2)}) collective-permute-start(bf16[2,256,512]{2,1,0:T(8,128)(2,1)S(1)} %collective-permute-done.6.refs_0_), channel_id=1, source_target_pairs={{0,8},{8,0},{1,9},{9,1},{2,10},{10,2},{3,11},{11,3},{4,12},{12,4},... | collective-permute-start | bytes 1572872 | tf_op jit(solution)/shard_map/ppermute | solution.py:247
  41.2 5.0 %collective-permute-start.5 = (bf16[2,256,512]{2,1,0:T(8,128)(2,1)S(1)}, bf16[2,256,512]{2,1,0:T(8,128)(2,1)S(1)}, u32[]{:S(2)}, u32[]{:S(2)}) collective-permute-start(bf16[2,256,512]{2,1,0:T(8,128)(2,1)S(1)} %collective-permute-done.4.refs_4_), channel_id=1, source_target_pairs={{0,8},{8,0},{1,9},{9,1},{2,10},{10,2},{3,11},{11,3},{4,12},{12,4},... | collective-permute-start | bytes 1572872 | tf_op jit(solution)/shard_map/ppermute | solution.py:247
  46.2 11.2 %collective-permute-start.12 = (bf16[2,256,512]{2,1,0:T(8,128)(2,1)S(1)}, bf16[2,256,512]{2,1,0:T(8,128)(2,1)S(1)}, u32[]{:S(2)}, u32[]{:S(2)}) collective-permute-start(bf16[2,256,512]{2,1,0:T(8,128)(2,1)S(1)} %collective-permute-done.10.refs_4_), channel_id=1, source_target_pairs={{0,8},{8,0},{1,9},{9,1},{2,10},{10,2},{3,11},{11,3},{4,12},{12,4},... | collective-permute-start | bytes 1572872 | tf_op jit(solution)/shard_map/ppermute | solution.py:247
  49.8 0.9 copy-start.2
  53.4 3.9 %collective-permute-start.11 = (bf16[32,512]{1,0:T(8,128)(2,1)S(1)}, bf16[32,512]{1,0:T(8,128)(2,1)S(1)}, u32[]{:S(2)}, u32[]{:S(2)}) collective-permute-start(bf16[32,512]{1,0:T(8,128)(2,1)S(1)} %get-tuple-element.48), channel_id=1, source_target_pairs={{0,6},{2,4},{1,7},{3,5},{8,14},{10,12},{9,15},{11,13},{16,22},{18,... | collective-permute-start | bytes 98312 | tf_op jit(solution)/shard_map/ppermute | solution.py:266
  57.3 9.9 %copy-start.3 = (bf16[4,32,512]{2,1,0:T(8,128)(2,1)S(1)}, bf16[4,32,512]{2,1,0:T(8,128)(2,1)}, u32[]{:S(2)}) copy-start(bf16[4,32,512]{2,1,0:T(8,128)(2,1)} %cotangent.1) | copy-start | bytes 393220
  58.3 9.0 %collective-permute-start.13 = (bf16[32,512]{1,0:T(8,128)(2,1)S(1)}, bf16[32,512]{1,0:T(8,128)(2,1)S(1)}, u32[]{:S(2)}, u32[]{:S(2)}) collective-permute-start(bf16[32,512]{1,0:T(8,128)(2,1)S(1)} %get-tuple-element.56), channel_id=1, source_target_pairs={{6,0},{4,2},{7,1},{5,3},{14,8},{12,10},{15,9},{13,11},{22,16},{20,... | collective-permute-start | bytes 98312 | tf_op jit(solution)/shard_map/ppermute | solution.py:273
  71.2 2.3 %collective-permute-start.14 = (bf16[32,512]{1,0:T(8,128)(2,1)S(1)}, bf16[32,512]{1,0:T(8,128)(2,1)S(1)}, u32[]{:S(2)}, u32[]{:S(2)}) collective-permute-start(bf16[32,512]{1,0:T(8,128)(2,1)S(1)} %get-tuple-element.59), channel_id=1, source_target_pairs={{0,6},{2,4},{1,7},{3,5},{8,14},{10,12},{9,15},{11,13},{16,22},{18,... | collective-permute-start | bytes 98312 | tf_op jit(solution)/shard_map/ppermute | solution.py:278
  74.0 9.3 %collective-permute-start.15 = (bf16[32,512]{1,0:T(8,128)(2,1)S(1)}, bf16[32,512]{1,0:T(8,128)(2,1)S(1)}, u32[]{:S(2)}, u32[]{:S(2)}) collective-permute-start(bf16[32,512]{1,0:T(8,128)(2,1)S(1)} %get-tuple-element.69), channel_id=1, source_target_pairs={{6,0},{4,2},{7,1},{5,3},{14,8},{12,10},{15,9},{13,11},{22,16},{20,... | collective-permute-start | bytes 98312 | tf_op jit(solution)/shard_map/ppermute | solution.py:283
